TPU v7x, 32 devices: a whole 2x2x4 slice. The times are simulated.
32 devices in a mesh: stack: 4 (over y, x), plane: 4 (over z), phys: 2 (over core).
Axes of the slice: x: 2, y: 2, z: 4, core: 2. Of those that a mesh axis runs over, the one named last changes fastest.
Arguments:
- thermal_offset: float32 [256, 64, 512], P('stack', 'plane', 'phys'), may hold values from -6 to 6
- volume_power_source: float32 [256, 64, 512], P('stack', 'plane', 'phys'), may hold values from -0.024 to 0.024
- substance_code: int32 [256, 64, 512], P('stack', 'plane', 'phys'), may hold values from 0 to 4
- creeping_joint_flag: int32 [256, 64, 512], P('stack', 'plane', 'phys'), may hold values 0 or 1
- imposed_overall_distortion: float32 [256, 64, 512], P('stack', 'plane', 'phys'), may hold values from -1 to 1
- plastic_distortion: float32 [256, 64, 512], P('stack', 'plane', 'phys'), may hold values from -3 to 3
- anand_hardness: float32 [256, 64, 512], P('stack', 'plane', 'phys'), may hold values from 0.8 to 2.4
Outputs:
- new_temperature: float32 [256, 64, 512], P('stack', 'plane', 'phys')
- new_creep_strain: float32 [256, 64, 512], P('stack', 'plane', 'phys')
- new_resistance: float32 [256, 64, 512], P('stack', 'plane', 'phys')
- stress_residual: float32 [256, 64, 512], P('stack', 'plane', 'phys')
Inputs may be any that keep to these rules, and one draw needn't show every extreme that they name: `substance_code`: material of each cell: 0 die, 1 underfill, 2 solder ball, 3 substrate, 4 board.
All inputs are finite; a program needn't handle non-finite values. No bound on the sum of `creeping_joint_flag` on one device may be relied on, other than what follows from the above.
Results may differ from a plain program's by a relative error of at most 0.0003.
Values sent between devices are 32-bit elements; how exact they have to be, the bound alone decides.
No kernel may reach another device: no remote copies, remote signals or barrier semaphores. Data moves between devices by JAX's collectives and lax.ppermute only.
A program may use at most 128 MiB of HBM per device.

v0:
```python
import functools

import jax
import jax.numpy as jnp
from jax import lax
from jax.experimental import pallas as pl
from jax.experimental.pallas import tpu as pltpu
from jax.sharding import PartitionSpec as P

TSTEPS = 3

k_table = (4.0, 0.6, 2.5, 1.2, 0.8)
cap_table = (1.6, 1.8, 1.7, 2.0, 1.9)
mod_table = (1.5, 0.6, 0.9, 1.2, 0.8)
expand_table = (0.1, 0.3, 0.25, 0.15, 0.2)
cap_unit = 0.0003
lat_unit = 1.2e-05
h_conv = 0.05
creep_rate = 0.05
log2e = 1.4426950408889634
inv_e = 0.36787944117144233

LANES = 128
SUB = 8
F32 = jnp.float32


def loop(count, body, init, unroll=4, reverse=False):
    while count % unroll:
        unroll -= 1

    def group(step, carry):
        for j in range(unroll):
            place = step * unroll + j
            carry = body(count - 1 - place if reverse else place, carry)
        return carry

    return lax.fori_loop(0, count // unroll, group, init)


def rcp(x):
    return pl.reciprocal(x, approx=True)


def by_code(code, table, scale=1.0):
    result = jnp.full(code.shape, table[4] * scale, F32)
    for entry in range(4):
        result = jnp.where(code == entry, F32(table[entry] * scale), result)
    return result


def cap_by_k(k):
    result = jnp.full(k.shape, cap_unit * cap_table[4], F32)
    for entry in range(4):
        result = jnp.where(k == F32(k_table[entry]), F32(cap_unit * cap_table[entry]), result)
    return result


def conductance(p, q, scale=1.0):
    return (2.0 * scale) * p * q * rcp(jnp.maximum(p + q, 1e-6))


def call(body, ins, outs, name, flops=0, scratch=()):
    spec = pl.BlockSpec(memory_space=pltpu.VMEM)
    size = sum(a.size * 4 for a in ins) + sum(4 * functools.reduce(lambda x, y: x * y, s) for s in outs)
    return pl.pallas_call(
        body,
        in_specs=[spec] * len(ins),
        out_specs=[spec] * len(outs),
        out_shape=[jax.ShapeDtypeStruct(s, F32) for s in outs],
        scratch_shapes=list(scratch),
        compiler_params=pltpu.CompilerParams(vmem_limit_bytes=16 * 2**20),
        cost_estimate=pl.CostEstimate(flops=flops, bytes_accessed=size, transcendentals=0),
        name=name,
    )(*ins)


def pair_swaps(axis):
    count = lax.axis_size(axis)
    first = [(i, i + 1) for i in range(0, count - 1, 2)]
    second = [(i, i + 1) for i in range(1, count - 1, 2)]
    return [pairs + [(b, a) for a, b in pairs] for pairs in (first, second)]


def even(axis):
    return lax.rem(lax.axis_index(axis), 2) == 0


def edge_rows(t_ref, q_ref, code_ref, a_ref, b_ref):
    x = t_ref.shape[1]
    is_even = even("plane")

    def side(near, far, beyond):
        k1 = by_code(code_ref[:, near, :], k_table)
        k2 = by_code(code_ref[:, far, :], k_table)
        k3 = by_code(code_ref[:, beyond, :], k_table)
        t2 = t_ref[:, far, :]
        flow = conductance(k2, k3, lat_unit) * (t_ref[:, beyond, :] - t2)
        return (t_ref[:, near, :], t2, k1, k2, q_ref[:, near, :], q_ref[:, far, :] + flow)

    top = side(x - 1, x - 2, x - 3)
    bottom = side(0, 1, 2)
    for i in range(6):
        a_ref[i] = jnp.where(is_even, top[i], bottom[i])
        b_ref[i] = jnp.where(is_even, bottom[i], top[i])


def factor_rows(get_k, capm_extra, levels, out):
    cap_ref, w_ref, r_ref, yr_ref, left_ref, g_ref = out
    first_extra, last_extra = capm_extra
    zero = jnp.zeros(w_ref.shape[1:], F32)

    def forward(i, carry):
        ws, y, k_here = carry
        k_next = get_k(jnp.minimum(i + 1, levels - 1))
        cap = cap_by_k(k_here)
        cap_ref[i] = cap
        extra = jnp.where(i == 0, first_extra, 0.0) + jnp.where(i == levels - 1, last_extra, 0.0)
        s = cap + extra + ws
        u = jnp.where(i == levels - 1, 0.0, conductance(k_here, k_next))
        r = rcp(s + u)
        w = u * r
        w_ref[i] = w
        r_ref[i] = r
        yr_ref[i] = y * r
        return (w * s, y * w, k_next)

    k_first = get_k(0)
    _, _, k_last = loop(levels, forward, (zero, zero + 1.0, k_first))

    def backward(i, left):
        left = yr_ref[i] + w_ref[i] * left
        left_ref[i] = left
        return left

    left = loop(levels, backward, zero, reverse=True)
    g_ref[0] = left + 0.5 * rcp(jnp.maximum(k_first, 1e-3))
    g_ref[1] = yr_ref[levels - 1]
    g_ref[2] = r_ref[levels - 1] + 0.5 * rcp(jnp.maximum(k_last, 1e-3))


def end_losses():
    place, count = lax.axis_index("stack"), lax.axis_size("stack")
    return (jnp.where(place == 0, F32(h_conv), F32(0.0)), jnp.where(place == count - 1, F32(h_conv), F32(0.0)))


def factor_main(code_ref, k_ref, *out):
    def get_k(i):
        return by_code(code_ref[i], k_table)

    def keep(i, carry):
        k_ref[i] = get_k(i)
        return carry

    levels = code_ref.shape[0]
    loop(levels, keep, 0)
    factor_rows(lambda i: k_ref[i], end_losses(), levels, out)


def lane_edge(tile_pair, i, pack):
    low, high = tile_pair
    at_low = lax.axis_index("phys") == 1
    edge = jnp.where(at_low, low, high)
    shift = jnp.where(at_low, i, lax.rem(i + 1, LANES))
    lane = lax.broadcasted_iota(jnp.int32, edge.shape, 1)
    return jnp.where(lane == i, pltpu.roll(edge, shift, 1), pack)


def lane_unedge(pack, i):
    at_low = lax.axis_index("phys") == 1
    shift = jnp.where(at_low, lax.rem(LANES - i, LANES), LANES - 1 - i)
    moved = pltpu.roll(pack, shift, 1)
    lane = lax.broadcasted_iota(jnp.int32, pack.shape, 1)
    return (jnp.where((lane == 0) & at_low, moved, 0.0), jnp.where((lane == LANES - 1) & (~at_low), moved, 0.0))


def add_lane_edges(value, pack, i):
    low, high = lane_unedge(pack, i)
    tiles = [value[:, j : j + LANES] for j in range(0, value.shape[1], LANES)]
    tiles[0] = tiles[0] + low
    tiles[-1] = tiles[-1] + high
    return jnp.concatenate(tiles, axis=1)


def assemble_halo(a_ref, b_ref, k_ref, t_ref, kh_ref, th_ref, qh_ref, pack_ref):
    is_even = even("plane")
    levels, x, width = k_ref.shape
    row = lax.broadcasted_iota(jnp.int32, (SUB, width), 0)

    def level(i, carry):
        pack_t, pack_k = carry
        halos = []
        for first, ref in ((0, th_ref), (2, kh_ref), (4, qh_ref)):
            values = []
            for j in (first, first + 1):
                a = a_ref[j, pl.ds(i, 1), :]
                b = b_ref[j, pl.ds(i, 1), :]
                values.append((jnp.where(is_even, a, b), jnp.where(is_even, b, a)))
            halo = jnp.where(row == 0, values[0][0], 0.0)
            halo = jnp.where(row == 1, values[1][0], halo)
            halo = jnp.where(row == SUB - 1, values[0][1], halo)
            halo = jnp.where(row == SUB - 2, values[1][1], halo)
            ref[i] = halo
            halos.append(halo)
        t = jnp.concatenate([t_ref[i], halos[0]], axis=0)
        k = jnp.concatenate([k_ref[i], halos[1]], axis=0)
        pack_t = lane_edge((t[:, :LANES], t[:, width - LANES :]), i, pack_t)
        pack_k = lane_edge((k[:, :LANES], k[:, width - LANES :]), i, pack_k)
        return (pack_t, pack_k)

    zero = jnp.zeros((x + SUB, LANES), F32)
    pack_t, pack_k = loop(levels, level, (zero, zero))
    pack_ref[0] = pack_t
    pack_ref[1] = pack_k


def factor_halo(k_ref, kh_ref, gx_ref, gxh_ref, gy_ref, gyh_ref, *out):
    levels, x, width = k_ref.shape
    lane = lax.broadcasted_iota(jnp.int32, (x + SUB, width), 1)

    def lateral(i, carry):
        k = jnp.concatenate([k_ref[i], kh_ref[i]], axis=0)
        gx = conductance(k, pltpu.roll(k, x + SUB - 1, 0), lat_unit)
        gy = conductance(k, pltpu.roll(k, width - 1, 1), lat_unit)
        gy = jnp.where(lane == width - 1, 0.0, gy)
        gx_ref[i], gxh_ref[i] = gx[:x], gx[x:]
        gy_ref[i], gyh_ref[i] = gy[:x], gy[x:]
        return carry

    loop(levels, lateral, 0)
    factor_rows(lambda i: kh_ref[i], end_losses(), levels, out)


def both(main_ref, halo_ref, i):
    return jnp.concatenate([main_ref[i], halo_ref[i]], axis=0)


def right_side(send_g, last, *refs):
    (t, th, q, qh, cap, caph, gx, gxh, gy, gyh, w, wh, r, rh, left, lefth, own, other, own_k, other_k) = refs[:20]
    refs = refs[20:]
    if send_g:
        g, gh = refs[:2]
        refs = refs[2:]
    levels, x, width = t.shape
    if last:
        z, send = refs
    else:
        z, zh, send = refs
    rows = x if last else x + SUB
    flow = conductance(own_k[...], other_k[...], lat_unit) * (other[...] - own[...])

    def pick(main_ref, halo_ref, i):
        return main_ref[i] if last else both(main_ref, halo_ref, i)

    def level(i, carry):
        wy, bf = carry
        temp = both(t, th, i)
        fy = both(gy, gyh, i) * (pltpu.roll(temp, width - 1, 1) - temp)
        fx = both(gx, gxh, i) * (pltpu.roll(temp, x + SUB - 1, 0) - temp)
        lateral = fx - pltpu.roll(fx, 1, 0) + fy - pltpu.roll(fy, 1, 1)
        lateral = add_lane_edges(lateral, flow, i)[:rows]
        rhs = pick(cap, caph, i) * temp[:rows] + pick(q, qh, i) + lateral
        y = rhs + wy
        zz = y * pick(r, rh, i)
        z[i] = zz[:x]
        if not last:
            zh[i] = zz[x:]
        return (pick(w, wh, i) * y, bf + pick(left, lefth, i) * rhs)

    zero = jnp.zeros((rows, width), F32)
    _, bf = loop(levels, level, (zero, zero))
    send[0] = bf
    send[1] = pick(z, None if last else zh, levels - 1)
    if send_g:
        for j in range(3):
            send[2 + j] = both(g, gh, j)


def interface_flows(g_sets, b_sets, rows, place, count):
    def at(sets, entry, block):
        value = sets[0][entry][:rows]
        for j in range(1, count):
            value = jnp.where((place ^ j) == block, sets[j][entry][:rows], value)
        return value

    diag, off, rhs = [], [], []
    for j in range(count - 1):
        diag.append(at(g_sets, 4, j) + at(g_sets, 2, j + 1))
        off.append(at(g_sets, 3, j + 1))
        rhs.append(at(b_sets, 0, j + 1) - at(b_sets, 1, j))
    ups, vals = [], []
    for j in range(count - 1):
        pivot, value = diag[j], rhs[j]
        if j:
            pivot = pivot - off[j - 1] * ups[j - 1]
            value = value + off[j - 1] * vals[j - 1]
        inverse = rcp(pivot)
        ups.append(off[j] * inverse)
        vals.append(value * inverse)
    flows = [None] * (count - 1)
    for j in reversed(range(count - 1)):
        flows[j] = vals[j] if j == count - 2 else vals[j] + ups[j] * flows[j + 1]
    return flows


def column_solve(count, first, last, *refs):
    g_sets, refs = refs[:count], refs[count:]
    if first:
        b_sets = g_sets
    else:
        b_sets, refs = refs[:count], refs[count:]
    if last:
        z, w, r, yr, t = refs
    else:
        z, zh, w, wh, r, rh, yr, yrh, t, th, pack_ref = refs
    levels, x, width = z.shape
    rows = x if last else x + SUB
    place = lax.axis_index("stack")

    def pick(main_ref, halo_ref, i):
        return main_ref[i] if last else both(main_ref, halo_ref, i)

    flows = interface_flows(g_sets, b_sets, rows, place, count)
    zero = jnp.zeros((rows, width), F32)
    top, bottom = zero, zero
    for j in range(count - 1):
        top = jnp.where(place == j + 1, -flows[j], top)
        bottom = jnp.where(place == j, flows[j], bottom)

    def level(i, carry):
        add, pack = carry
        value = pick(z, None if last else zh, i) + top * pick(yr, None if last else yrh, i) + add
        t[i] = value[:x]
        if not last:
            th[i] = value[x:]
            pack = lane_edge((value[:, :LANES], value[:, width - LANES :]), i, pack)
        below = jnp.maximum(i - 1, 0)
        return (pick(w, None if last else wh, below) * value, pack)

    init = (bottom * pick(r, None if last else rh, levels - 1), jnp.zeros((rows, LANES), F32))
    _, pack = loop(levels, level, init, reverse=True)
    if not last:
        pack_ref[...] = pack


def prepare_creep(code_ref, flag_ref, mod_ref, exp_ref, rate_ref):
    def level(i, carry):
        code = code_ref[i]
        mod_ref[i] = by_code(code, mod_table)
        exp_ref[i] = by_code(code, expand_table)
        rate_ref[i] = jnp.where(flag_ref[i] == 1, F32(0.5 * creep_rate * inv_e), F32(0.0))
        return carry

    loop(code_ref.shape[0], level, 0)


def creep_cells(temp, mod, exp, rate, dist, creep, hard):
    elastic = dist - exp * temp
    drive = jnp.exp2((0.5 * log2e) * mod * (elastic - creep) * rcp(hard))
    drive = drive - rcp(drive)
    size = jnp.abs(drive)
    rate = rate * jnp.exp2(-log2e * rcp(jnp.exp2((0.5 * log2e) * temp + 1.0) + 1.0))
    gap = 1.0 - hard * jnp.exp2(-0.1 * jnp.log2(1.0 + size) - 0.9)
    gap_size = jnp.abs(gap)
    root = gap_size * lax.rsqrt(jnp.maximum(gap_size, 1e-30))
    creep = creep + rate * drive
    hard = hard + gap * root * (rate * size)
    return (elastic, creep, hard)


def creep_step(t, mod, exp, rate, dist, creep, hard, creep_out, hard_out):
    def level(i, carry):
        _, creep_out[i], hard_out[i] = creep_cells(t[i], mod[i], exp[i], rate[i], dist[i], creep[i], hard[i])
        return carry

    loop(t.shape[0], level, 0, unroll=2)


def creep_last(t, mod, exp, rate, dist, creep, hard, creep_out, hard_out, s, xa, xb, za, zb, pack_ref):
    levels, x, width = t.shape

    def level(i, pack):
        m = mod[i]
        elastic, new, hard_out[i] = creep_cells(t[i], m, exp[i], rate[i], dist[i], creep[i], hard[i])
        creep_out[i] = new
        stress = m * (elastic - new)
        s[i] = stress
        return lane_edge((stress[:, :LANES], stress[:, width - LANES :]), i, pack)

    pack_ref[...] = loop(levels, level, jnp.zeros((x, LANES), F32), unroll=2)
    is_even = even("plane")
    top, bottom = s[:, x - 1, :], s[:, 0, :]
    xa[...] = jnp.where(is_even, top, bottom)
    xb[...] = jnp.where(is_even, bottom, top)
    is_even = even("stack")
    za[...] = jnp.where(is_even, s[levels - 1], s[0])
    zb[...] = jnp.where(is_even, s[0], s[levels - 1])


def balance(s, xa, xb, za, zb, other, out):
    levels, x, width = s.shape
    plane_even, stack_even = even("plane"), even("stack")
    row = lax.broadcasted_iota(jnp.int32, (x, width), 0)
    lane = lax.broadcasted_iota(jnp.int32, (x, width), 1)
    z_after = jnp.where(stack_even, za[...], zb[...])
    z_before = jnp.where(stack_even, zb[...], za[...])

    def level(i, before):
        here = s[i]
        a, b = xa[pl.ds(i, 1), :], xb[pl.ds(i, 1), :]
        upper, lower = jnp.where(plane_even, a, b), jnp.where(plane_even, b, a)
        after = jnp.where(i == levels - 1, z_after, s[jnp.minimum(i + 1, levels - 1)])
        total = before + after - 6.0 * here
        total = total + jnp.where(row == 0, lower, pltpu.roll(here, 1, 0))
        total = total + jnp.where(row == x - 1, upper, pltpu.roll(here, x - 1, 0))
        total = total + jnp.where(lane == 0, 0.0, pltpu.roll(here, 1, 1))
        total = total + jnp.where(lane == width - 1, 0.0, pltpu.roll(here, width - 1, 1))
        out[i] = add_lane_edges(total, other[...], i)
        return here

    loop(levels, level, z_before)


def per_device(temp, source, code, flag, distortion, creep, hard):
    levels, x, width = temp.shape
    count = lax.axis_size("stack")
    if lax.axis_size("phys") != 2 or count & (count - 1) or levels > LANES or x % SUB or width % LANES:
        raise ValueError("unsupported sizes")
    main, halo = (levels, x, width), (levels, SUB, width)
    cells = levels * x * width
    swap = [(0, 1), (1, 0)]
    plane_swaps, stack_swaps = pair_swaps("plane"), pair_swaps("stack")
    peers = [[(i, i ^ j) for i in range(count)] for j in range(1, count)]

    rows_a, rows_b = call(edge_rows, (temp, source, code), [(6, levels, width)] * 2, "edge_rows", cells)
    rows_a = lax.ppermute(rows_a, "plane", plane_swaps[0])
    rows_b = lax.ppermute(rows_b, "plane", plane_swaps[1])
    k, *fact = call(factor_main, (code,), [main] * 6 + [(3, x, width)], "factor_main", 20 * cells)
    kh, th, qh, pack = call(
        assemble_halo, (rows_a, rows_b, k, temp), [halo] * 3 + [(2, x + SUB, LANES)], "assemble_halo", 3 * cells
    )
    other = lax.ppermute(pack, "phys", swap)
    gx, gxh, gy, gyh, *facth = call(
        factor_halo, (k, kh), [main, halo, main, halo] + [halo] * 5 + [(3, SUB, width)], "factor_halo", 20 * cells
    )
    own_k, other_k, own, other = pack[1], other[1], pack[0], other[0]
    cap, w, r, yr, left, g = fact
    caph, wh, rh, yrh, lefth, gh = facth
    mod, exp, rate = call(prepare_creep, (code, flag), [main] * 3, "prepare_creep", 10 * cells)

    rows = x + SUB
    for step in range(TSTEPS):
        first, last = step == 0, step == TSTEPS - 1
        ins = [temp, th, source, qh, cap, caph, gx, gxh, gy, gyh, w, wh, r, rh, left, lefth, own, other, own_k, other_k]
        ins += [g, gh] if first else []
        send = (5 if first else 2, x if last else rows, width)
        outs = call(
            functools.partial(right_side, first, last), ins, [main, send] if last else [main, halo, send], "right_side", 30 * cells
        )
        z, zh, own_b = outs[0], outs[1], outs[-1]
        b_sets = [own_b] + [lax.ppermute(own_b, "stack", peer) for peer in peers]
        if first:
            g_sets = b_sets
        if step:
            creep, hard = call(
                creep_step, (temp, mod, exp, rate, distortion, creep, hard), [main] * 2, "creep_step", 60 * cells
            )
        ins = list(g_sets) + ([] if first else b_sets)
        if last:
            (temp,) = call(
                functools.partial(column_solve, count, first, last), ins + [z, w, r, yr], [main], "column_solve", 10 * cells
            )
        else:
            temp, th, own = call(
                functools.partial(column_solve, count, first, last),
                ins + [z, zh, w, wh, r, rh, yr, yrh],
                [main, halo, (rows, LANES)],
                "column_solve",
                10 * cells,
            )
            other = lax.ppermute(own, "phys", swap)

    creep, hard, stress, xa, xb, za, zb, pack = call(
        creep_last,
        (temp, mod, exp, rate, distortion, creep, hard),
        [main] * 3 + [(levels, width)] * 2 + [(x, width)] * 2 + [(x, LANES)],
        "creep_last",
        60 * cells,
    )
    xa = lax.ppermute(xa, "plane", plane_swaps[0])
    xb = lax.ppermute(xb, "plane", plane_swaps[1])
    za = lax.ppermute(za, "stack", stack_swaps[0])
    zb = lax.ppermute(zb, "stack", stack_swaps[1])
    other = lax.ppermute(pack, "phys", swap)
    (residual,) = call(balance, (stress, xa, xb, za, zb, other), [main], "balance", 10 * cells)
    return (temp, creep, hard, residual)


def solution(mesh):
    spec = P("stack", "plane", "phys")
    return jax.shard_map(per_device, mesh=mesh, in_specs=(spec,) * 7, out_specs=(spec,) * 4, check_vma=False)
```

profile of v0, /device:TPU:10, one launch (start us, length us, event | category | flops | bytes accessed | tf_op | source)
XLA Modules:
  0.0 85.9 jit_solution(34076283093008268)
XLA Ops:
  6.0 4.6 %collective-permute-start.1 = (f32[6,64,256]{2,1,0:T(8,128)S(1)}, f32[6,64,256]{2,1,0:T(8,128)S(1)}, u32[]{:S(2)}, u32[]{:S(2)}) collective-permute-start(f32[6,64,256]{2,1,0:T(8,128)S(1)} %get-tuple-element.57), channel_id=1, source_target_pairs={{2,4},{4,2},{3,5},{5,3},{10,12},{12,10},{11,13},{13,11},{18,20},{2... | collective-permute-start | bytes 1179656 | tf_op jit(solution)/shard_map/ppermute | solution.py:437
  10.6 1.5 %factor_main.1 = (f32[64,16,256]{2,1,0:T(8,128)S(1)}, f32[64,16,256]{2,1,0:T(8,128)S(1)}, f32[64,16,256]{2,1,0:T(8,128)S(1)}, f32[64,16,256]{2,1,0:T(8,128)S(1)}...) custom-call(s32[64,16,256]{2,1,0:T(8,128)S(1)} %copy-done.4), custom_call_target="tpu_custom_call" | custom-call | flops 5242880 | bytes 7389184 | tf_op jit(solution)/shard_map/factor_main/pallas_call | solution.py:66
  12.2 4.2 %collective-permute-done.a_ref = f32[6,64,256]{2,1,0:T(8,128)S(1)} collective-permute-done((f32[6,64,256]{2,1,0:T(8,128)S(1)}, f32[6,64,256]{2,1,0:T(8,128)S(1)}, u32[]{:S(2)}, u32[]{:S(2)}) %collective-permute-start) | collective-permute-done | bytes 393248 | tf_op jit(solution)/shard_map/ppermute | solution.py:436
  16.4 3.0 %collective-permute-done.1.b_ref = f32[6,64,256]{2,1,0:T(8,128)S(1)} collective-permute-done((f32[6,64,256]{2,1,0:T(8,128)S(1)}, f32[6,64,256]{2,1,0:T(8,128)S(1)}, u32[]{:S(2)}, u32[]{:S(2)}) %collective-permute-start.1) | collective-permute-done | bytes 393248 | tf_op jit(solution)/shard_map/ppermute | solution.py:437
  19.4 1.9 %assemble_halo.1 = (f32[64,8,256]{2,1,0:T(8,128)S(1)}, f32[64,8,256]{2,1,0:T(8,128)S(1)}, f32[64,8,256]{2,1,0:T(8,128)S(1)}, f32[2,24,128]{2,1,0:T(8,128)S(1)}) custom-call(f32[6,64,256]{2,1,0:T(8,128)S(1)} %collective-permute-done.a_ref, f32[6,64,256]{2,1,0:T(8,128)S(1)} %collective-permute-done.1.b_ref, f32[64,16,256]{2,1,0:T(8,128)S(1)} %get-tuple-element.58.k_ref, ...), custom_call_target="tpu_custom_call" | custom-call | flops 786432 | bytes 4481024 | tf_op jit(solution)/shard_map/assemble_halo/pallas_call | solution.py:66
  21.4 2.7 %factor_halo.1 = (f32[64,16,256]{2,1,0:T(8,128)S(1)}, f32[64,8,256]{2,1,0:T(8,128)S(1)}, f32[64,16,256]{2,1,0:T(8,128)S(1)}, f32[64,8,256]{2,1,0:T(8,128)S(1)}, ...) custom-call(f32[64,16,256]{2,1,0:T(8,128)S(1)} %get-tuple-element.58, ...), custom_call_target="tpu_custom_call" | custom-call | flops 5242880 | bytes 7364608 | tf_op jit(solution)/shard_map/factor_halo/pallas_call | solution.py:66
  24.2 3.0 %right_side.3 = (f32[64,16,256]{2,1,0:T(8,128)S(1)}, f32[64,8,256]{2,1,0:T(8,128)S(1)}, f32[5,24,256]{2,1,0:T(8,128)S(1)}) custom-call(f32[64,16,256]{2,1,0:T(8,128)S(1)} %copy-done.6, f32[64,8,256]{2,1,0:T(8,128)S(1)} %get-tuple-element.59.refs_1_, f32[64,16,256]{2,1,0:T(8,128)S(1)} %copy-done.1, f32[64,8,256]{2,1,0:T(8,128)S(1)} %get-tuple-element.60.refs_3_, ...), custom_call_target="tpu_custom_call" | custom-call | flops 7864320 | bytes 14401536 | tf_op jit(solution)/shard_map/right_side/pallas_call | solution.py:66
  30.8 2.6 %collective-permute-done.3.refs_1_ = f32[5,24,256]{2,1,0:T(8,128)S(1)} collective-permute-done((f32[5,24,256]{2,1,0:T(8,128)S(1)}, f32[5,24,256]{2,1,0:T(8,128)S(1)}, u32[]{:S(2)}, u32[]{:S(2)}) %collective-permute-start.3) | collective-permute-done | bytes 122912 | tf_op jit(solution)/shard_map/ppermute | solution.py:461
  33.4 1.6 %collective-permute-done.4.refs_2_ = f32[5,24,256]{2,1,0:T(8,128)S(1)} collective-permute-done((f32[5,24,256]{2,1,0:T(8,128)S(1)}, f32[5,24,256]{2,1,0:T(8,128)S(1)}, u32[]{:S(2)}, u32[]{:S(2)}) %collective-permute-start.4) | collective-permute-done | bytes 122912 | tf_op jit(solution)/shard_map/ppermute | solution.py:461
  34.9 1.6 %collective-permute-done.5.refs_3_ = f32[5,24,256]{2,1,0:T(8,128)S(1)} collective-permute-done((f32[5,24,256]{2,1,0:T(8,128)S(1)}, f32[5,24,256]{2,1,0:T(8,128)S(1)}, u32[]{:S(2)}, u32[]{:S(2)}) %collective-permute-start.5) | collective-permute-done | bytes 122912 | tf_op jit(solution)/shard_map/ppermute | solution.py:461
  36.6 1.7 %column_solve.3 = (f32[64,16,256]{2,1,0:T(8,128)S(1)}, f32[64,8,256]{2,1,0:T(8,128)S(1)}, f32[24,128]{1,0:T(8,128)S(1)}) custom-call(f32[5,24,256]{2,1,0:T(8,128)S(1)} %get-tuple-element.77.refs_0_, f32[5,24,256]{2,1,0:T(8,128)S(1)} %collective-permute-done.3.refs_1_, f32[5,24,256]{2,1,0:T(8,128)S(1)} %collective-permute-done.4.refs_2_, ...), custom_call_target="tpu_custom_call" | custom-call | flops 2621440 | bytes 8368128 | tf_op jit(solution)/shard_map/column_solve/pallas_call | solution.py:66
  39.5 3.0 %right_side.4 = (f32[64,16,256]{2,1,0:T(8,128)S(1)}, f32[64,8,256]{2,1,0:T(8,128)S(1)}, f32[2,24,256]{2,1,0:T(8,128)S(1)}) custom-call(f32[64,16,256]{2,1,0:T(8,128)S(1)} %get-tuple-element.82.refs_0_.t, f32[64,8,256]{2,1,0:T(8,128)S(1)} %get-tuple-element.83.refs_1_, f32[64,16,256]{2,1,0:T(8,128)S(1)} %copy-done.1, ...), custom_call_target="tpu_custom_call" | custom-call | flops 7864320 | bytes 14254080 | tf_op jit(solution)/shard_map/right_side/pallas_call | solution.py:66
  43.3 1.5 %collective-permute-start.8 = (f32[2,24,256]{2,1,0:T(8,128)S(1)}, f32[2,24,256]{2,1,0:T(8,128)S(1)}, u32[]{:S(2)}, u32[]{:S(2)}) collective-permute-start(f32[2,24,256]{2,1,0:T(8,128)S(1)} %get-tuple-element.85.refs_4_), channel_id=1, source_target_pairs={{0,16},{8,24},{16,0},{24,8},{1,17},{9,25},{17,1},{25,9},{2,18},{10... | collective-permute-start | bytes 147464 | tf_op jit(solution)/shard_map/ppermute | solution.py:461
  47.4 2.4 %collective-permute-done.9.refs_7_ = f32[2,24,256]{2,1,0:T(8,128)S(1)} collective-permute-done((f32[2,24,256]{2,1,0:T(8,128)S(1)}, f32[2,24,256]{2,1,0:T(8,128)S(1)}, u32[]{:S(2)}, u32[]{:S(2)}) %collective-permute-start.9) | collective-permute-done | bytes 49184 | tf_op jit(solution)/shard_map/ppermute | solution.py:461
  49.9 1.7 %column_solve.4 = (f32[64,16,256]{2,1,0:T(8,128)S(1)}, f32[64,8,256]{2,1,0:T(8,128)S(1)}, f32[24,128]{1,0:T(8,128)S(1)}) custom-call(f32[5,24,256]{2,1,0:T(8,128)S(1)} %get-tuple-element.77.refs_0_, f32[5,24,256]{2,1,0:T(8,128)S(1)} %collective-permute-done.3.refs_1_, f32[5,24,256]{2,1,0:T(8,128)S(1)} %collective-permute-done.4.refs_2_, ...), custom_call_target="tpu_custom_call" | custom-call | flops 2621440 | bytes 8564736 | tf_op jit(solution)/shard_map/column_solve/pallas_call | solution.py:66
  52.8 2.7 %right_side.5 = (f32[64,16,256]{2,1,0:T(8,128)S(1)}, f32[2,16,256]{2,1,0:T(8,128)S(1)}) custom-call(f32[64,16,256]{2,1,0:T(8,128)S(1)} %get-tuple-element.88.refs_0_.t, f32[64,8,256]{2,1,0:T(8,128)S(1)} %get-tuple-element.89.refs_1_, f32[64,16,256]{2,1,0:T(8,128)S(1)} %copy-done.1, f32[64,8,256]{2,1,0:T(8,128)S(1)} %get-tuple-element.60.refs_3_, ...), custom_call_target="tpu_custom_call" | custom-call | flops 7864320 | bytes 13713408 | tf_op jit(solution)/shard_map/right_side/pallas_call | solution.py:66
  57.3 1.8 %collective-permute-start.13 = (f32[2,16,256]{2,1,0:T(8,128)S(1)}, f32[2,16,256]{2,1,0:T(8,128)S(1)}, u32[]{:S(2)}, u32[]{:S(2)}) collective-permute-start(f32[2,16,256]{2,1,0:T(8,128)S(1)} %get-tuple-element.91.refs_4_), channel_id=1, source_target_pairs={{0,24},{8,16},{16,8},{24,0},{1,25},{9,17},{17,9},{25,1},{2,26},{10... | collective-permute-start | bytes 98312 | tf_op jit(solution)/shard_map/ppermute | solution.py:461
  59.8 2.4 %creep_step.2 = (f32[64,16,256]{2,1,0:T(8,128)S(1)}, f32[64,16,256]{2,1,0:T(8,128)S(1)}) custom-call(f32[64,16,256]{2,1,0:T(8,128)S(1)} %get-tuple-element.82.refs_0_.t, f32[64,16,256]{2,1,0:T(8,128)S(1)} %get-tuple-element.93.mod, f32[64,16,256]{2,1,0:T(8,128)S(1)} %get-tuple-element.94.exp, f32[64,16,256]{2,1,0:T(8,128)S(1)} %get-tuple-element.95.rate, ...), custom_call_target="tpu_custom_call" | custom-call | flops 15728640 | bytes 9437184 | tf_op jit(solution)/shard_map/creep_step/pallas_call | solution.py:66
  62.2 2.4 %creep_step.3 = (f32[64,16,256]{2,1,0:T(8,128)S(1)}, f32[64,16,256]{2,1,0:T(8,128)S(1)}) custom-call(f32[64,16,256]{2,1,0:T(8,128)S(1)} %get-tuple-element.88.refs_0_.t, f32[64,16,256]{2,1,0:T(8,128)S(1)} %get-tuple-element.93.mod, f32[64,16,256]{2,1,0:T(8,128)S(1)} %get-tuple-element.94.exp, f32[64,16,256]{2,1,0:T(8,128)S(1)} %get-tuple-element.95.rate, ...), custom_call_target="tpu_custom_call" | custom-call | flops 15728640 | bytes 9437184 | tf_op jit(solution)/shard_map/creep_step/pallas_call | solution.py:66
  67.1 5.2 %creep_last.1 = (f32[64,16,256]{2,1,0:T(8,128)}, f32[64,16,256]{2,1,0:T(8,128)}, f32[64,16,256]{2,1,0:T(8,128)S(1)}, f32[64,256]{1,0:T(8,128)S(1)}, f32[64,256]{...) custom-call(f32[64,16,256]{2,1,0:T(8,128)S(1)} %copy-done.7, ...), custom_call_target="tpu_custom_call" | custom-call | flops 15728640 | bytes 10657792 | tf_op jit(solution)/shard_map/creep_last/pallas_call | solution.py:66
  72.3 3.6 %collective-permute-start.15 = (f32[64,256]{1,0:T(8,128)S(1)}, f32[64,256]{1,0:T(8,128)S(1)}, u32[]{:S(2)}, u32[]{:S(2)}) collective-permute-start(f32[64,256]{1,0:T(8,128)S(1)} %get-tuple-element.104), channel_id=1, source_target_pairs={{2,4},{4,2},{3,5},{5,3},{10,12},{12,10},{11,13},{13,11},{18,20},{2... | collective-permute-start | bytes 196616 | tf_op jit(solution)/shard_map/ppermute | solution.py:491
  76.5 3.3 %collective-permute-start.17 = (f32[16,256]{1,0:T(8,128)S(1)}, f32[16,256]{1,0:T(8,128)S(1)}, u32[]{:S(2)}, u32[]{:S(2)}) collective-permute-start(f32[16,256]{1,0:T(8,128)S(1)} %get-tuple-element.106), channel_id=1, source_target_pairs={{8,16},{16,8},{9,17},{17,9},{10,18},{18,10},{11,19},{19,11},{12,20... | collective-permute-start | bytes 49160 | tf_op jit(solution)/shard_map/ppermute | solution.py:493
  81.1 1.9 %collective-permute-done.17.zb = f32[16,256]{1,0:T(8,128)S(1)} collective-permute-done((f32[16,256]{1,0:T(8,128)S(1)}, f32[16,256]{1,0:T(8,128)S(1)}, u32[]{:S(2)}, u32[]{:S(2)}) %collective-permute-start.17) | collective-permute-done | bytes 16416 | tf_op jit(solution)/shard_map/ppermute | solution.py:493
  83.1 2.8 %balance.1 = f32[64,16,256]{2,1,0:T(8,128)} custom-call(f32[64,16,256]{2,1,0:T(8,128)S(1)} %get-tuple-element.102.s, f32[64,256]{1,0:T(8,128)S(1)} %collective-permute-done.14.xa, f32[64,256]{1,0:T(8,128)S(1)} %collective-permute-done.15.xb, f32[16,256]{1,0:T(8,128)S(1)} %collective-permute-done.16.za, f32[16,256]{1,0:T(8,128)S(1)} %collective-permute-done.17.zb, ...), custom_call_target="tpu_custom_call" | custom-call | flops 2621440 | bytes 2269184 | tf_op jit(solution)/shard_map/balance/pallas_call | solution.py:66
  (53 shorter events, 21.7 us)
Async XLA Ops:
  4.3 6.3 %copy-start.4 = (s32[64,16,256]{2,1,0:T(8,128)S(1)}, s32[64,16,256]{2,1,0:T(8,128)}, u32[]{:S(2)}) copy-start(s32[64,16,256]{2,1,0:T(8,128)} %code_ref.5) | copy-start | bytes 3145732
  5.5 10.9 %collective-permute-start = (f32[6,64,256]{2,1,0:T(8,128)S(1)}, f32[6,64,256]{2,1,0:T(8,128)S(1)}, u32[]{:S(2)}, u32[]{:S(2)}) collective-permute-start(f32[6,64,256]{2,1,0:T(8,128)S(1)} %get-tuple-element.56), channel_id=1, source_target_pairs={{0,2},{4,6},{2,0},{6,4},{1,3},{5,7},{3,1},{7,5},{8,10},{12,14},{10... | collective-permute-start | bytes 1179656 | tf_op jit(solution)/shard_map/ppermute | solution.py:436
  6.0 13.4 %collective-permute-start.1 = (f32[6,64,256]{2,1,0:T(8,128)S(1)}, f32[6,64,256]{2,1,0:T(8,128)S(1)}, u32[]{:S(2)}, u32[]{:S(2)}) collective-permute-start(f32[6,64,256]{2,1,0:T(8,128)S(1)} %get-tuple-element.57), channel_id=1, source_target_pairs={{2,4},{4,2},{3,5},{5,3},{10,12},{12,10},{11,13},{13,11},{18,20},{2... | collective-permute-start | bytes 1179656 | tf_op jit(solution)/shard_map/ppermute | solution.py:437
  19.4 4.8 %copy-start.6 = (f32[64,16,256]{2,1,0:T(8,128)S(1)}, f32[64,16,256]{2,1,0:T(8,128)}, u32[]{:S(2)}) copy-start(f32[64,16,256]{2,1,0:T(8,128)} %refs_0_.1) | copy-start | bytes 3145732
  21.3 2.8 %collective-permute-start.2 = (f32[2,24,128]{2,1,0:T(8,128)S(1)}, f32[2,24,128]{2,1,0:T(8,128)S(1)}, u32[]{:S(2)}, u32[]{:S(2)}) collective-permute-start(f32[2,24,128]{2,1,0:T(8,128)S(1)} %get-tuple-element.74), channel_id=1, source_target_pairs={{0,1},{1,0},{2,3},{3,2},{4,5},{5,4},{6,7},{7,6},{8,9},{9,8},{10,11... | collective-permute-start | bytes 73736 | tf_op jit(solution)/shard_map/ppermute | solution.py:442
  27.2 6.2 %collective-permute-start.3 = (f32[5,24,256]{2,1,0:T(8,128)S(1)}, f32[5,24,256]{2,1,0:T(8,128)S(1)}, u32[]{:S(2)}, u32[]{:S(2)}) collective-permute-start(f32[5,24,256]{2,1,0:T(8,128)S(1)} %get-tuple-element.77.refs_0_), channel_id=1, source_target_pairs={{0,8},{8,0},{16,24},{24,16},{1,9},{9,1},{17,25},{25,17},{2,10},{10... | collective-permute-start | bytes 368648 | tf_op jit(solution)/shard_map/ppermute | solution.py:461
  27.8 7.1 %collective-permute-start.4 = (f32[5,24,256]{2,1,0:T(8,128)S(1)}, f32[5,24,256]{2,1,0:T(8,128)S(1)}, u32[]{:S(2)}, u32[]{:S(2)}) collective-permute-start(f32[5,24,256]{2,1,0:T(8,128)S(1)} %get-tuple-element.77.refs_0_), channel_id=1, source_target_pairs={{0,16},{8,24},{16,0},{24,8},{1,17},{9,25},{17,1},{25,9},{2,18},{10... | collective-permute-start | bytes 368648 | tf_op jit(solution)/shard_map/ppermute | solution.py:461
  29.3 7.2 %collective-permute-start.5 = (f32[5,24,256]{2,1,0:T(8,128)S(1)}, f32[5,24,256]{2,1,0:T(8,128)S(1)}, u32[]{:S(2)}, u32[]{:S(2)}) collective-permute-start(f32[5,24,256]{2,1,0:T(8,128)S(1)} %get-tuple-element.77.refs_0_), channel_id=1, source_target_pairs={{0,24},{8,16},{16,8},{24,0},{1,25},{9,17},{17,9},{25,1},{2,26},{10... | collective-permute-start | bytes 368648 | tf_op jit(solution)/shard_map/ppermute | solution.py:461
  38.3 1.2 %collective-permute-start.6 = (f32[24,128]{1,0:T(8,128)S(1)}, f32[24,128]{1,0:T(8,128)S(1)}, u32[]{:S(2)}, u32[]{:S(2)}) collective-permute-start(f32[24,128]{1,0:T(8,128)S(1)} %get-tuple-element.84.refs_16_), channel_id=1, source_target_pairs={{0,1},{1,0},{2,3},{3,2},{4,5},{5,4},{6,7},{7,6},{8,9},{9,8},{10,11... | collective-permute-start | bytes 36872 | tf_op jit(solution)/shard_map/ppermute | solution.py:481
  42.5 4.2 %collective-permute-start.7 = (f32[2,24,256]{2,1,0:T(8,128)S(1)}, f32[2,24,256]{2,1,0:T(8,128)S(1)}, u32[]{:S(2)}, u32[]{:S(2)}) collective-permute-start(f32[2,24,256]{2,1,0:T(8,128)S(1)} %get-tuple-element.85.refs_4_), channel_id=1, source_target_pairs={{0,8},{8,0},{16,24},{24,16},{1,9},{9,1},{17,25},{25,17},{2,10},{10... | collective-permute-start | bytes 147464 | tf_op jit(solution)/shard_map/ppermute | solution.py:461
  43.3 4.1 %collective-permute-start.8 = (f32[2,24,256]{2,1,0:T(8,128)S(1)}, f32[2,24,256]{2,1,0:T(8,128)S(1)}, u32[]{:S(2)}, u32[]{:S(2)}) collective-permute-start(f32[2,24,256]{2,1,0:T(8,128)S(1)} %get-tuple-element.85.refs_4_), channel_id=1, source_target_pairs={{0,16},{8,24},{16,0},{24,8},{1,17},{9,25},{17,1},{25,9},{2,18},{10... | collective-permute-start | bytes 147464 | tf_op jit(solution)/shard_map/ppermute | solution.py:461
  44.9 5.0 %collective-permute-start.9 = (f32[2,24,256]{2,1,0:T(8,128)S(1)}, f32[2,24,256]{2,1,0:T(8,128)S(1)}, u32[]{:S(2)}, u32[]{:S(2)}) collective-permute-start(f32[2,24,256]{2,1,0:T(8,128)S(1)} %get-tuple-element.85.refs_4_), channel_id=1, source_target_pairs={{0,24},{8,16},{16,8},{24,0},{1,25},{9,17},{17,9},{25,1},{2,26},{10... | collective-permute-start | bytes 147464 | tf_op jit(solution)/shard_map/ppermute | solution.py:461
  51.5 1.2 %collective-permute-start.10 = (f32[24,128]{1,0:T(8,128)S(1)}, f32[24,128]{1,0:T(8,128)S(1)}, u32[]{:S(2)}, u32[]{:S(2)}) collective-permute-start(f32[24,128]{1,0:T(8,128)S(1)} %get-tuple-element.90.refs_16_), channel_id=1, source_target_pairs={{0,1},{1,0},{2,3},{3,2},{4,5},{5,4},{6,7},{7,6},{8,9},{9,8},{10,11... | collective-permute-start | bytes 36872 | tf_op jit(solution)/shard_map/ppermute | solution.py:481
  52.7 6.3 %copy-start.10 = (s32[64,16,256]{2,1,0:T(8,128)S(1)}, s32[64,16,256]{2,1,0:T(8,128)}, u32[]{:S(2)}) copy-start(s32[64,16,256]{2,1,0:T(8,128)} %flag_ref.1) | copy-start | bytes 3145732
  52.7 7.0 %copy-start.9 = (f32[64,16,256]{2,1,0:T(8,128)S(1)}, f32[64,16,256]{2,1,0:T(8,128)}, u32[]{:S(2)}) copy-start(f32[64,16,256]{2,1,0:T(8,128)} %hard.1) | copy-start | bytes 3145732
  55.5 4.3 %copy-start.2 = (f32[64,16,256]{2,1,0:T(8,128)S(1)}, f32[64,16,256]{2,1,0:T(8,128)}, u32[]{:S(2)}) copy-start(f32[64,16,256]{2,1,0:T(8,128)} %dist.5) | copy-start | bytes 3145732
  55.5 9.1 %collective-permute-start.11 = (f32[2,16,256]{2,1,0:T(8,128)S(1)}, f32[2,16,256]{2,1,0:T(8,128)S(1)}, u32[]{:S(2)}, u32[]{:S(2)}) collective-permute-start(f32[2,16,256]{2,1,0:T(8,128)S(1)} %get-tuple-element.91.refs_4_), channel_id=1, source_target_pairs={{0,8},{8,0},{16,24},{24,16},{1,9},{9,1},{17,25},{25,17},{2,10},{10... | collective-permute-start | bytes 98312 | tf_op jit(solution)/shard_map/ppermute | solution.py:461
  56.1 8.5 %collective-permute-start.12 = (f32[2,16,256]{2,1,0:T(8,128)S(1)}, f32[2,16,256]{2,1,0:T(8,128)S(1)}, u32[]{:S(2)}, u32[]{:S(2)}) collective-permute-start(f32[2,16,256]{2,1,0:T(8,128)S(1)} %get-tuple-element.91.refs_4_), channel_id=1, source_target_pairs={{0,16},{8,24},{16,0},{24,8},{1,17},{9,25},{17,1},{25,9},{2,18},{10... | collective-permute-start | bytes 98312 | tf_op jit(solution)/shard_map/ppermute | solution.py:461
  57.3 7.3 %collective-permute-start.13 = (f32[2,16,256]{2,1,0:T(8,128)S(1)}, f32[2,16,256]{2,1,0:T(8,128)S(1)}, u32[]{:S(2)}, u32[]{:S(2)}) collective-permute-start(f32[2,16,256]{2,1,0:T(8,128)S(1)} %get-tuple-element.91.refs_4_), channel_id=1, source_target_pairs={{0,24},{8,16},{16,8},{24,0},{1,25},{9,17},{17,9},{25,1},{2,26},{10... | collective-permute-start | bytes 98312 | tf_op jit(solution)/shard_map/ppermute | solution.py:461
  72.3 10.8 %collective-permute-start.14 = (f32[64,256]{1,0:T(8,128)S(1)}, f32[64,256]{1,0:T(8,128)S(1)}, u32[]{:S(2)}, u32[]{:S(2)}) collective-permute-start(f32[64,256]{1,0:T(8,128)S(1)} %get-tuple-element.103), channel_id=1, source_target_pairs={{0,2},{4,6},{2,0},{6,4},{1,3},{5,7},{3,1},{7,5},{8,10},{12,14},{10... | collective-permute-start | bytes 196616 | tf_op jit(solution)/shard_map/ppermute | solution.py:490
  72.3 10.8 %collective-permute-start.15 = (f32[64,256]{1,0:T(8,128)S(1)}, f32[64,256]{1,0:T(8,128)S(1)}, u32[]{:S(2)}, u32[]{:S(2)}) collective-permute-start(f32[64,256]{1,0:T(8,128)S(1)} %get-tuple-element.104), channel_id=1, source_target_pairs={{2,4},{4,2},{3,5},{5,3},{10,12},{12,10},{11,13},{13,11},{18,20},{2... | collective-permute-start | bytes 196616 | tf_op jit(solution)/shard_map/ppermute | solution.py:491
  75.9 5.2 %collective-permute-start.16 = (f32[16,256]{1,0:T(8,128)S(1)}, f32[16,256]{1,0:T(8,128)S(1)}, u32[]{:S(2)}, u32[]{:S(2)}) collective-permute-start(f32[16,256]{1,0:T(8,128)S(1)} %get-tuple-element.105), channel_id=1, source_target_pairs={{0,8},{16,24},{8,0},{24,16},{1,9},{17,25},{9,1},{25,17},{2,10},{18... | collective-permute-start | bytes 49160 | tf_op jit(solution)/shard_map/ppermute | solution.py:492
  76.5 6.5 %collective-permute-start.17 = (f32[16,256]{1,0:T(8,128)S(1)}, f32[16,256]{1,0:T(8,128)S(1)}, u32[]{:S(2)}, u32[]{:S(2)}) collective-permute-start(f32[16,256]{1,0:T(8,128)S(1)} %get-tuple-element.106), channel_id=1, source_target_pairs={{8,16},{16,8},{9,17},{17,9},{10,18},{18,10},{11,19},{19,11},{12,20... | collective-permute-start | bytes 49160 | tf_op jit(solution)/shard_map/ppermute | solution.py:493
  79.9 1.2 %collective-permute-start.18 = (f32[16,128]{1,0:T(8,128)S(1)}, f32[16,128]{1,0:T(8,128)S(1)}, u32[]{:S(2)}, u32[]{:S(2)}) collective-permute-start(f32[16,128]{1,0:T(8,128)S(1)} %get-tuple-element.107), channel_id=1, source_target_pairs={{0,1},{1,0},{2,3},{3,2},{4,5},{5,4},{6,7},{7,6},{8,9},{9,8},{10,11... | collective-permute-start | bytes 24584 | tf_op jit(solution)/shard_map/ppermute | solution.py:494
  (6 other events, 12.1 us)
where the time goes:
time: 86.2 us; the launch traced here: 85.9 us
  Pallas kernels  34.1 us (40%)
  starting transfers between devices  23.6 us (27%)
  waiting for transfers between devices  22.3 us (26%)
  local copies, waits for them, and re-layouts  4.93 us (6%)
  between operations  0.89 us (1%)
    pallas_call x15, Pallas kernels, call(): pl.pallas_call(body, in_specs=[spec] * len(ins), out_specs=[spec] * len(o...  34.1 us
    ppermute x9, starting transfers between devices, per_device(): b_sets = [own_b] + [lax.ppermute(own_b, 'stack', peer) for peer in peers]  10.7 us
    ppermute x9, waiting for transfers between devices, per_device(): b_sets = [own_b] + [lax.ppermute(own_b, 'stack', peer) for peer in peers]  9.63 us
    unnamed x22, local copies, waits for them, and re-layouts  4.93 us
    ppermute x1, starting transfers between devices, per_device(): rows_b = lax.ppermute(rows_b, 'plane', plane_swaps[1])  4.6 us
    ppermute x1, waiting for transfers between devices, per_device(): rows_a = lax.ppermute(rows_a, 'plane', plane_swaps[0])  4.24 us
    ppermute x1, starting transfers between devices, per_device(): xb = lax.ppermute(xb, 'plane', plane_swaps[1])  3.63 us
    ppermute x1, starting transfers between devices, per_device(): zb = lax.ppermute(zb, 'stack', stack_swaps[1])  3.33 us
  transfers between devices with their start and end apart: 19, of which 12 were waited for; matrix products, arithmetic and copies ran while one was open for 0% of the time, Pallas kernels for 11%

commit v1 on v0

v1 whole, which is shorter than its diff:
```python
import functools

import jax
import jax.numpy as jnp
from jax import lax
from jax.experimental import pallas as pl
from jax.experimental.pallas import tpu as pltpu
from jax.sharding import PartitionSpec as P

TSTEPS = 3

k_table = (4.0, 0.6, 2.5, 1.2, 0.8)
cap_table = (1.6, 1.8, 1.7, 2.0, 1.9)
mod_table = (1.5, 0.6, 0.9, 1.2, 0.8)
expand_table = (0.1, 0.3, 0.25, 0.15, 0.2)
cap_unit = 0.0003
lat_unit = 1.2e-05
h_conv = 0.05
creep_rate = 0.05
log2e = 1.4426950408889634
inv_e = 0.36787944117144233

LANES = 128
SUB = 8
F32 = jnp.float32


def loop(count, body, init, unroll=16, reverse=False):
    while count % unroll:
        unroll -= 1

    def group(step, carry):
        for j in range(unroll):
            place = step * unroll + j
            carry = body(count - 1 - place if reverse else place, carry)
        return carry

    return lax.fori_loop(0, count // unroll, group, init)


def rcp(x):
    return pl.reciprocal(x, approx=True)


def by_code(code, table, scale=1.0):
    result = jnp.full(code.shape, table[4] * scale, F32)
    for entry in range(4):
        result = jnp.where(code == entry, F32(table[entry] * scale), result)
    return result


def cap_by_k(k):
    result = jnp.full(k.shape, cap_unit * cap_table[4], F32)
    for entry in range(4):
        result = jnp.where(k == F32(k_table[entry]), F32(cap_unit * cap_table[entry]), result)
    return result


def conductance(p, q, scale=1.0):
    return (2.0 * scale) * p * q * rcp(jnp.maximum(p + q, 1e-6))


VMEM = pl.BlockSpec(memory_space=pltpu.VMEM)
HBM = pl.BlockSpec(memory_space=pltpu.HBM)
ANY = pl.BlockSpec(memory_space=pl.ANY)


def call(body, ins, outs, name, flops=0, scratch=(), after=(), in_hbm=0, out_hbm=0, aliases=None, vmem=16):
    n_in, n_after = len(ins), len(after)

    def kernel(*refs):
        body(*refs[:n_in], *refs[n_in + n_after :])

    outs = [o if isinstance(o, jax.ShapeDtypeStruct) else jax.ShapeDtypeStruct(o, F32) for o in outs]
    size = sum(a.size * 4 for a in list(ins) + outs)
    return pl.pallas_call(
        kernel if after else body,
        in_specs=[HBM] * in_hbm + [VMEM] * (n_in - in_hbm) + [ANY] * n_after,
        out_specs=[HBM] * out_hbm + [VMEM] * (len(outs) - out_hbm),
        out_shape=outs,
        scratch_shapes=list(scratch),
        input_output_aliases=aliases or {},
        compiler_params=pltpu.CompilerParams(vmem_limit_bytes=vmem * 2**20),
        cost_estimate=pl.CostEstimate(flops=flops, bytes_accessed=size, transcendentals=0),
        name=name,
    )(*ins, *after)


def pair_swaps(axis):
    count = lax.axis_size(axis)
    first = [(i, i + 1) for i in range(0, count - 1, 2)]
    second = [(i, i + 1) for i in range(1, count - 1, 2)]
    return [pairs + [(b, a) for a, b in pairs] for pairs in (first, second)]


def even(axis):
    return lax.rem(lax.axis_index(axis), 2) == 0


def edge_rows(t_in, code_in, q_in, a_ref, b_ref, t, code, q, sem):
    levels, x, width = t_in.shape
    rows = (x - 1, x - 2, x - 3, 0, 1, 2)
    copies = []
    for j, row in enumerate(rows):
        for entry, (source, held) in enumerate(((t_in, t), (code_in, code), (q_in, q))):
            if entry < 2 or j % 3 < 2:
                copies.append(pltpu.make_async_copy(source.at[:, row, :], held.at[j], sem.at[entry, j]))
    for copy in copies:
        copy.start()
    for copy in copies:
        copy.wait()
    is_even = even("plane")

    def side(near):
        k1, k2, k3 = (by_code(code[near + j], k_table) for j in range(3))
        flow = conductance(k2, k3, lat_unit) * (t[near + 2] - t[near + 1])
        return (t[near], t[near + 1], k1, k2, q[near], q[near + 1] + flow)

    top, bottom = side(0), side(3)
    for i in range(6):
        a_ref[i] = jnp.where(is_even, top[i], bottom[i])
        b_ref[i] = jnp.where(is_even, bottom[i], top[i])


def edge_layers(code, flag, dist, creep, hard, g, a_ref, b_ref):
    last = code.shape[0] - 1
    is_even = even("stack")
    for j in range(3):
        a_ref[j] = g[j]
        b_ref[j] = g[j]
    for j, source in enumerate((code, flag, dist, creep, hard)):
        after, before = source[last].astype(F32), source[0].astype(F32)
        a_ref[3 + j] = jnp.where(is_even, after, before)
        b_ref[3 + j] = jnp.where(is_even, before, after)


def factor_rows(get_k, capm_extra, levels, out):
    cap_ref, w_ref, r_ref, yr_ref, left_ref, g_ref = out
    first_extra, last_extra = capm_extra
    zero = jnp.zeros(w_ref.shape[1:], F32)

    def forward(i, carry):
        ws, y, k_here = carry
        k_next = get_k(jnp.minimum(i + 1, levels - 1))
        cap = cap_by_k(k_here)
        cap_ref[i] = cap
        extra = jnp.where(i == 0, first_extra, 0.0) + jnp.where(i == levels - 1, last_extra, 0.0)
        s = cap + extra + ws
        u = jnp.where(i == levels - 1, 0.0, conductance(k_here, k_next))
        r = rcp(s + u)
        w = u * r
        w_ref[i] = w
        r_ref[i] = r
        yr_ref[i] = y * r
        return (w * s, y * w, k_next)

    k_first = get_k(0)
    _, _, k_last = loop(levels, forward, (zero, zero + 1.0, k_first))

    def backward(i, left):
        left = yr_ref[i] + w_ref[i] * left
        left_ref[i] = left
        return left

    left = loop(levels, backward, zero, reverse=True)
    g_ref[0] = left + 0.5 * rcp(jnp.maximum(k_first, 1e-3))
    g_ref[1] = yr_ref[levels - 1]
    g_ref[2] = r_ref[levels - 1] + 0.5 * rcp(jnp.maximum(k_last, 1e-3))


def end_losses():
    place, count = lax.axis_index("stack"), lax.axis_size("stack")
    return (jnp.where(place == 0, F32(h_conv), F32(0.0)), jnp.where(place == count - 1, F32(h_conv), F32(0.0)))


def lane_edge(tile_pair, i, pack):
    low, high = tile_pair
    at_low = lax.axis_index("phys") == 1
    edge = jnp.where(at_low, low, high)
    shift = jnp.where(at_low, i, lax.rem(i + 1, LANES))
    lane = lax.broadcasted_iota(jnp.int32, edge.shape, 1)
    return jnp.where(lane == i, pltpu.roll(edge, shift, 1), pack)


def lane_unedge(pack, i):
    at_low = lax.axis_index("phys") == 1
    shift = jnp.where(at_low, lax.rem(LANES - i, LANES), LANES - 1 - i)
    moved = pltpu.roll(pack, shift, 1)
    lane = lax.broadcasted_iota(jnp.int32, pack.shape, 1)
    return (jnp.where((lane == 0) & at_low, moved, 0.0), jnp.where((lane == LANES - 1) & (~at_low), moved, 0.0))


def add_lane_edges(value, pack, i):
    low, high = lane_unedge(pack, i)
    tiles = [value[:, j : j + LANES] for j in range(0, value.shape[1], LANES)]
    tiles[0] = tiles[0] + low
    tiles[-1] = tiles[-1] + high
    return jnp.concatenate(tiles, axis=1)


def factor_main(code_ref, t_ref, gx_ref, gy_ref, pack_ref, k_ref, *out):
    levels, x, width = t_ref.shape
    row = lax.broadcasted_iota(jnp.int32, (x, width), 0)
    lane = lax.broadcasted_iota(jnp.int32, (x, width), 1)

    def lateral(i, carry):
        pack_t, pack_k = carry
        k = by_code(code_ref[i], k_table)
        k_ref[i] = k
        gx = conductance(k, pltpu.roll(k, x - 1, 0), lat_unit)
        gx_ref[i] = jnp.where(row == x - 1, 0.0, gx)
        gy = conductance(k, pltpu.roll(k, width - 1, 1), lat_unit)
        gy_ref[i] = jnp.where(lane == width - 1, 0.0, gy)
        t = t_ref[i]
        pack_t = lane_edge((t[:, :LANES], t[:, width - LANES :]), i, pack_t)
        pack_k = lane_edge((k[:, :LANES], k[:, width - LANES :]), i, pack_k)
        return (pack_t, pack_k)

    zero = jnp.zeros((x, LANES), F32)
    pack_ref[0], pack_ref[1] = loop(levels, lateral, (zero, zero))
    factor_rows(lambda i: k_ref[i], end_losses(), levels, out)


def assemble_halo(a_ref, b_ref, kh_ref, th_ref, qh_ref, pack_ref):
    is_even = even("plane")
    levels, _, width = kh_ref.shape
    row = lax.broadcasted_iota(jnp.int32, (SUB, width), 0)
    a_rows = [row == jnp.where(is_even, j, SUB - 1 - j) for j in (0, 1)]
    b_rows = [row == jnp.where(is_even, SUB - 1 - j, j) for j in (0, 1)]

    def level(i, carry):
        pack_t, pack_k = carry
        halos = []
        for first, ref in ((0, th_ref), (2, kh_ref), (4, qh_ref)):
            halo = jnp.zeros((SUB, width), F32)
            for source, rows in ((a_ref, a_rows), (b_ref, b_rows)):
                for j in (0, 1):
                    halo = jnp.where(rows[j], source[first + j, pl.ds(i, 1), :], halo)
            ref[i] = halo
            halos.append(halo)
        t, k = halos[0], halos[1]
        pack_t = lane_edge((t[:, :LANES], t[:, width - LANES :]), i, pack_t)
        pack_k = lane_edge((k[:, :LANES], k[:, width - LANES :]), i, pack_k)
        return (pack_t, pack_k)

    zero = jnp.zeros((SUB, LANES), F32)
    pack_ref[0], pack_ref[1] = loop(levels, level, (zero, zero))


def factor_halo(k_ref, kh_ref, gx_in, gx_ref, gxh_ref, gyh_ref, *out):
    levels, x, width = k_ref.shape
    row = lax.broadcasted_iota(jnp.int32, (SUB, width), 0)
    lane = lax.broadcasted_iota(jnp.int32, (SUB, width), 1)

    def lateral(i, carry):
        k = kh_ref[i]
        k_next = jnp.where(row == SUB - 1, k_ref[i, 0:1, :], pltpu.roll(k, SUB - 1, 0))
        gxh_ref[i] = conductance(k, k_next, lat_unit)
        gx_ref[i, x - 1 : x, :] = conductance(k_ref[i, x - 1 : x, :], k[0:1], lat_unit)
        gy = conductance(k, pltpu.roll(k, width - 1, 1), lat_unit)
        gyh_ref[i] = jnp.where(lane == width - 1, 0.0, gy)
        return carry

    loop(levels, lateral, 0)
    factor_rows(lambda i: kh_ref[i], end_losses(), levels, out)


def both(main_ref, halo_ref, i):
    return jnp.concatenate([main_ref[i], halo_ref[i]], axis=0)


def right_side(first, last, *refs):
    (t, th, q, qh, cap, caph, gx, gxh, gy, gyh, w, wh, r, rh, left, lefth, km, kh, other_km, other_kh) = refs[:20]
    refs = refs[20:]
    own_k = jnp.concatenate([km[1], kh[1]], axis=0)
    other_k = jnp.concatenate([other_km[1], other_kh[1]], axis=0)
    if first:
        gh, refs = refs[0], refs[1:]
        own = jnp.concatenate([km[0], kh[0]], axis=0)
        other = jnp.concatenate([other_km[0], other_kh[0]], axis=0)
    else:
        own, other = refs[0][...], refs[1][...]
        refs = refs[2:]
    levels, x, width = t.shape
    if last:
        z, send = refs
    else:
        z, zh, send = refs
    rows = x if last else x + SUB
    flow = conductance(own_k, other_k, lat_unit) * (other - own)
    flow = flow[:rows]

    def pick(main_ref, halo_ref, i):
        return main_ref[i] if last else both(main_ref, halo_ref, i)

    def level(i, carry):
        wy, bf = carry
        temp = both(t, th, i)
        here = temp[:rows]
        fy = pick(gy, gyh, i) * (pltpu.roll(here, width - 1, 1) - here)
        fx = both(gx, gxh, i) * (pltpu.roll(temp, x + SUB - 1, 0) - temp)
        lateral = (fx - pltpu.roll(fx, 1, 0))[:rows] + fy - pltpu.roll(fy, 1, 1)
        lateral = add_lane_edges(lateral, flow, i)
        rhs = pick(cap, caph, i) * here + pick(q, qh, i) + lateral
        y = rhs + wy
        zz = y * pick(r, rh, i)
        z[i] = zz[:x]
        if not last:
            zh[i] = zz[x:]
        return (pick(w, wh, i) * y, bf + pick(left, lefth, i) * rhs)

    zero = jnp.zeros((rows, width), F32)
    _, bf = loop(levels, level, (zero, zero), unroll=16 if last else 8)
    parts = [bf, pick(z, None if last else zh, levels - 1)]
    groups = [part[j : j + SUB] for part in parts for j in range(0, x, SUB)]
    if not last:
        groups.append(packed(*[part[x:] for part in parts]))
    if first:
        groups += [packed(gh[0], gh[1]), packed(gh[2], gh[2])]
    for j, group in enumerate(groups):
        send[j] = group


def packed(a, b):
    row = lax.broadcasted_iota(jnp.int32, a.shape, 0)
    return jnp.where((row >= 2) & (row < 6), pltpu.roll(b, 4, 0), a)


def block_flows(g_sets, h_sets, b_sets, x, rows):
    place, count = lax.axis_index("stack"), lax.axis_size("stack")

    def at(sets, block, read):
        value = read(sets[0])
        for j in range(1, count):
            value = jnp.where((place ^ j) == block, read(sets[j]), value)
        return value

    def ends(block):
        group = at(b_sets, block, lambda ref: ref[0 : 2 * x // SUB])
        group = group.reshape(2, x, group.shape[-1])
        if rows == x:
            return (group[0], group[1])
        tail = at(b_sets, block, lambda ref: ref[2 * x // SUB])
        return (
            jnp.concatenate([group[0], tail], axis=0),
            jnp.concatenate([group[1], pltpu.roll(tail, 4, 0)], axis=0),
        )

    def responses(block):
        group = at(g_sets, block, lambda ref: ref[0:3])
        if rows == x:
            return group
        tail = at(h_sets, block, lambda ref: ref[2 * x // SUB + 1 : 2 * x // SUB + 3])
        tails = (tail[0], pltpu.roll(tail[0], 4, 0), tail[1])
        return [jnp.concatenate([group[j], tails[j]], axis=0) for j in range(3)]

    end = [ends(block) for block in range(count)]
    g = [responses(block) for block in range(count)]
    ups, flows = [], []
    for j in range(count - 1):
        pivot = g[j][2] + g[j + 1][0]
        value = end[j + 1][0] - end[j][1]
        if j:
            pivot = pivot - g[j][1] * ups[j - 1]
            value = value + g[j][1] * flows[j - 1]
        inverse = rcp(pivot)
        ups.append(g[j + 1][1] * inverse)
        flows.append(value * inverse)
    for j in reversed(range(count - 2)):
        flows[j] = flows[j] + ups[j] * flows[j + 1]
    top = jnp.zeros_like(flows[0])
    bottom = top
    for j in range(count - 1):
        top = jnp.where(place == j + 1, -flows[j], top)
        bottom = jnp.where(place == j, flows[j], bottom)
    return top, bottom


def beside(edge, flow, k_edge, code_beside):
    return edge + flow * (0.5 * rcp(k_edge) + 0.5 * rcp(by_code(code_beside, k_table)))


def layers_beside(za, zb):
    is_even = even("stack")
    sides = []
    for j in (0, 1):
        value = [jnp.where(is_even, (zb, za)[j][3 + e], (za, zb)[j][3 + e]) for e in range(5)]
        value[4] = jnp.maximum(value[4], 0.1)
        sides.append(value)
    return sides


def rate_by_flag(active):
    return jnp.where(active, F32(0.5 * creep_rate * inv_e), F32(0.0))


def column_solve(count, first, *refs):
    g_sets, h_sets, refs = refs[:count], refs[count : 2 * count], refs[2 * count :]
    b_sets = h_sets
    if not first:
        b_sets, refs = refs[:count], refs[count:]
    z, zh, w, wh, r, rh, yr, yrh, t, th, pack_ref, flow_ref = refs
    levels, x, width = z.shape
    rows = x + SUB
    top, bottom = block_flows(g_sets, h_sets, b_sets, x, rows)
    flow_ref[0], flow_ref[1] = top[:x], bottom[:x]

    def level(i, carry):
        add, pack = carry
        value = both(z, zh, i) + top * both(yr, yrh, i) + add
        t[i] = value[:x]
        th[i] = value[x:]
        pack = lane_edge((value[:, :LANES], value[:, width - LANES :]), i, pack)
        return (both(w, wh, jnp.maximum(i - 1, 0)) * value, pack)

    init = (bottom * both(r, rh, levels - 1), jnp.zeros((rows, LANES), F32))
    _, pack_ref[...] = loop(levels, level, init, reverse=True)


def prepare_creep(code_ref, flag_ref, mod, exp, rate):
    def level(i, carry):
        code = code_ref[i]
        mod[i] = by_code(code, mod_table)
        exp[i] = by_code(code, expand_table)
        rate[i] = rate_by_flag(flag_ref[i] == 1)
        return carry

    loop(code_ref.shape[0], level, 0)


def creep_cells(temp, mod, exp, rate, dist, creep, hard):
    elastic = dist - exp * temp
    drive = jnp.exp2((0.5 * log2e) * mod * (elastic - creep) * rcp(hard))
    drive = drive - rcp(drive)
    size = jnp.abs(drive)
    rate = rate * jnp.exp2(-log2e * rcp(jnp.exp2((0.5 * log2e) * temp + 1.0) + 1.0))
    gap = 1.0 - hard * jnp.exp2(-0.1 * jnp.log2(1.0 + size) - 0.9)
    gap_size = jnp.abs(gap)
    root = gap_size * lax.rsqrt(jnp.maximum(gap_size, 1e-30))
    creep = creep + rate * drive
    hard = hard + gap * root * (rate * size)
    return (elastic, creep, hard)


def creep_beside(t, flow, k, za, zb, state):
    ends, results = (0, t.shape[0] - 1), []
    for j, (code, flag, dist, creep, hard) in enumerate(layers_beside(za, zb)):
        if state is not None:
            creep, hard = state[j], state[2 + j]
        temp = beside(t[ends[j]], flow[j], k[ends[j]], code)
        mod = by_code(code, mod_table)
        cells = creep_cells(temp, mod, by_code(code, expand_table), rate_by_flag(flag == 1.0), dist, creep, hard)
        results.append((*cells, mod))
    return results


def creep_step(first, *refs):
    main, refs = refs[:7], refs[7:]
    flow, k, za, zb = refs[:4]
    state, out = (None, refs[4:]) if first else (refs[4], refs[5:])

    def level(i, carry):
        _, out[0][i], out[1][i] = creep_cells(*[ref[i] for ref in main])
        return carry

    loop(main[0].shape[0], level, 0, unroll=8)
    for j, (_, creep, hard, _) in enumerate(creep_beside(main[0], flow, k, za, zb, state)):
        out[2][j] = creep
        out[2][2 + j] = hard


def solve_and_creep(count, *refs):
    g_sets, b_sets, refs = refs[:count], refs[count : 2 * count], refs[2 * count :]
    z, w, r, yr, k, za, zb, state = refs[:8]
    mod, exp, rate, dist, creep, hard = refs[8:14]
    t, creep_out, hard_out, s, zs, xa, xb, pack_ref = refs[14:]
    levels, x, width = z.shape
    top, bottom = block_flows(g_sets, None, b_sets, x, x)

    def level(i, carry):
        add, pack = carry
        value = z[i] + top * yr[i] + add
        t[i] = value
        m = mod[i]
        elastic, new, hard_out[i] = creep_cells(value, m, exp[i], rate[i], dist[i], creep[i], hard[i])
        creep_out[i] = new
        stress = m * (elastic - new)
        s[i] = stress
        pack = lane_edge((stress[:, :LANES], stress[:, width - LANES :]), i, pack)
        return (w[jnp.maximum(i - 1, 0)] * value, pack)

    init = (bottom * r[levels - 1], jnp.zeros((x, LANES), F32))
    _, pack_ref[...] = loop(levels, level, init, unroll=8, reverse=True)
    place = lax.axis_index("stack")
    for j, (elastic, new, _, m) in enumerate(creep_beside(t, (top, bottom), k, za, zb, state)):
        zs[j] = jnp.where(place == (0, count - 1)[j], 0.0, m * (elastic - new))
    is_even = even("plane")
    upper, lower = s[:, x - 1, :], s[:, 0, :]
    xa[...] = jnp.where(is_even, upper, lower)
    xb[...] = jnp.where(is_even, lower, upper)


def balance_inside(s, zs, t, creep, hard, t_out, creep_out, hard_out, inside, sem):
    copies = [
        pltpu.make_async_copy(held, out, sem.at[j])
        for j, (held, out) in enumerate(((t, t_out), (creep, creep_out), (hard, hard_out)))
    ]
    for copy in copies:
        copy.start()
    levels, x, width = s.shape
    row = lax.broadcasted_iota(jnp.int32, (x, width), 0)
    lane = lax.broadcasted_iota(jnp.int32, (x, width), 1)

    def level(i, before):
        here = s[i]
        after = jnp.where(i == levels - 1, zs[1], s[jnp.minimum(i + 1, levels - 1)])
        total = before + after - 6.0 * here
        total = total + jnp.where(row == 0, 0.0, pltpu.roll(here, 1, 0))
        total = total + jnp.where(row == x - 1, 0.0, pltpu.roll(here, x - 1, 0))
        total = total + jnp.where(lane == 0, 0.0, pltpu.roll(here, 1, 1))
        inside[i] = total + jnp.where(lane == width - 1, 0.0, pltpu.roll(here, width - 1, 1))
        return here

    loop(levels, level, zs[0])
    for copy in copies:
        copy.wait()


def balance_edges(inside, xa, xb, other, out, held, sem):
    levels, x, width = inside.shape
    is_even = even("plane")
    row = lax.broadcasted_iota(jnp.int32, (x, width), 0)
    a_row = row == jnp.where(is_even, x - 1, 0)
    b_row = row == jnp.where(is_even, 0, x - 1)
    chunks = sem.shape[0]
    part = levels // chunks
    copies = []
    for chunk in range(chunks):

        def level(j, carry, chunk=chunk):
            i = chunk * part + j
            total = inside[i] + jnp.where(a_row, xa[pl.ds(i, 1), :], 0.0)
            total = total + jnp.where(b_row, xb[pl.ds(i, 1), :], 0.0)
            held[i] = add_lane_edges(total, other[...], i)
            return carry

        loop(part, level, 0)
        place = pl.ds(chunk * part, part)
        copies.append(pltpu.make_async_copy(held.at[place], out.at[place], sem.at[chunk]))
        copies[-1].start()
    for copy in copies:
        copy.wait()


def per_device(temp, source, code, flag, distortion, creep, hard):
    levels, x, width = temp.shape
    count = lax.axis_size("stack")
    if lax.axis_size("phys") != 2 or count != 4 or levels > LANES or x % SUB or width % LANES:
        raise ValueError("unsupported sizes")
    main, halo, layers = (levels, x, width), (levels, SUB, width), (2, x, width)
    cells = levels * x * width
    swap = [(0, 1), (1, 0)]
    plane_swaps = pair_swaps("plane")
    peers = [[(i, i ^ j) for i in range(count)] for j in range(1, count)]
    dma = pltpu.SemaphoreType.DMA

    edge = (6, levels, width)
    rows_a, rows_b = call(
        edge_rows,
        (temp, code, source),
        [edge] * 2,
        "edge_rows",
        cells,
        [pltpu.VMEM(edge, F32), pltpu.VMEM(edge, jnp.int32), pltpu.VMEM(edge, F32), dma((3, 6))],
        in_hbm=3,
        vmem=60,
    )
    rows_a = lax.ppermute(rows_a, "plane", plane_swaps[0])
    rows_b = lax.ppermute(rows_b, "plane", plane_swaps[1])
    gx, gy, pack, k, *fact = call(
        factor_main, (code, temp), [main, main, (2, x, LANES)] + [main] * 6 + [(3, x, width)], "factor_main", 40 * cells
    )
    cap, w, r, yr, left, g = fact
    other_pack = lax.ppermute(pack, "phys", swap)
    za, zb = call(edge_layers, (code, flag, distortion, creep, hard, g), [(8, x, width)] * 2, "edge_layers", cells)
    za, g_two, zb = lax.ppermute(za, "stack", peers[0]), lax.ppermute(g, "stack", peers[1]), lax.ppermute(zb, "stack", peers[2])
    g_sets = [g, za, g_two, zb]
    mod, exp, rate = call(prepare_creep, (code, flag), [main] * 3, "prepare_creep", 10 * cells)

    kh, th, qh, packh = call(
        assemble_halo, (rows_a, rows_b), [halo] * 3 + [(2, SUB, LANES)], "assemble_halo", cells, after=(rate, other_pack)
    )
    other_packh = lax.ppermute(packh, "phys", swap)
    gx, gxh, gyh, caph, wh, rh, yrh, lefth, gh = call(
        factor_halo,
        (k, kh, gx),
        [main, halo, halo] + [halo] * 5 + [(3, SUB, width)],
        "factor_halo",
        20 * cells,
        aliases={2: 0},
    )

    rows = x + SUB
    own = other = state = None
    for step in range(TSTEPS):
        first, last = step == 0, step == TSTEPS - 1
        ins = [temp, th, source, qh, cap, caph, gx, gxh, gy, gyh, w, wh, r, rh, left, lefth]
        ins += [pack, packh, other_pack, other_packh]
        ins += [gh] if first else [own, other]
        send = (2 * x // SUB + (3 if first else 0 if last else 1), SUB, width)
        outs = call(
            functools.partial(right_side, first, last), ins, [main, send] if last else [main, halo, send], "right_side", 30 * cells
        )
        z, zh, own_b = outs[0], outs[1], outs[-1]
        b_sets = [own_b] + [lax.ppermute(own_b, "stack", peer) for peer in peers]
        if first:
            h_sets = b_sets
        else:
            creep, hard, state = call(
                functools.partial(creep_step, step == 1),
                [temp, mod, exp, rate, distortion, creep, hard, flow, k, za, zb] + ([] if step == 1 else [state]),
                [main] * 2 + [(4, x, width)],
                "creep_step",
                60 * cells,
            )
        if last:
            break
        temp, th, own, flow = call(
            functools.partial(column_solve, count, first),
            g_sets + h_sets + ([] if first else b_sets) + [z, zh, w, wh, r, rh, yr, yrh],
            [main, halo, (rows, LANES), layers],
            "column_solve",
            10 * cells,
            after=() if first else (creep,),
        )
        other = lax.ppermute(own, "phys", swap)

    temp, creep, hard, stress, zs, xa, xb, pack = call(
        functools.partial(solve_and_creep, count),
        g_sets + b_sets + [z, w, r, yr, k, za, zb, state, mod, exp, rate, distortion, creep, hard],
        [main] * 4 + [layers] + [(levels, width)] * 2 + [(x, LANES)],
        "solve_and_creep",
        70 * cells,
    )
    xa = lax.ppermute(xa, "plane", plane_swaps[0])
    xb = lax.ppermute(xb, "plane", plane_swaps[1])
    other = lax.ppermute(pack, "phys", swap)
    temp, creep, hard, inside = call(
        balance_inside, (stress, zs, temp, creep, hard), [main] * 4, "balance_inside", 20 * cells, [dma((3,))], out_hbm=3
    )
    (residual,) = call(
        balance_edges,
        (inside, xa, xb, other),
        [main],
        "balance_edges",
        10 * cells,
        [pltpu.VMEM(main, F32), dma((4,))],
        out_hbm=1,
    )
    return (temp, creep, hard, residual)


def solution(mesh):
    spec = P("stack", "plane", "phys")
    return jax.shard_map(per_device, mesh=mesh, in_specs=(spec,) * 7, out_specs=(spec,) * 4, check_vma=False)
```

time: 86.2 us -> 59.8 us (0.69)
  the two profiles are of different devices: /device:TPU:10 before, /device:TPU:0 now
where the time goes in v1:
time: 59.8 us; the launch traced here: 58.8 us
  starting transfers between devices  23.8 us (40%)
  Pallas kernels  23.2 us (39%)
  waiting for transfers between devices  9.55 us (16%)
  local copies, waits for them, and re-layouts  1.25 us (2%)
  between operations  0.91 us (2%)
    pallas_call x16, Pallas kernels, call(): pl.pallas_call(kernel if after else body, in_specs=[HBM] * in_hbm + [VMEM...  23.2 us
    ppermute x9, starting transfers between devices, per_device(): b_sets = [own_b] + [lax.ppermute(own_b, 'stack', peer) for peer in peers]  10.7 us
    ppermute x9, waiting for transfers between devices, per_device(): b_sets = [own_b] + [lax.ppermute(own_b, 'stack', peer) for peer in peers]  6.01 us
    ppermute x1, starting transfers between devices, per_device(): xa = lax.ppermute(xa, 'plane', plane_swaps[0])  4.79 us
    ppermute x1, starting transfers between devices, per_device(): rows_a = lax.ppermute(rows_a, 'plane', plane_swaps[0])  3.09 us
    ppermute x2, waiting for transfers between devices, per_device(): other = lax.ppermute(own, 'phys', swap)  2.33 us
    ppermute x1, starting transfers between devices, per_device(): lax.ppermute(za, 'stack', peers[0])  1.56 us
    ppermute x1, starting transfers between devices, per_device(): lax.ppermute(zb, 'stack', peers[2])  1.49 us
  transfers between devices with their start and end apart: 21, of which 10 were waited for; matrix products, arithmetic and copies ran while one was open for 0% of the time, Pallas kernels for 20%

profile of v1, /device:TPU:0, one launch (start us, length us, event | category | flops | bytes accessed | tf_op | source)
XLA Modules:
  0.0 58.8 jit_solution(16464215488240351933)
XLA Ops:
  0.7 2.8 %edge_rows.1 = (f32[6,64,256]{2,1,0:T(8,128)}, f32[6,64,256]{2,1,0:T(8,128)}) custom-call(f32[64,16,256]{2,1,0:T(8,128)} %refs_0_.1, s32[64,16,256]{2,1,0:T(8,128)} %code_ref.3, f32[64,16,256]{2,1,0:T(8,128)} %refs_2_.5), custom_call_target="tpu_custom_call" | custom-call | flops 262144 | bytes 3932160 | tf_op jit(solution)/shard_map/edge_rows/pallas_call | solution.py:76
  3.4 3.1 %collective-permute-start.3 = (f32[6,64,256]{2,1,0:T(8,128)}, f32[6,64,256]{2,1,0:T(8,128)S(1)}, u32[]{:S(2)}, u32[]{:S(2)}) collective-permute-start(f32[6,64,256]{2,1,0:T(8,128)} %get-tuple-element.71), channel_id=1, source_target_pairs={{0,2},{4,6},{2,0},{6,4},{1,3},{5,7},{3,1},{7,5},{8,10},{12,14},{10... | collective-permute-start | bytes 1179656 | tf_op jit(solution)/shard_map/ppermute | solution.py:578
  7.3 2.0 %factor_main.1 = (f32[64,16,256]{2,1,0:T(8,128)S(1)}, f32[64,16,256]{2,1,0:T(8,128)S(1)}, f32[2,16,128]{2,1,0:T(8,128)S(1)}, f32[64,16,256]{2,1,0:T(8,128)S(1)},...) custom-call(s32[64,16,256]{2,1,0:T(8,128)S(1)} %copy-done.1, ...), custom_call_target="tpu_custom_call" | custom-call | flops 10485760 | bytes 10551296 | tf_op jit(solution)/shard_map/factor_main/pallas_call | solution.py:76
  9.4 1.2 %copy-done.6 = s32[64,16,256]{2,1,0:T(8,128)S(1)} copy-done((s32[64,16,256]{2,1,0:T(8,128)S(1)}, s32[64,16,256]{2,1,0:T(8,128)}, u32[]{:S(2)}) %copy-start.6) | copy-done | bytes 1048600
  10.6 1.6 %collective-permute-start = (f32[8,16,256]{2,1,0:T(8,128)S(1)}, f32[8,16,256]{2,1,0:T(8,128)S(1)}, u32[]{:S(2)}, u32[]{:S(2)}) collective-permute-start(f32[8,16,256]{2,1,0:T(8,128)S(1)} %get-tuple-element.69), channel_id=1, source_target_pairs={{0,8},{8,0},{16,24},{24,16},{1,9},{9,1},{17,25},{25,17},{2,10},{10... | collective-permute-start | bytes 393224 | tf_op jit(solution)/shard_map/ppermute | solution.py:586
  12.2 1.5 %collective-permute-start.2 = (f32[8,16,256]{2,1,0:T(8,128)S(1)}, f32[8,16,256]{2,1,0:T(8,128)S(1)}, u32[]{:S(2)}, u32[]{:S(2)}) collective-permute-start(f32[8,16,256]{2,1,0:T(8,128)S(1)} %get-tuple-element.70), channel_id=1, source_target_pairs={{0,24},{8,16},{16,8},{24,0},{1,25},{9,17},{17,9},{25,1},{2,26},{10... | collective-permute-start | bytes 393224 | tf_op jit(solution)/shard_map/ppermute | solution.py:586
  13.7 1.2 %collective-permute-done.5.refs_3_.refs_18_ = f32[2,16,128]{2,1,0:T(8,128)S(1)} collective-permute-done((f32[2,16,128]{2,1,0:T(8,128)S(1)}, f32[2,16,128]{2,1,0:T(8,128)S(1)}, u32[]{:S(2)}, u32[]{:S(2)}) %collective-permute-start.5) | collective-permute-done | bytes 16416 | tf_op jit(solution)/shard_map/ppermute | solution.py:584
  16.8 1.3 %factor_halo.1 = (f32[64,16,256]{2,1,0:T(8,128)S(1)}, f32[64,8,256]{2,1,0:T(8,128)S(1)}, f32[64,8,256]{2,1,0:T(8,128)S(1)}, f32[64,8,256]{2,1,0:T(8,128)S(1)}, f...) custom-call(f32[64,16,256]{2,1,0:T(8,128)S(1)} %get-tuple-element.78, ...), custom_call_target="tpu_custom_call", output_to_operand_aliasing={{0}: (2, {})} | custom-call | flops 5242880 | bytes 7364608 | tf_op jit(solution)/shard_map/factor_halo/pallas_call | solution.py:76
  18.1 2.2 %right_side.3 = (f32[64,16,256]{2,1,0:T(8,128)S(1)}, f32[64,8,256]{2,1,0:T(8,128)S(1)}, f32[7,8,256]{2,1,0:T(8,128)S(1)}) custom-call(f32[64,16,256]{2,1,0:T(8,128)S(1)} %copy-done.3, f32[64,8,256]{2,1,0:T(8,128)S(1)} %get-tuple-element.75.refs_1_, f32[64,16,256]{2,1,0:T(8,128)S(1)} %copy-done.2, f32[64,8,256]{2,1,0:T(8,128)S(1)} %get-tuple-element.76.refs_3_, ...), custom_call_target="tpu_custom_call" | custom-call | flops 7864320 | bytes 14286848 | tf_op jit(solution)/shard_map/right_side/pallas_call | solution.py:76
  20.3 2.5 %collective-permute-start.9 = (f32[7,8,256]{2,1,0:T(8,128)S(1)}, f32[7,8,256]{2,1,0:T(8,128)S(1)}, u32[]{:S(2)}, u32[]{:S(2)}) collective-permute-start(f32[7,8,256]{2,1,0:T(8,128)S(1)} %get-tuple-element.94.refs_4_), channel_id=1, source_target_pairs={{0,24},{8,16},{16,8},{24,0},{1,25},{9,17},{17,9},{25,1},{2,26},{10... | collective-permute-start | bytes 172040 | tf_op jit(solution)/shard_map/ppermute | solution.py:615
  23.9 1.7 %collective-permute-done.9.refs_7_ = f32[7,8,256]{2,1,0:T(8,128)S(1)} collective-permute-done((f32[7,8,256]{2,1,0:T(8,128)S(1)}, f32[7,8,256]{2,1,0:T(8,128)S(1)}, u32[]{:S(2)}, u32[]{:S(2)}) %collective-permute-start.9) | collective-permute-done | bytes 57376 | tf_op jit(solution)/shard_map/ppermute | solution.py:615
  25.6 1.4 %collective-permute-done.8.refs_6_ = f32[7,8,256]{2,1,0:T(8,128)S(1)} collective-permute-done((f32[7,8,256]{2,1,0:T(8,128)S(1)}, f32[7,8,256]{2,1,0:T(8,128)S(1)}, u32[]{:S(2)}, u32[]{:S(2)}) %collective-permute-start.8) | collective-permute-done | bytes 57376 | tf_op jit(solution)/shard_map/ppermute | solution.py:615
  28.4 1.2 %collective-permute-done.10.refs_21_ = f32[24,128]{1,0:T(8,128)S(1)} collective-permute-done((f32[24,128]{1,0:T(8,128)S(1)}, f32[24,128]{1,0:T(8,128)S(1)}, u32[]{:S(2)}, u32[]{:S(2)}) %collective-permute-start.10) | collective-permute-done | bytes 12320 | tf_op jit(solution)/shard_map/ppermute | solution.py:636
  29.6 2.1 %right_side.4 = (f32[64,16,256]{2,1,0:T(8,128)S(1)}, f32[64,8,256]{2,1,0:T(8,128)S(1)}, f32[5,8,256]{2,1,0:T(8,128)S(1)}) custom-call(f32[64,16,256]{2,1,0:T(8,128)S(1)} %get-tuple-element.99.refs_0_, f32[64,8,256]{2,1,0:T(8,128)S(1)} %get-tuple-element.100.refs_1_, f32[64,16,256]{2,1,0:T(8,128)S(1)} %copy-done.2, ...), custom_call_target="tpu_custom_call" | custom-call | flops 7864320 | bytes 14270464 | tf_op jit(solution)/shard_map/right_side/pallas_call | solution.py:76
  31.7 1.6 %collective-permute-start.13 = (f32[5,8,256]{2,1,0:T(8,128)S(1)}, f32[5,8,256]{2,1,0:T(8,128)S(1)}, u32[]{:S(2)}, u32[]{:S(2)}) collective-permute-start(f32[5,8,256]{2,1,0:T(8,128)S(1)} %get-tuple-element.102.refs_8_), channel_id=1, source_target_pairs={{0,24},{8,16},{16,8},{24,0},{1,25},{9,17},{17,9},{25,1},{2,26},{10... | collective-permute-start | bytes 122888 | tf_op jit(solution)/shard_map/ppermute | solution.py:615
  34.1 1.2 %collective-permute-start.11 = (f32[5,8,256]{2,1,0:T(8,128)S(1)}, f32[5,8,256]{2,1,0:T(8,128)S(1)}, u32[]{:S(2)}, u32[]{:S(2)}) collective-permute-start(f32[5,8,256]{2,1,0:T(8,128)S(1)} %get-tuple-element.102.refs_8_), channel_id=1, source_target_pairs={{0,8},{8,0},{16,24},{24,16},{1,9},{9,1},{17,25},{25,17},{2,10},{10... | collective-permute-start | bytes 122888 | tf_op jit(solution)/shard_map/ppermute | solution.py:615
  35.3 1.8 %creep_step.2 = (f32[64,16,256]{2,1,0:T(8,128)S(1)}, f32[64,16,256]{2,1,0:T(8,128)S(1)}, f32[4,16,256]{2,1,0:T(8,128)S(1)}) custom-call(f32[64,16,256]{2,1,0:T(8,128)S(1)} %get-tuple-element.99.refs_0_, f32[64,16,256]{2,1,0:T(8,128)S(1)} %get-tuple-element.105.refs_1_.refs_16_, f32[64,16,256]{2,1,0:T(8,128)S(1)} %get-tuple-element.106.refs_2_.refs_17_, ...), custom_call_target="tpu_custom_call" | custom-call | flops 15728640 | bytes 10846208 | tf_op jit(solution)/shard_map/creep_step/pallas_call | solution.py:76
  39.0 1.2 %collective-permute-done.14.refs_21_ = f32[24,128]{1,0:T(8,128)S(1)} collective-permute-done((f32[24,128]{1,0:T(8,128)S(1)}, f32[24,128]{1,0:T(8,128)S(1)}, u32[]{:S(2)}, u32[]{:S(2)}) %collective-permute-start.14) | collective-permute-done | bytes 12320 | tf_op jit(solution)/shard_map/ppermute | solution.py:636
  40.2 1.5 %right_side.5 = (f32[64,16,256]{2,1,0:T(8,128)S(1)}, f32[4,8,256]{2,1,0:T(8,128)S(1)}) custom-call(f32[64,16,256]{2,1,0:T(8,128)S(1)} %get-tuple-element.109.refs_0_, f32[64,8,256]{2,1,0:T(8,128)S(1)} %get-tuple-element.110.refs_1_, f32[64,16,256]{2,1,0:T(8,128)S(1)} %copy-done.2, f32[64,8,256]{2,1,0:T(8,128)S(1)} %get-tuple-element.76.refs_3_, ...), custom_call_target="tpu_custom_call" | custom-call | flops 7864320 | bytes 13737984 | tf_op jit(solution)/shard_map/right_side/pallas_call | solution.py:76
  41.7 2.2 %collective-permute-start.17 = (f32[4,8,256]{2,1,0:T(8,128)S(1)}, f32[4,8,256]{2,1,0:T(8,128)S(1)}, u32[]{:S(2)}, u32[]{:S(2)}) collective-permute-start(f32[4,8,256]{2,1,0:T(8,128)S(1)} %get-tuple-element.112.refs_4_), channel_id=1, source_target_pairs={{0,24},{8,16},{16,8},{24,0},{1,25},{9,17},{17,9},{25,1},{2,26},{10... | collective-permute-start | bytes 98312 | tf_op jit(solution)/shard_map/ppermute | solution.py:615
  45.2 1.7 %creep_step.3 = (f32[64,16,256]{2,1,0:T(8,128)S(1)}, f32[64,16,256]{2,1,0:T(8,128)S(1)}, f32[4,16,256]{2,1,0:T(8,128)S(1)}) custom-call(f32[64,16,256]{2,1,0:T(8,128)S(1)} %get-tuple-element.109.refs_0_, f32[64,16,256]{2,1,0:T(8,128)S(1)} %get-tuple-element.105.refs_1_.refs_16_, f32[64,16,256]{2,1,0:T(8,128)S(1)} %get-tuple-element.106.refs_2_.refs_17_, ...), custom_call_target="tpu_custom_call" | custom-call | flops 15728640 | bytes 10911744 | tf_op jit(solution)/shard_map/creep_step/pallas_call | solution.py:76
  48.3 2.1 %solve_and_creep.1 = (f32[64,16,256]{2,1,0:T(8,128)S(1)}, f32[64,16,256]{2,1,0:T(8,128)S(1)}, f32[64,16,256]{2,1,0:T(8,128)S(1)}, f32[64,16,256]{2,1,0:T(8,128)S...) custom-call(f32[3,16,256]{2,1,0:T(8,128)S(1)} %get-tuple-element.68.g.re, ...), custom_call_target="tpu_custom_call" | custom-call | flops 18350080 | bytes 16719872 | tf_op jit(solution)/shard_map/solve_and_creep/pallas_call | solution.py:76
  50.4 4.8 %collective-permute-start.18 = (f32[64,256]{1,0:T(8,128)S(1)}, f32[64,256]{1,0:T(8,128)S(1)}, u32[]{:S(2)}, u32[]{:S(2)}) collective-permute-start(f32[64,256]{1,0:T(8,128)S(1)} %get-tuple-element.129), channel_id=1, source_target_pairs={{0,2},{4,6},{2,0},{6,4},{1,3},{5,7},{3,1},{7,5},{8,10},{12,14},{10... | collective-permute-start | bytes 196616 | tf_op jit(solution)/shard_map/ppermute | solution.py:645
  55.9 1.7 %balance_inside.1 = (f32[64,16,256]{2,1,0:T(8,128)}, f32[64,16,256]{2,1,0:T(8,128)}, f32[64,16,256]{2,1,0:T(8,128)}, f32[64,16,256]{2,1,0:T(8,128)S(1)}) custom-call(f32[64,16,256]{2,1,0:T(8,128)S(1)} %get-tuple-element.120.s, f32[2,16,256]{2,1,0:T(8,128)S(1)} %get-tuple-element.121.zs, f32[64,16,256]{2,1,0:T(8,128)S(1)} %get-tuple-element.122.t, ...), custom_call_target="tpu_custom_call" | custom-call | flops 5242880 | bytes 8421376 | tf_op jit(solution)/shard_map/balance_inside/pallas_call | solution.py:76
  (50 shorter events, 12.5 us)
Async XLA Ops:
  0.6 6.7 %copy-start.1 = (s32[64,16,256]{2,1,0:T(8,128)S(1)}, s32[64,16,256]{2,1,0:T(8,128)}, u32[]{:S(2)}) copy-start(s32[64,16,256]{2,1,0:T(8,128)} %code_ref.3) | copy-start | bytes 3145732
  0.6 6.7 %copy-start.3 = (f32[64,16,256]{2,1,0:T(8,128)S(1)}, f32[64,16,256]{2,1,0:T(8,128)}, u32[]{:S(2)}) copy-start(f32[64,16,256]{2,1,0:T(8,128)} %refs_0_.1) | copy-start | bytes 3145732
  0.7 8.7 %copy-start.5 = (f32[64,16,256]{2,1,0:T(8,128)S(1)}, f32[64,16,256]{2,1,0:T(8,128)}, u32[]{:S(2)}) copy-start(f32[64,16,256]{2,1,0:T(8,128)} %refs_6_.1) | copy-start | bytes 3145732
  3.4 12.5 %collective-permute-start.3 = (f32[6,64,256]{2,1,0:T(8,128)}, f32[6,64,256]{2,1,0:T(8,128)S(1)}, u32[]{:S(2)}, u32[]{:S(2)}) collective-permute-start(f32[6,64,256]{2,1,0:T(8,128)} %get-tuple-element.71), channel_id=1, source_target_pairs={{0,2},{4,6},{2,0},{6,4},{1,3},{5,7},{3,1},{7,5},{8,10},{12,14},{10... | collective-permute-start | bytes 1179656 | tf_op jit(solution)/shard_map/ppermute | solution.py:578
  6.5 9.5 %collective-permute-start.4 = (f32[6,64,256]{2,1,0:T(8,128)}, f32[6,64,256]{2,1,0:T(8,128)S(1)}, u32[]{:S(2)}, u32[]{:S(2)}) collective-permute-start(f32[6,64,256]{2,1,0:T(8,128)} %get-tuple-element.72), channel_id=1, source_target_pairs={{2,4},{4,2},{3,5},{5,3},{10,12},{12,10},{11,13},{13,11},{18,20},{2... | collective-permute-start | bytes 1179656 | tf_op jit(solution)/shard_map/ppermute | solution.py:579
  10.6 13.3 %collective-permute-start = (f32[8,16,256]{2,1,0:T(8,128)S(1)}, f32[8,16,256]{2,1,0:T(8,128)S(1)}, u32[]{:S(2)}, u32[]{:S(2)}) collective-permute-start(f32[8,16,256]{2,1,0:T(8,128)S(1)} %get-tuple-element.69), channel_id=1, source_target_pairs={{0,8},{8,0},{16,24},{24,16},{1,9},{9,1},{17,25},{25,17},{2,10},{10... | collective-permute-start | bytes 393224 | tf_op jit(solution)/shard_map/ppermute | solution.py:586
  12.2 11.7 %collective-permute-start.2 = (f32[8,16,256]{2,1,0:T(8,128)S(1)}, f32[8,16,256]{2,1,0:T(8,128)S(1)}, u32[]{:S(2)}, u32[]{:S(2)}) collective-permute-start(f32[8,16,256]{2,1,0:T(8,128)S(1)} %get-tuple-element.70), channel_id=1, source_target_pairs={{0,24},{8,16},{16,8},{24,0},{1,25},{9,17},{17,9},{25,1},{2,26},{10... | collective-permute-start | bytes 393224 | tf_op jit(solution)/shard_map/ppermute | solution.py:586
  13.6 1.2 %collective-permute-start.5 = (f32[2,16,128]{2,1,0:T(8,128)S(1)}, f32[2,16,128]{2,1,0:T(8,128)S(1)}, u32[]{:S(2)}, u32[]{:S(2)}) collective-permute-start(f32[2,16,128]{2,1,0:T(8,128)S(1)} %get-tuple-element.74.refs_16_), channel_id=1, source_target_pairs={{0,1},{1,0},{2,3},{3,2},{4,5},{5,4},{6,7},{7,6},{8,9},{9,8},{10,11... | collective-permute-start | bytes 49160 | tf_op jit(solution)/shard_map/ppermute | solution.py:584
  14.8 8.5 %collective-permute-start.1 = (f32[3,16,256]{2,1,0:T(8,128)S(1)}, f32[3,16,256]{2,1,0:T(8,128)S(1)}, u32[]{:S(2)}, u32[]{:S(2)}) collective-permute-start(f32[3,16,256]{2,1,0:T(8,128)S(1)} %get-tuple-element.68.g.refs_0_), channel_id=1, source_target_pairs={{0,16},{8,24},{16,0},{24,8},{1,17},{9,25},{17,1},{25,9},{2,18},{10... | collective-permute-start | bytes 147464 | tf_op jit(solution)/shard_map/ppermute | solution.py:586
  16.7 1.4 %collective-permute-start.6 = (f32[2,8,128]{2,1,0:T(8,128)S(1)}, f32[2,8,128]{2,1,0:T(8,128)S(1)}, u32[]{:S(2)}, u32[]{:S(2)}) collective-permute-start(f32[2,8,128]{2,1,0:T(8,128)S(1)} %get-tuple-element.92.refs_17_), channel_id=1, source_target_pairs={{0,1},{1,0},{2,3},{3,2},{4,5},{5,4},{6,7},{7,6},{8,9},{9,8},{10,11... | collective-permute-start | bytes 24584 | tf_op jit(solution)/shard_map/ppermute | solution.py:593
  20.3 5.3 %collective-permute-start.9 = (f32[7,8,256]{2,1,0:T(8,128)S(1)}, f32[7,8,256]{2,1,0:T(8,128)S(1)}, u32[]{:S(2)}, u32[]{:S(2)}) collective-permute-start(f32[7,8,256]{2,1,0:T(8,128)S(1)} %get-tuple-element.94.refs_4_), channel_id=1, source_target_pairs={{0,24},{8,16},{16,8},{24,0},{1,25},{9,17},{17,9},{25,1},{2,26},{10... | collective-permute-start | bytes 172040 | tf_op jit(solution)/shard_map/ppermute | solution.py:615
  22.9 4.2 %collective-permute-start.8 = (f32[7,8,256]{2,1,0:T(8,128)S(1)}, f32[7,8,256]{2,1,0:T(8,128)S(1)}, u32[]{:S(2)}, u32[]{:S(2)}) collective-permute-start(f32[7,8,256]{2,1,0:T(8,128)S(1)} %get-tuple-element.94.refs_4_), channel_id=1, source_target_pairs={{0,16},{8,24},{16,0},{24,8},{1,17},{9,25},{17,1},{25,9},{2,18},{10... | collective-permute-start | bytes 172040 | tf_op jit(solution)/shard_map/ppermute | solution.py:615
  23.4 4.2 %collective-permute-start.7 = (f32[7,8,256]{2,1,0:T(8,128)S(1)}, f32[7,8,256]{2,1,0:T(8,128)S(1)}, u32[]{:S(2)}, u32[]{:S(2)}) collective-permute-start(f32[7,8,256]{2,1,0:T(8,128)S(1)} %get-tuple-element.94.refs_4_), channel_id=1, source_target_pairs={{0,8},{8,0},{16,24},{24,16},{1,9},{9,1},{17,25},{25,17},{2,10},{10... | collective-permute-start | bytes 172040 | tf_op jit(solution)/shard_map/ppermute | solution.py:615
  28.4 1.2 %collective-permute-start.10 = (f32[24,128]{1,0:T(8,128)S(1)}, f32[24,128]{1,0:T(8,128)S(1)}, u32[]{:S(2)}, u32[]{:S(2)}) collective-permute-start(f32[24,128]{1,0:T(8,128)S(1)} %get-tuple-element.101.refs_20_), channel_id=1, source_target_pairs={{0,1},{1,0},{2,3},{3,2},{4,5},{5,4},{6,7},{7,6},{8,9},{9,8},{10,11... | collective-permute-start | bytes 36872 | tf_op jit(solution)/shard_map/ppermute | solution.py:636
  31.7 5.3 %collective-permute-start.13 = (f32[5,8,256]{2,1,0:T(8,128)S(1)}, f32[5,8,256]{2,1,0:T(8,128)S(1)}, u32[]{:S(2)}, u32[]{:S(2)}) collective-permute-start(f32[5,8,256]{2,1,0:T(8,128)S(1)} %get-tuple-element.102.refs_8_), channel_id=1, source_target_pairs={{0,24},{8,16},{16,8},{24,0},{1,25},{9,17},{17,9},{25,1},{2,26},{10... | collective-permute-start | bytes 122888 | tf_op jit(solution)/shard_map/ppermute | solution.py:615
  33.3 4.0 %collective-permute-start.12 = (f32[5,8,256]{2,1,0:T(8,128)S(1)}, f32[5,8,256]{2,1,0:T(8,128)S(1)}, u32[]{:S(2)}, u32[]{:S(2)}) collective-permute-start(f32[5,8,256]{2,1,0:T(8,128)S(1)} %get-tuple-element.102.refs_8_), channel_id=1, source_target_pairs={{0,16},{8,24},{16,0},{24,8},{1,17},{9,25},{17,1},{25,9},{2,18},{10... | collective-permute-start | bytes 122888 | tf_op jit(solution)/shard_map/ppermute | solution.py:615
  34.1 4.0 %collective-permute-start.11 = (f32[5,8,256]{2,1,0:T(8,128)S(1)}, f32[5,8,256]{2,1,0:T(8,128)S(1)}, u32[]{:S(2)}, u32[]{:S(2)}) collective-permute-start(f32[5,8,256]{2,1,0:T(8,128)S(1)} %get-tuple-element.102.refs_8_), channel_id=1, source_target_pairs={{0,8},{8,0},{16,24},{24,16},{1,9},{9,1},{17,25},{25,17},{2,10},{10... | collective-permute-start | bytes 122888 | tf_op jit(solution)/shard_map/ppermute | solution.py:615
  38.9 1.2 %collective-permute-start.14 = (f32[24,128]{1,0:T(8,128)S(1)}, f32[24,128]{1,0:T(8,128)S(1)}, u32[]{:S(2)}, u32[]{:S(2)}) collective-permute-start(f32[24,128]{1,0:T(8,128)S(1)} %get-tuple-element.111.refs_20_), channel_id=1, source_target_pairs={{0,1},{1,0},{2,3},{3,2},{4,5},{5,4},{6,7},{7,6},{8,9},{9,8},{10,11... | collective-permute-start | bytes 36872 | tf_op jit(solution)/shard_map/ppermute | solution.py:636
  41.7 5.3 %collective-permute-start.17 = (f32[4,8,256]{2,1,0:T(8,128)S(1)}, f32[4,8,256]{2,1,0:T(8,128)S(1)}, u32[]{:S(2)}, u32[]{:S(2)}) collective-permute-start(f32[4,8,256]{2,1,0:T(8,128)S(1)} %get-tuple-element.112.refs_4_), channel_id=1, source_target_pairs={{0,24},{8,16},{16,8},{24,0},{1,25},{9,17},{17,9},{25,1},{2,26},{10... | collective-permute-start | bytes 98312 | tf_op jit(solution)/shard_map/ppermute | solution.py:615
  43.9 3.9 %collective-permute-start.16 = (f32[4,8,256]{2,1,0:T(8,128)S(1)}, f32[4,8,256]{2,1,0:T(8,128)S(1)}, u32[]{:S(2)}, u32[]{:S(2)}) collective-permute-start(f32[4,8,256]{2,1,0:T(8,128)S(1)} %get-tuple-element.112.refs_4_), channel_id=1, source_target_pairs={{0,16},{8,24},{16,0},{24,8},{1,17},{9,25},{17,1},{25,9},{2,18},{10... | collective-permute-start | bytes 98312 | tf_op jit(solution)/shard_map/ppermute | solution.py:615
  44.4 3.9 %collective-permute-start.15 = (f32[4,8,256]{2,1,0:T(8,128)S(1)}, f32[4,8,256]{2,1,0:T(8,128)S(1)}, u32[]{:S(2)}, u32[]{:S(2)}) collective-permute-start(f32[4,8,256]{2,1,0:T(8,128)S(1)} %get-tuple-element.112.refs_4_), channel_id=1, source_target_pairs={{0,8},{8,0},{16,24},{24,16},{1,9},{9,1},{17,25},{25,17},{2,10},{10... | collective-permute-start | bytes 98312 | tf_op jit(solution)/shard_map/ppermute | solution.py:615
  50.4 7.2 %collective-permute-start.18 = (f32[64,256]{1,0:T(8,128)S(1)}, f32[64,256]{1,0:T(8,128)S(1)}, u32[]{:S(2)}, u32[]{:S(2)}) collective-permute-start(f32[64,256]{1,0:T(8,128)S(1)} %get-tuple-element.129), channel_id=1, source_target_pairs={{0,2},{4,6},{2,0},{6,4},{1,3},{5,7},{3,1},{7,5},{8,10},{12,14},{10... | collective-permute-start | bytes 196616 | tf_op jit(solution)/shard_map/ppermute | solution.py:645
  55.2 2.5 %collective-permute-start.19 = (f32[64,256]{1,0:T(8,128)S(1)}, f32[64,256]{1,0:T(8,128)S(1)}, u32[]{:S(2)}, u32[]{:S(2)}) collective-permute-start(f32[64,256]{1,0:T(8,128)S(1)} %get-tuple-element.130), channel_id=1, source_target_pairs={{2,4},{4,2},{3,5},{5,3},{10,12},{12,10},{11,13},{13,11},{18,20},{2... | collective-permute-start | bytes 196616 | tf_op jit(solution)/shard_map/ppermute | solution.py:646
  55.8 1.8 %collective-permute-start.20 = (f32[16,128]{1,0:T(8,128)S(1)}, f32[16,128]{1,0:T(8,128)S(1)}, u32[]{:S(2)}, u32[]{:S(2)}) collective-permute-start(f32[16,128]{1,0:T(8,128)S(1)} %get-tuple-element.131), channel_id=1, source_target_pairs={{0,1},{1,0},{2,3},{3,2},{4,5},{5,4},{6,7},{7,6},{8,9},{9,8},{10,11... | collective-permute-start | bytes 24584 | tf_op jit(solution)/shard_map/ppermute | solution.py:647
  (5 other events, 13.0 us)

commit v2 on v1

--- a/solution.py
+++ b/solution.py
@@ -134,18 +134,72 @@
         b_ref[3 + j] = jnp.where(is_even, before, after)
 
 
-def factor_rows(get_k, capm_extra, levels, out):
-    cap_ref, w_ref, r_ref, yr_ref, left_ref, g_ref = out
-    first_extra, last_extra = capm_extra
-    zero = jnp.zeros(w_ref.shape[1:], F32)
+def end_losses():
+    place, count = lax.axis_index("stack"), lax.axis_size("stack")
+    return (jnp.where(place == 0, F32(h_conv), F32(0.0)), jnp.where(place == count - 1, F32(h_conv), F32(0.0)))
+
+
+def lane_edge(tile_pair, i, pack):
+    low, high = tile_pair
+    at_low = lax.axis_index("phys") == 1
+    edge = jnp.where(at_low, low, high)
+    shift = jnp.where(at_low, i, lax.rem(i + 1, LANES))
+    lane = lax.broadcasted_iota(jnp.int32, edge.shape, 1)
+    return jnp.where(lane == i, pltpu.roll(edge, shift, 1), pack)
+
+
+def lane_edge_of(value, i, pack):
+    return lane_edge((value[:, :LANES], value[:, value.shape[1] - LANES :]), i, pack)
+
+
+def lane_unedge(pack, i):
+    at_low = lax.axis_index("phys") == 1
+    shift = jnp.where(at_low, lax.rem(LANES - i, LANES), LANES - 1 - i)
+    lane = lax.broadcasted_iota(jnp.int32, pack.shape, 1)
+    return jnp.where(lane == jnp.where(at_low, 0, LANES - 1), pltpu.roll(pack, shift, 1), 0.0)
+
+
+def add_at_edge(value, edge):
+    at_low = lax.axis_index("phys") == 1
+    tiles = [value[:, j : j + LANES] for j in range(0, value.shape[1], LANES)]
+    tiles[0] = tiles[0] + jnp.where(at_low, edge, 0.0)
+    tiles[-1] = tiles[-1] + jnp.where(at_low, 0.0, edge)
+    return jnp.concatenate(tiles, axis=1)
+
+
+def factor_main(code_ref, t_ref, q_ref, gx_ref, gy_ref, p_ref, pack_ref, k_ref, cap_ref, w_ref, r_ref, yr_ref, left_ref, g_ref):
+    levels, x, width = t_ref.shape
+    row = lax.broadcasted_iota(jnp.int32, (x, width), 0)
+    lane = lax.broadcasted_iota(jnp.int32, (x, width), 1)
+    first_loss, last_loss = end_losses()
+
+    def lateral(i, carry):
+        pack_t, pack_k = carry
+        k = by_code(code_ref[i], k_table)
+        k_ref[i] = k
+        cap = by_code(code_ref[i], cap_table, cap_unit)
+        cap_ref[i] = cap
+        gx = conductance(k, pltpu.roll(k, x - 1, 0), lat_unit)
+        gx = jnp.where(row == x - 1, 0.0, gx)
+        gx_ref[i] = gx
+        gy = conductance(k, pltpu.roll(k, width - 1, 1), lat_unit)
+        gy = jnp.where(lane == width - 1, 0.0, gy)
+        gy_ref[i] = gy
+        t = t_ref[i]
+        fy = gy * (pltpu.roll(t, width - 1, 1) - t)
+        fx = gx * (pltpu.roll(t, x - 1, 0) - t)
+        p_ref[i] = cap * t + q_ref[i] + fx - pltpu.roll(fx, 1, 0) + fy - pltpu.roll(fy, 1, 1)
+        return (lane_edge_of(t, i, pack_t), lane_edge_of(k, i, pack_k))
+
+    tile = jnp.zeros((x, LANES), F32)
+    pack_ref[0], pack_ref[1] = loop(levels, lateral, (tile, tile), unroll=8)
+    zero = jnp.zeros((x, width), F32)
 
     def forward(i, carry):
         ws, y, k_here = carry
-        k_next = get_k(jnp.minimum(i + 1, levels - 1))
-        cap = cap_by_k(k_here)
-        cap_ref[i] = cap
-        extra = jnp.where(i == 0, first_extra, 0.0) + jnp.where(i == levels - 1, last_extra, 0.0)
-        s = cap + extra + ws
+        k_next = k_ref[jnp.minimum(i + 1, levels - 1)]
+        loss = jnp.where(i == 0, first_loss, 0.0) + jnp.where(i == levels - 1, last_loss, 0.0)
+        s = cap_ref[i] + loss + ws
         u = jnp.where(i == levels - 1, 0.0, conductance(k_here, k_next))
         r = rcp(s + u)
         w = u * r
@@ -154,71 +208,20 @@
         yr_ref[i] = y * r
         return (w * s, y * w, k_next)
 
-    k_first = get_k(0)
-    _, _, k_last = loop(levels, forward, (zero, zero + 1.0, k_first))
-
-    def backward(i, left):
-        left = yr_ref[i] + w_ref[i] * left
+    loop(levels, forward, (zero, zero + 1.0, k_ref[0]))
+
+    def backward(i, carry):
+        left, right, pack_l, pack_r = carry
+        w = w_ref[i]
+        left = yr_ref[i] + w * left
+        right = jnp.where(i == levels - 1, r_ref[i], w * right)
         left_ref[i] = left
-        return left
-
-    left = loop(levels, backward, zero, reverse=True)
-    g_ref[0] = left + 0.5 * rcp(jnp.maximum(k_first, 1e-3))
+        return (left, right, lane_edge_of(left, i, pack_l), lane_edge_of(right, i, pack_r))
+
+    left, _, pack_ref[2], pack_ref[3] = loop(levels, backward, (zero, zero, tile, tile), reverse=True)
+    g_ref[0] = left + 0.5 * rcp(k_ref[0])
     g_ref[1] = yr_ref[levels - 1]
-    g_ref[2] = r_ref[levels - 1] + 0.5 * rcp(jnp.maximum(k_last, 1e-3))
-
-
-def end_losses():
-    place, count = lax.axis_index("stack"), lax.axis_size("stack")
-    return (jnp.where(place == 0, F32(h_conv), F32(0.0)), jnp.where(place == count - 1, F32(h_conv), F32(0.0)))
-
-
-def lane_edge(tile_pair, i, pack):
-    low, high = tile_pair
-    at_low = lax.axis_index("phys") == 1
-    edge = jnp.where(at_low, low, high)
-    shift = jnp.where(at_low, i, lax.rem(i + 1, LANES))
-    lane = lax.broadcasted_iota(jnp.int32, edge.shape, 1)
-    return jnp.where(lane == i, pltpu.roll(edge, shift, 1), pack)
-
-
-def lane_unedge(pack, i):
-    at_low = lax.axis_index("phys") == 1
-    shift = jnp.where(at_low, lax.rem(LANES - i, LANES), LANES - 1 - i)
-    moved = pltpu.roll(pack, shift, 1)
-    lane = lax.broadcasted_iota(jnp.int32, pack.shape, 1)
-    return (jnp.where((lane == 0) & at_low, moved, 0.0), jnp.where((lane == LANES - 1) & (~at_low), moved, 0.0))
-
-
-def add_lane_edges(value, pack, i):
-    low, high = lane_unedge(pack, i)
-    tiles = [value[:, j : j + LANES] for j in range(0, value.shape[1], LANES)]
-    tiles[0] = tiles[0] + low
-    tiles[-1] = tiles[-1] + high
-    return jnp.concatenate(tiles, axis=1)
-
-
-def factor_main(code_ref, t_ref, gx_ref, gy_ref, pack_ref, k_ref, *out):
-    levels, x, width = t_ref.shape
-    row = lax.broadcasted_iota(jnp.int32, (x, width), 0)
-    lane = lax.broadcasted_iota(jnp.int32, (x, width), 1)
-
-    def lateral(i, carry):
-        pack_t, pack_k = carry
-        k = by_code(code_ref[i], k_table)
-        k_ref[i] = k
-        gx = conductance(k, pltpu.roll(k, x - 1, 0), lat_unit)
-        gx_ref[i] = jnp.where(row == x - 1, 0.0, gx)
-        gy = conductance(k, pltpu.roll(k, width - 1, 1), lat_unit)
-        gy_ref[i] = jnp.where(lane == width - 1, 0.0, gy)
-        t = t_ref[i]
-        pack_t = lane_edge((t[:, :LANES], t[:, width - LANES :]), i, pack_t)
-        pack_k = lane_edge((k[:, :LANES], k[:, width - LANES :]), i, pack_k)
-        return (pack_t, pack_k)
-
-    zero = jnp.zeros((x, LANES), F32)
-    pack_ref[0], pack_ref[1] = loop(levels, lateral, (zero, zero))
-    factor_rows(lambda i: k_ref[i], end_losses(), levels, out)
+    g_ref[2] = r_ref[levels - 1] + 0.5 * rcp(k_ref[levels - 1])
 
 
 def assemble_halo(a_ref, b_ref, kh_ref, th_ref, qh_ref, pack_ref):
@@ -238,57 +241,88 @@
                     halo = jnp.where(rows[j], source[first + j, pl.ds(i, 1), :], halo)
             ref[i] = halo
             halos.append(halo)
-        t, k = halos[0], halos[1]
-        pack_t = lane_edge((t[:, :LANES], t[:, width - LANES :]), i, pack_t)
-        pack_k = lane_edge((k[:, :LANES], k[:, width - LANES :]), i, pack_k)
-        return (pack_t, pack_k)
+        return (lane_edge_of(halos[0], i, pack_t), lane_edge_of(halos[1], i, pack_k))
 
     zero = jnp.zeros((SUB, LANES), F32)
     pack_ref[0], pack_ref[1] = loop(levels, level, (zero, zero))
 
 
-def factor_halo(k_ref, kh_ref, gx_in, gx_ref, gxh_ref, gyh_ref, *out):
-    levels, x, width = k_ref.shape
+def first_side(p, t, k, w, r, left, th, kh, qh, gx_in, gx_ref, gxh, gyh, caph, wh, rh, yrh, lefth, z, zh, send, pack_ref):
+    levels, x, width = t.shape
     row = lax.broadcasted_iota(jnp.int32, (SUB, width), 0)
     lane = lax.broadcasted_iota(jnp.int32, (SUB, width), 1)
-
-    def lateral(i, carry):
-        k = kh_ref[i]
-        k_next = jnp.where(row == SUB - 1, k_ref[i, 0:1, :], pltpu.roll(k, SUB - 1, 0))
-        gxh_ref[i] = conductance(k, k_next, lat_unit)
-        gx_ref[i, x - 1 : x, :] = conductance(k_ref[i, x - 1 : x, :], k[0:1], lat_unit)
-        gy = conductance(k, pltpu.roll(k, width - 1, 1), lat_unit)
-        gyh_ref[i] = jnp.where(lane == width - 1, 0.0, gy)
-        return carry
-
-    loop(levels, lateral, 0)
-    factor_rows(lambda i: kh_ref[i], end_losses(), levels, out)
+    first_loss, last_loss = end_losses()
+
+    def forward(i, carry):
+        ws, yy, wy, k_here, wy_main, bf = carry
+        k_next = kh[jnp.minimum(i + 1, levels - 1)]
+        cap = cap_by_k(k_here)
+        caph[i] = cap
+        loss = jnp.where(i == 0, first_loss, 0.0) + jnp.where(i == levels - 1, last_loss, 0.0)
+        s = cap + loss + ws
+        u = jnp.where(i == levels - 1, 0.0, conductance(k_here, k_next))
+        rr = rcp(s + u)
+        ww = u * rr
+        wh[i] = ww
+        rh[i] = rr
+        yrh[i] = yy * rr
+
+        temp, t_main, k_main = th[i], t[i], k[i]
+        gx = conductance(k_here, jnp.where(row == SUB - 1, k_main[0:1], pltpu.roll(k_here, SUB - 1, 0)), lat_unit)
+        gxh[i] = gx
+        fx = gx * (jnp.where(row == SUB - 1, t_main[0:1], pltpu.roll(temp, SUB - 1, 0)) - temp)
+        g_top = conductance(k_main[x - SUB :], pltpu.roll(k_here, SUB - 1, 0), lat_unit)
+        gx_ref[i, x - 1 : x, :] = g_top[SUB - 1 :]
+        f_top = g_top * (pltpu.roll(temp, SUB - 1, 0) - t_main[x - SUB :])
+        gy = conductance(k_here, pltpu.roll(k_here, width - 1, 1), lat_unit)
+        gy = jnp.where(lane == width - 1, 0.0, gy)
+        gyh[i] = gy
+        fy = gy * (pltpu.roll(temp, width - 1, 1) - temp)
+        f_low = pltpu.roll(fx, 1, 0)
+        lateral = fx - jnp.where(row == 0, pltpu.roll(f_top, 1, 0), f_low) + fy - pltpu.roll(fy, 1, 1)
+        y = cap * temp + qh[i] + lateral + wy
+        zh[i] = y * rr
+
+        rhs = p[i]
+        parts = [rhs[j : j + SUB] for j in range(0, x, SUB)]
+        parts[0] = parts[0] - jnp.where(row == 0, f_low, 0.0)
+        parts[-1] = parts[-1] + jnp.where(row == SUB - 1, f_top, 0.0)
+        rhs = jnp.concatenate(parts, axis=0)
+        y_main = rhs + wy_main
+        z[i] = y_main * r[i]
+        return (ww * s, yy * ww, ww * y, k_next, w[i] * y_main, bf + left[i] * rhs)
+
+    zero, zero_main = jnp.zeros((SUB, width), F32), jnp.zeros((x, width), F32)
+    *_, bf = loop(levels, forward, (zero, zero + 1.0, zero, kh[0], zero_main, zero_main), unroll=8)
+
+    def backward(i, carry):
+        ll, right, value, pack_l, pack_r = carry
+        ww = wh[i]
+        ll = yrh[i] + ww * ll
+        right = jnp.where(i == levels - 1, rh[i], ww * right)
+        lefth[i] = ll
+        return (ll, right, zh[i] + ww * value, lane_edge_of(ll, i, pack_l), lane_edge_of(right, i, pack_r))
+
+    tile = jnp.zeros((SUB, LANES), F32)
+    ll, _, bfh, pack_ref[0], pack_ref[1] = loop(levels, backward, (zero, zero, zero, tile, tile), reverse=True)
+    for j in range(0, x, SUB):
+        send[j // SUB] = bf[j : j + SUB]
+        send[(x + j) // SUB] = z[levels - 1, j : j + SUB, :]
+    send[2 * x // SUB] = packed(bfh, zh[levels - 1])
+    half = [0.5 * rcp(jnp.maximum(kh[i], 1e-3)) for i in (0, levels - 1)]
+    send[2 * x // SUB + 1] = packed(ll + half[0], yrh[levels - 1])
+    send[2 * x // SUB + 2] = packed(rh[levels - 1] + half[1], rh[levels - 1])
 
 
 def both(main_ref, halo_ref, i):
     return jnp.concatenate([main_ref[i], halo_ref[i]], axis=0)
 
 
-def right_side(first, last, *refs):
-    (t, th, q, qh, cap, caph, gx, gxh, gy, gyh, w, wh, r, rh, left, lefth, km, kh, other_km, other_kh) = refs[:20]
-    refs = refs[20:]
-    own_k = jnp.concatenate([km[1], kh[1]], axis=0)
-    other_k = jnp.concatenate([other_km[1], other_kh[1]], axis=0)
-    if first:
-        gh, refs = refs[0], refs[1:]
-        own = jnp.concatenate([km[0], kh[0]], axis=0)
-        other = jnp.concatenate([other_km[0], other_kh[0]], axis=0)
-    else:
-        own, other = refs[0][...], refs[1][...]
-        refs = refs[2:]
+def right_side(last, *refs):
+    t, th, q, qh, cap, caph, gx, gxh, gy, gyh, w, wh, r, rh, left, lefth, *out = refs
     levels, x, width = t.shape
-    if last:
-        z, send = refs
-    else:
-        z, zh, send = refs
+    z, send = out[0], out[-1]
     rows = x if last else x + SUB
-    flow = conductance(own_k, other_k, lat_unit) * (other - own)
-    flow = flow[:rows]
 
     def pick(main_ref, halo_ref, i):
         return main_ref[i] if last else both(main_ref, halo_ref, i)
@@ -300,25 +334,67 @@
         fy = pick(gy, gyh, i) * (pltpu.roll(here, width - 1, 1) - here)
         fx = both(gx, gxh, i) * (pltpu.roll(temp, x + SUB - 1, 0) - temp)
         lateral = (fx - pltpu.roll(fx, 1, 0))[:rows] + fy - pltpu.roll(fy, 1, 1)
-        lateral = add_lane_edges(lateral, flow, i)
         rhs = pick(cap, caph, i) * here + pick(q, qh, i) + lateral
         y = rhs + wy
         zz = y * pick(r, rh, i)
         z[i] = zz[:x]
         if not last:
-            zh[i] = zz[x:]
+            out[1][i] = zz[x:]
         return (pick(w, wh, i) * y, bf + pick(left, lefth, i) * rhs)
 
     zero = jnp.zeros((rows, width), F32)
     _, bf = loop(levels, level, (zero, zero), unroll=16 if last else 8)
-    parts = [bf, pick(z, None if last else zh, levels - 1)]
+    parts = [bf, pick(z, None if last else out[1], levels - 1)]
     groups = [part[j : j + SUB] for part in parts for j in range(0, x, SUB)]
     if not last:
         groups.append(packed(*[part[x:] for part in parts]))
-    if first:
-        groups += [packed(gh[0], gh[1]), packed(gh[2], gh[2])]
     for j, group in enumerate(groups):
         send[j] = group
+
+
+def edge_flow(first, x, rows, *refs):
+    raw, pack, packh, packh_lr, other, otherh, *refs = refs
+    own_k, other_k = (jnp.concatenate([a[1], b[1]], axis=0)[:rows] for a, b in ((pack, packh), (other, otherh)))
+    if first:
+        own_t, other_t = (jnp.concatenate([a[0], b[0]], axis=0)[:rows] for a, b in ((pack, packh), (other, otherh)))
+    else:
+        own_t, other_t = refs[0][:rows], refs[1][:rows]
+    flow_ref, send = refs[-2:]
+    flow = conductance(own_k, other_k, lat_unit) * (other_t - own_t)
+    flow_ref[...] = flow
+    at_low = lax.axis_index("phys") == 1
+    lane = lax.broadcasted_iota(jnp.int32, flow.shape, 1)
+    changes = []
+    for j in (0, 1):
+        response = jnp.concatenate([pack[2 + j], packh_lr[j]], axis=0)[:rows]
+        change = jnp.sum(flow * response, axis=1, keepdims=True)
+        changes.append(jnp.where(lane == jnp.where(at_low, 0, LANES - 1), change, 0.0))
+    groups = [change[j : j + SUB] for change in changes for j in range(0, x, SUB)]
+    if rows > x:
+        groups.append(packed(*[change[x:] for change in changes]))
+    for j in range(send.shape[0]):
+        send[j] = add_at_edge(raw[j], groups[j]) if j < len(groups) else raw[j]
+
+
+def fix_sweep(flow, *refs):
+    half = (len(refs) - 0) // 4
+    w, r, z_in, z = (refs[j * half : (j + 1) * half] for j in range(4))
+    levels, x, width = z[0].shape
+    start = pl.multiple_of(jnp.where(lax.axis_index("phys") == 1, 0, width - LANES), LANES)
+    tile = pl.ds(start, LANES)
+
+    def pick(pair, i):
+        return jnp.concatenate([ref[i, :, tile] for ref in pair], axis=0)
+
+    def level(i, wy):
+        y = lane_unedge(flow[...], i) + wy
+        value = pick(z_in, i) + pick(r, i) * y
+        z[0][i, :, tile] = value[:x]
+        if half > 1:
+            z[1][i, :, tile] = value[x:]
+        return pick(w, i) * y
+
+    loop(levels, level, jnp.zeros(flow.shape, F32))
 
 
 def packed(a, b):
@@ -410,7 +486,7 @@
         value = both(z, zh, i) + top * both(yr, yrh, i) + add
         t[i] = value[:x]
         th[i] = value[x:]
-        pack = lane_edge((value[:, :LANES], value[:, width - LANES :]), i, pack)
+        pack = lane_edge_of(value, i, pack)
         return (both(w, wh, jnp.maximum(i - 1, 0)) * value, pack)
 
     init = (bottom * both(r, rh, levels - 1), jnp.zeros((rows, LANES), F32))
@@ -486,7 +562,7 @@
         creep_out[i] = new
         stress = m * (elastic - new)
         s[i] = stress
-        pack = lane_edge((stress[:, :LANES], stress[:, width - LANES :]), i, pack)
+        pack = lane_edge_of(stress, i, pack)
         return (w[jnp.maximum(i - 1, 0)] * value, pack)
 
     init = (bottom * r[levels - 1], jnp.zeros((x, LANES), F32))
@@ -541,7 +617,7 @@
             i = chunk * part + j
             total = inside[i] + jnp.where(a_row, xa[pl.ds(i, 1), :], 0.0)
             total = total + jnp.where(b_row, xb[pl.ds(i, 1), :], 0.0)
-            held[i] = add_lane_edges(total, other[...], i)
+            held[i] = add_at_edge(total, lane_unedge(other[...], i))
             return carry
 
         loop(part, level, 0)
@@ -577,44 +653,60 @@
     )
     rows_a = lax.ppermute(rows_a, "plane", plane_swaps[0])
     rows_b = lax.ppermute(rows_b, "plane", plane_swaps[1])
-    gx, gy, pack, k, *fact = call(
-        factor_main, (code, temp), [main, main, (2, x, LANES)] + [main] * 6 + [(3, x, width)], "factor_main", 40 * cells
+    gx, gy, part, pack, k, cap, w, r, yr, left, g = call(
+        factor_main,
+        (code, temp, source),
+        [main] * 3 + [(4, x, LANES)] + [main] * 6 + [(3, x, width)],
+        "factor_main",
+        60 * cells,
     )
-    cap, w, r, yr, left, g = fact
-    other_pack = lax.ppermute(pack, "phys", swap)
     za, zb = call(edge_layers, (code, flag, distortion, creep, hard, g), [(8, x, width)] * 2, "edge_layers", cells)
     za, g_two, zb = lax.ppermute(za, "stack", peers[0]), lax.ppermute(g, "stack", peers[1]), lax.ppermute(zb, "stack", peers[2])
     g_sets = [g, za, g_two, zb]
-    mod, exp, rate = call(prepare_creep, (code, flag), [main] * 3, "prepare_creep", 10 * cells)
+    other_pack = lax.ppermute(pack[:2], "phys", swap)
 
     kh, th, qh, packh = call(
-        assemble_halo, (rows_a, rows_b), [halo] * 3 + [(2, SUB, LANES)], "assemble_halo", cells, after=(rate, other_pack)
+        assemble_halo, (rows_a, rows_b), [halo] * 3 + [(2, SUB, LANES)], "assemble_halo", cells
     )
     other_packh = lax.ppermute(packh, "phys", swap)
-    gx, gxh, gyh, caph, wh, rh, yrh, lefth, gh = call(
-        factor_halo,
-        (k, kh, gx),
-        [main, halo, halo] + [halo] * 5 + [(3, SUB, width)],
-        "factor_halo",
-        20 * cells,
-        aliases={2: 0},
+    rows = x + SUB
+    groups = 2 * x // SUB
+    gx, gxh, gyh, caph, wh, rh, yrh, lefth, z, zh, send, packh_lr = call(
+        first_side,
+        (part, temp, k, w, r, left, th, kh, qh, gx),
+        [main] + [halo] * 7 + [main, halo, (groups + 3, SUB, width), (2, SUB, LANES)],
+        "first_side",
+        40 * cells,
+        aliases={9: 0},
     )
 
-    rows = x + SUB
     own = other = state = None
     for step in range(TSTEPS):
         first, last = step == 0, step == TSTEPS - 1
-        ins = [temp, th, source, qh, cap, caph, gx, gxh, gy, gyh, w, wh, r, rh, left, lefth]
-        ins += [pack, packh, other_pack, other_packh]
-        ins += [gh] if first else [own, other]
-        send = (2 * x // SUB + (3 if first else 0 if last else 1), SUB, width)
-        outs = call(
-            functools.partial(right_side, first, last), ins, [main, send] if last else [main, halo, send], "right_side", 30 * cells
+        if not first:
+            ins = (temp, th, source, qh, cap, caph, gx, gxh, gy, gyh, w, wh, r, rh, left, lefth)
+            send = (groups if last else groups + 1, SUB, width)
+            z, *zh, send = call(
+                functools.partial(right_side, last), ins, [main, send] if last else [main, halo, send], "right_side", 30 * cells
+            )
+            zh = zh[0] if zh else None
+        flow_rows = x if last else rows
+        lane_flow, send = call(
+            functools.partial(edge_flow, first, x, flow_rows),
+            [send, pack, packh, packh_lr, other_pack, other_packh] + ([] if first else [own, other]),
+            [(flow_rows, LANES), send.shape],
+            "edge_flow",
+            cells // 8,
         )
-        z, zh, own_b = outs[0], outs[1], outs[-1]
-        b_sets = [own_b] + [lax.ppermute(own_b, "stack", peer) for peer in peers]
+        b_sets = [send] + [lax.ppermute(send, "stack", peer) for peer in peers]
+        ins = [lane_flow, w, r, z] if last else [lane_flow, w, wh, r, rh, z, zh]
+        fixed = call(
+            fix_sweep, ins, [main] if last else [main, halo], "fix_sweep", cells, aliases={3: 0} if last else {5: 0, 6: 1}
+        )
+        z, zh = (fixed[0], None) if last else fixed
         if first:
             h_sets = b_sets
+            mod, exp, rate = call(prepare_creep, (code, flag), [main] * 3, "prepare_creep", 10 * cells, after=(z,))
         else:
             creep, hard, state = call(
                 functools.partial(creep_step, step == 1),
@@ -631,7 +723,7 @@
             [main, halo, (rows, LANES), layers],
             "column_solve",
             10 * cells,
-            after=() if first else (creep,),
+            after=(rate,) if first else (creep,),
         )
         other = lax.ppermute(own, "phys", swap)
 

time: 59.8 us -> 56.4 us (0.943)
  waiting for transfers between devices: 9.55 us -> 3.71 us
  Pallas kernels: 23.2 us -> 25.7 us
    ppermute x10, waiting for transfers between devices: 7.19 us -> 3.68 us  [the longest x9 3.68 us: per_device(): b_sets = [send] + [lax.ppermute(send, 'stack', peer) for peer in peers]]
    pallas_call x16 -> x21, Pallas kernels: 23.2 us -> 25.7 us  [call(): pl.pallas_call(kernel if after else body, in_specs=[HBM] * in_hbm + [VMEM...]
    ppermute x2, waiting for transfers between devices: 2.33 us -> 0.01 us  [per_device(): other = lax.ppermute(own, 'phys', swap)]
  transfers between devices with their start and end apart: 21 -> 21, of which waited for: 10 -> 5; matrix products, arithmetic and copies ran while one was open for 0% -> 0% of each run, Pallas kernels for 20% -> 32%
where the time goes in v2:
time: 56.4 us; the launch traced here: 55.4 us
  Pallas kernels  25.7 us (46%)
  starting transfers between devices  23.8 us (42%)
  waiting for transfers between devices  3.71 us (7%)
  local copies, waits for them, and re-layouts  1.25 us (2%)
  between operations  0.96 us (2%)
    pallas_call x21, Pallas kernels, call(): pl.pallas_call(kernel if after else body, in_specs=[HBM] * in_hbm + [VMEM...  25.7 us
    ppermute x9, starting transfers between devices, per_device(): b_sets = [send] + [lax.ppermute(send, 'stack', peer) for peer in peers]  10.5 us
    ppermute x1, starting transfers between devices, per_device(): xa = lax.ppermute(xa, 'plane', plane_swaps[0])  4.46 us
    ppermute x9, waiting for transfers between devices, per_device(): b_sets = [send] + [lax.ppermute(send, 'stack', peer) for peer in peers]  3.68 us
    ppermute x1, starting transfers between devices, per_device(): rows_a = lax.ppermute(rows_a, 'plane', plane_swaps[0])  3.09 us
    ppermute x1, starting transfers between devices, per_device(): lax.ppermute(za, 'stack', peers[0])  1.56 us
    ppermute x1, starting transfers between devices, per_device(): lax.ppermute(zb, 'stack', peers[2])  1.49 us
    unnamed x16, local copies, waits for them, and re-layouts  1.25 us
  transfers between devices with their start and end apart: 21, of which 5 were waited for; matrix products, arithmetic and copies ran while one was open for 0% of the time, Pallas kernels for 32%

profile of v2, /device:TPU:0, one launch (start us, length us, event | category | flops | bytes accessed | tf_op | source)
XLA Modules:
  0.0 55.4 jit_solution(14416527101732113853)
XLA Ops:
  0.7 2.7 %edge_rows.1 = (f32[6,64,256]{2,1,0:T(8,128)}, f32[6,64,256]{2,1,0:T(8,128)}) custom-call(f32[64,16,256]{2,1,0:T(8,128)} %t.1, s32[64,16,256]{2,1,0:T(8,128)} %refs_0_.1, f32[64,16,256]{2,1,0:T(8,128)} %refs_2_.3), custom_call_target="tpu_custom_call" | custom-call | flops 262144 | bytes 3932160 | tf_op jit(solution)/shard_map/edge_rows/pallas_call | solution.py:76
  3.4 3.1 %collective-permute-start.3 = (f32[6,64,256]{2,1,0:T(8,128)}, f32[6,64,256]{2,1,0:T(8,128)S(1)}, u32[]{:S(2)}, u32[]{:S(2)}) collective-permute-start(f32[6,64,256]{2,1,0:T(8,128)} %get-tuple-element.87), channel_id=1, source_target_pairs={{0,2},{4,6},{2,0},{6,4},{1,3},{5,7},{3,1},{7,5},{8,10},{12,14},{10... | collective-permute-start | bytes 1179656 | tf_op jit(solution)/shard_map/ppermute | solution.py:654
  6.5 0.8 %collective-permute-start.4 = (f32[6,64,256]{2,1,0:T(8,128)}, f32[6,64,256]{2,1,0:T(8,128)S(1)}, u32[]{:S(2)}, u32[]{:S(2)}) collective-permute-start(f32[6,64,256]{2,1,0:T(8,128)} %get-tuple-element.88), channel_id=1, source_target_pairs={{2,4},{4,2},{3,5},{5,3},{10,12},{12,10},{11,13},{13,11},{18,20},{2... | collective-permute-start | bytes 1179656 | tf_op jit(solution)/shard_map/ppermute | solution.py:655
  7.4 3.7 %factor_main.1 = (f32[64,16,256]{2,1,0:T(8,128)S(1)}, f32[64,16,256]{2,1,0:T(8,128)S(1)}, f32[64,16,256]{2,1,0:T(8,128)S(1)}, f32[4,16,128]{2,1,0:T(8,128)S(1)},...) custom-call(s32[64,16,256]{2,1,0:T(8,128)S(1)} %copy-done, ...), custom_call_target="tpu_custom_call" | custom-call | flops 15728640 | bytes 12664832 | tf_op jit(solution)/shard_map/factor_main/pallas_call | solution.py:76
  11.1 1.2 %copy-done.6 = f32[64,16,256]{2,1,0:T(8,128)S(1)} copy-done((f32[64,16,256]{2,1,0:T(8,128)S(1)}, f32[64,16,256]{2,1,0:T(8,128)}, u32[]{:S(2)}) %copy-start.6) | copy-done | bytes 1048600
  12.3 1.6 %collective-permute-start = (f32[8,16,256]{2,1,0:T(8,128)S(1)}, f32[8,16,256]{2,1,0:T(8,128)S(1)}, u32[]{:S(2)}, u32[]{:S(2)}) collective-permute-start(f32[8,16,256]{2,1,0:T(8,128)S(1)} %get-tuple-element.80), channel_id=1, source_target_pairs={{0,8},{8,0},{16,24},{24,16},{1,9},{9,1},{17,25},{25,17},{2,10},{10... | collective-permute-start | bytes 393224 | tf_op jit(solution)/shard_map/ppermute | solution.py:664
  13.9 1.5 %collective-permute-start.2 = (f32[8,16,256]{2,1,0:T(8,128)S(1)}, f32[8,16,256]{2,1,0:T(8,128)S(1)}, u32[]{:S(2)}, u32[]{:S(2)}) collective-permute-start(f32[8,16,256]{2,1,0:T(8,128)S(1)} %get-tuple-element.81), channel_id=1, source_target_pairs={{0,24},{8,16},{16,8},{24,0},{1,25},{9,17},{17,9},{25,1},{2,26},{10... | collective-permute-start | bytes 393224 | tf_op jit(solution)/shard_map/ppermute | solution.py:664
  15.9 0.7 %assemble_halo.1 = (f32[64,8,256]{2,1,0:T(8,128)S(1)}, f32[64,8,256]{2,1,0:T(8,128)S(1)}, f32[64,8,256]{2,1,0:T(8,128)S(1)}, f32[2,8,128]{2,1,0:T(8,128)S(1)}) custom-call(f32[6,64,256]{2,1,0:T(8,128)S(1)} %collective-permute-done.3.a_ref, f32[6,64,256]{2,1,0:T(8,128)S(1)} %collective-permute-done.4.b_ref), custom_call_target="tpu_custom_call" | custom-call | flops 262144 | bytes 2367488 | tf_op jit(solution)/shard_map/assemble_halo/pallas_call | solution.py:76
  17.2 2.3 %first_side.1 = (f32[64,16,256]{2,1,0:T(8,128)S(1)}, f32[64,8,256]{2,1,0:T(8,128)S(1)}, f32[64,8,256]{2,1,0:T(8,128)S(1)}, f32[64,8,256]{2,1,0:T(8,128)S(1)}, f3...) custom-call(f32[64,16,256]{2,1,0:T(8,128)S(1)} %get-tuple-element.82, ...), custom_call_target="tpu_custom_call", output_to_operand_aliasing={{0}: (9, {})} | custom-call | flops 10485760 | bytes 15269888 | tf_op jit(solution)/shard_map/first_side/pallas_call | solution.py:76
  19.6 2.6 %collective-permute-start.9 = (f32[7,8,256]{2,1,0:T(8,128)S(1)}, f32[7,8,256]{2,1,0:T(8,128)S(1)}, u32[]{:S(2)}, u32[]{:S(2)}) collective-permute-start(f32[7,8,256]{2,1,0:T(8,128)S(1)} %get-tuple-element.97.refs_4_), channel_id=1, source_target_pairs={{0,24},{8,16},{16,8},{24,0},{1,25},{9,17},{17,9},{25,1},{2,26},{10... | collective-permute-start | bytes 172040 | tf_op jit(solution)/shard_map/ppermute | solution.py:701
  24.7 1.6 %collective-permute-done.8.refs_6_ = f32[7,8,256]{2,1,0:T(8,128)S(1)} collective-permute-done((f32[7,8,256]{2,1,0:T(8,128)S(1)}, f32[7,8,256]{2,1,0:T(8,128)S(1)}, u32[]{:S(2)}, u32[]{:S(2)}) %collective-permute-start.8) | collective-permute-done | bytes 57376 | tf_op jit(solution)/shard_map/ppermute | solution.py:701
  26.9 0.9 %column_solve.2 = (f32[64,16,256]{2,1,0:T(8,128)S(1)}, f32[64,8,256]{2,1,0:T(8,128)S(1)}, f32[24,128]{1,0:T(8,128)S(1)}, f32[2,16,256]{2,1,0:T(8,128)S(1)}) custom-call(f32[3,16,256]{2,1,0:T(8,128)S(1)} %get-tuple-element.79.g.refs_0_, f32[8,16,256]{2,1,0:T(8,128)S(1)} %collective-permute-done.refs_1_.refs_9_.refs_13_, ...), custom_call_target="tpu_custom_call" | custom-call | flops 2621440 | bytes 8499200 | tf_op jit(solution)/shard_map/column_solve/pallas_call | solution.py:76
  27.8 2.1 %right_side.2 = (f32[64,16,256]{2,1,0:T(8,128)S(1)}, f32[64,8,256]{2,1,0:T(8,128)S(1)}, f32[5,8,256]{2,1,0:T(8,128)S(1)}) custom-call(f32[64,16,256]{2,1,0:T(8,128)S(1)} %get-tuple-element.108.refs_0_, f32[64,8,256]{2,1,0:T(8,128)S(1)} %get-tuple-element.109.refs_1_, f32[64,16,256]{2,1,0:T(8,128)S(1)} %copy-done.1, ...), custom_call_target="tpu_custom_call" | custom-call | flops 7864320 | bytes 14196736 | tf_op jit(solution)/shard_map/right_side/pallas_call | solution.py:76
  30.0 1.5 %collective-permute-start.13 = (f32[5,8,256]{2,1,0:T(8,128)S(1)}, f32[5,8,256]{2,1,0:T(8,128)S(1)}, u32[]{:S(2)}, u32[]{:S(2)}) collective-permute-start(f32[5,8,256]{2,1,0:T(8,128)S(1)} %get-tuple-element.119.refs_8_), channel_id=1, source_target_pairs={{0,24},{8,16},{16,8},{24,0},{1,25},{9,17},{17,9},{25,1},{2,26},{10... | collective-permute-start | bytes 122888 | tf_op jit(solution)/shard_map/ppermute | solution.py:701
  32.0 1.6 %collective-permute-start.11 = (f32[5,8,256]{2,1,0:T(8,128)S(1)}, f32[5,8,256]{2,1,0:T(8,128)S(1)}, u32[]{:S(2)}, u32[]{:S(2)}) collective-permute-start(f32[5,8,256]{2,1,0:T(8,128)S(1)} %get-tuple-element.119.refs_8_), channel_id=1, source_target_pairs={{0,8},{8,0},{16,24},{24,16},{1,9},{9,1},{17,25},{25,17},{2,10},{10... | collective-permute-start | bytes 122888 | tf_op jit(solution)/shard_map/ppermute | solution.py:701
  33.6 1.7 %creep_step.2 = (f32[64,16,256]{2,1,0:T(8,128)S(1)}, f32[64,16,256]{2,1,0:T(8,128)S(1)}, f32[4,16,256]{2,1,0:T(8,128)S(1)}) custom-call(f32[64,16,256]{2,1,0:T(8,128)S(1)} %get-tuple-element.108.refs_0_, f32[64,16,256]{2,1,0:T(8,128)S(1)} %get-tuple-element.125.refs_1_.refs_16_, f32[64,16,256]{2,1,0:T(8,128)S(1)} %get-tuple-element.126.refs_2_.refs_17_, ...), custom_call_target="tpu_custom_call" | custom-call | flops 15728640 | bytes 10846208 | tf_op jit(solution)/shard_map/creep_step/pallas_call | solution.py:76
  36.0 0.9 %column_solve.3 = (f32[64,16,256]{2,1,0:T(8,128)S(1)}, f32[64,8,256]{2,1,0:T(8,128)S(1)}, f32[24,128]{1,0:T(8,128)S(1)}, f32[2,16,256]{2,1,0:T(8,128)S(1)}) custom-call(f32[3,16,256]{2,1,0:T(8,128)S(1)} %get-tuple-element.79.g.refs_0_, f32[8,16,256]{2,1,0:T(8,128)S(1)} %collective-permute-done.refs_1_.refs_9_.refs_13_, ...), custom_call_target="tpu_custom_call" | custom-call | flops 2621440 | bytes 8663040 | tf_op jit(solution)/shard_map/column_solve/pallas_call | solution.py:76
  36.9 1.3 %right_side.3 = (f32[64,16,256]{2,1,0:T(8,128)S(1)}, f32[4,8,256]{2,1,0:T(8,128)S(1)}) custom-call(f32[64,16,256]{2,1,0:T(8,128)S(1)} %get-tuple-element.129.refs_0_, f32[64,8,256]{2,1,0:T(8,128)S(1)} %get-tuple-element.130.refs_1_, f32[64,16,256]{2,1,0:T(8,128)S(1)} %copy-done.1, f32[64,8,256]{2,1,0:T(8,128)S(1)} %get-tuple-element.91.qh.refs_3_, ...), custom_call_target="tpu_custom_call" | custom-call | flops 7864320 | bytes 13664256 | tf_op jit(solution)/shard_map/right_side/pallas_call | solution.py:76
  38.3 2.5 %collective-permute-start.17 = (f32[4,8,256]{2,1,0:T(8,128)S(1)}, f32[4,8,256]{2,1,0:T(8,128)S(1)}, u32[]{:S(2)}, u32[]{:S(2)}) collective-permute-start(f32[4,8,256]{2,1,0:T(8,128)S(1)} %get-tuple-element.133.refs_4_), channel_id=1, source_target_pairs={{0,24},{8,16},{16,8},{24,0},{1,25},{9,17},{17,9},{25,1},{2,26},{10... | collective-permute-start | bytes 98312 | tf_op jit(solution)/shard_map/ppermute | solution.py:701
  41.8 1.8 %creep_step.3 = (f32[64,16,256]{2,1,0:T(8,128)S(1)}, f32[64,16,256]{2,1,0:T(8,128)S(1)}, f32[4,16,256]{2,1,0:T(8,128)S(1)}) custom-call(f32[64,16,256]{2,1,0:T(8,128)S(1)} %get-tuple-element.129.refs_0_, f32[64,16,256]{2,1,0:T(8,128)S(1)} %get-tuple-element.125.refs_1_.refs_16_, f32[64,16,256]{2,1,0:T(8,128)S(1)} %get-tuple-element.126.refs_2_.refs_17_, ...), custom_call_target="tpu_custom_call" | custom-call | flops 15728640 | bytes 10911744 | tf_op jit(solution)/shard_map/creep_step/pallas_call | solution.py:76
  45.3 2.1 %solve_and_creep.1 = (f32[64,16,256]{2,1,0:T(8,128)S(1)}, f32[64,16,256]{2,1,0:T(8,128)S(1)}, f32[64,16,256]{2,1,0:T(8,128)S(1)}, f32[64,16,256]{2,1,0:T(8,128)S...) custom-call(f32[3,16,256]{2,1,0:T(8,128)S(1)} %get-tuple-element.79.g.re, ...), custom_call_target="tpu_custom_call" | custom-call | flops 18350080 | bytes 16719872 | tf_op jit(solution)/shard_map/solve_and_creep/pallas_call | solution.py:76
  47.4 4.5 %collective-permute-start.18 = (f32[64,256]{1,0:T(8,128)S(1)}, f32[64,256]{1,0:T(8,128)S(1)}, u32[]{:S(2)}, u32[]{:S(2)}) collective-permute-start(f32[64,256]{1,0:T(8,128)S(1)} %get-tuple-element.151), channel_id=1, source_target_pairs={{0,2},{4,6},{2,0},{6,4},{1,3},{5,7},{3,1},{7,5},{8,10},{12,14},{10... | collective-permute-start | bytes 196616 | tf_op jit(solution)/shard_map/ppermute | solution.py:737
  52.6 1.7 %balance_inside.1 = (f32[64,16,256]{2,1,0:T(8,128)}, f32[64,16,256]{2,1,0:T(8,128)}, f32[64,16,256]{2,1,0:T(8,128)}, f32[64,16,256]{2,1,0:T(8,128)S(1)}) custom-call(f32[64,16,256]{2,1,0:T(8,128)S(1)} %get-tuple-element.142.s, f32[2,16,256]{2,1,0:T(8,128)S(1)} %get-tuple-element.143.zs, f32[64,16,256]{2,1,0:T(8,128)S(1)} %get-tuple-element.144.t, ...), custom_call_target="tpu_custom_call" | custom-call | flops 5242880 | bytes 8421376 | tf_op jit(solution)/shard_map/balance_inside/pallas_call | solution.py:76
  54.3 1.1 %balance_edges.1 = f32[64,16,256]{2,1,0:T(8,128)} custom-call(f32[64,16,256]{2,1,0:T(8,128)S(1)} %get-tuple-element.150.inside, f32[64,256]{1,0:T(8,128)S(1)} %collective-permute-done.18.xa, f32[64,256]{1,0:T(8,128)S(1)} %collective-permute-done.19.xb, f32[16,128]{1,0:T(8,128)S(1)} %collective-permute-done.20.other), custom_call_target="tpu_custom_call" | custom-call | flops 2621440 | bytes 2236416 | tf_op jit(solution)/shard_map/balance_edges/pallas_call | solution.py:76
  (56 shorter events, 9.0 us)
Async XLA Ops:
  0.6 6.7 %copy-start = (s32[64,16,256]{2,1,0:T(8,128)S(1)}, s32[64,16,256]{2,1,0:T(8,128)}, u32[]{:S(2)}) copy-start(s32[64,16,256]{2,1,0:T(8,128)} %refs_0_.1) | copy-start | bytes 3145732
  0.6 6.7 %copy-start.1 = (f32[64,16,256]{2,1,0:T(8,128)S(1)}, f32[64,16,256]{2,1,0:T(8,128)}, u32[]{:S(2)}) copy-start(f32[64,16,256]{2,1,0:T(8,128)} %refs_2_.3) | copy-start | bytes 3145732
  0.7 6.7 %copy-start.3 = (f32[64,16,256]{2,1,0:T(8,128)S(1)}, f32[64,16,256]{2,1,0:T(8,128)}, u32[]{:S(2)}) copy-start(f32[64,16,256]{2,1,0:T(8,128)} %t.1) | copy-start | bytes 3145732
  3.4 12.5 %collective-permute-start.3 = (f32[6,64,256]{2,1,0:T(8,128)}, f32[6,64,256]{2,1,0:T(8,128)S(1)}, u32[]{:S(2)}, u32[]{:S(2)}) collective-permute-start(f32[6,64,256]{2,1,0:T(8,128)} %get-tuple-element.87), channel_id=1, source_target_pairs={{0,2},{4,6},{2,0},{6,4},{1,3},{5,7},{3,1},{7,5},{8,10},{12,14},{10... | collective-permute-start | bytes 1179656 | tf_op jit(solution)/shard_map/ppermute | solution.py:654
  6.5 9.4 %collective-permute-start.4 = (f32[6,64,256]{2,1,0:T(8,128)}, f32[6,64,256]{2,1,0:T(8,128)S(1)}, u32[]{:S(2)}, u32[]{:S(2)}) collective-permute-start(f32[6,64,256]{2,1,0:T(8,128)} %get-tuple-element.88), channel_id=1, source_target_pairs={{2,4},{4,2},{3,5},{5,3},{10,12},{12,10},{11,13},{13,11},{18,20},{2... | collective-permute-start | bytes 1179656 | tf_op jit(solution)/shard_map/ppermute | solution.py:655
  12.3 12.1 %collective-permute-start = (f32[8,16,256]{2,1,0:T(8,128)S(1)}, f32[8,16,256]{2,1,0:T(8,128)S(1)}, u32[]{:S(2)}, u32[]{:S(2)}) collective-permute-start(f32[8,16,256]{2,1,0:T(8,128)S(1)} %get-tuple-element.80), channel_id=1, source_target_pairs={{0,8},{8,0},{16,24},{24,16},{1,9},{9,1},{17,25},{25,17},{2,10},{10... | collective-permute-start | bytes 393224 | tf_op jit(solution)/shard_map/ppermute | solution.py:664
  13.9 10.5 %collective-permute-start.2 = (f32[8,16,256]{2,1,0:T(8,128)S(1)}, f32[8,16,256]{2,1,0:T(8,128)S(1)}, u32[]{:S(2)}, u32[]{:S(2)}) collective-permute-start(f32[8,16,256]{2,1,0:T(8,128)S(1)} %get-tuple-element.81), channel_id=1, source_target_pairs={{0,24},{8,16},{16,8},{24,0},{1,25},{9,17},{17,9},{25,1},{2,26},{10... | collective-permute-start | bytes 393224 | tf_op jit(solution)/shard_map/ppermute | solution.py:664
  15.4 7.3 %collective-permute-start.1 = (f32[3,16,256]{2,1,0:T(8,128)S(1)}, f32[3,16,256]{2,1,0:T(8,128)S(1)}, u32[]{:S(2)}, u32[]{:S(2)}) collective-permute-start(f32[3,16,256]{2,1,0:T(8,128)S(1)} %get-tuple-element.79.g.refs_0_), channel_id=1, source_target_pairs={{0,16},{8,24},{16,0},{24,8},{1,17},{9,25},{17,1},{25,9},{2,18},{10... | collective-permute-start | bytes 147464 | tf_op jit(solution)/shard_map/ppermute | solution.py:664
  15.9 3.6 %collective-permute-start.5 = (f32[2,16,128]{2,1,0:T(8,128)S(1)}, f32[2,16,128]{2,1,0:T(8,128)S(1)}, u32[]{:S(2)}, u32[]{:S(2)}) collective-permute-start(f32[2,16,128]{2,1,0:T(8,128)S(1)} %slice.3), channel_id=1, source_target_pairs={{0,1},{1,0},{2,3},{3,2},{4,5},{5,4},{6,7},{7,6},{8,9},{9,8},{10,11... | collective-permute-start | bytes 49160 | tf_op jit(solution)/shard_map/ppermute | solution.py:666
  16.6 2.9 %collective-permute-start.6 = (f32[2,8,128]{2,1,0:T(8,128)S(1)}, f32[2,8,128]{2,1,0:T(8,128)S(1)}, u32[]{:S(2)}, u32[]{:S(2)}) collective-permute-start(f32[2,8,128]{2,1,0:T(8,128)S(1)} %get-tuple-element.95.refs_2_), channel_id=1, source_target_pairs={{0,1},{1,0},{2,3},{3,2},{4,5},{5,4},{6,7},{7,6},{8,9},{9,8},{10,11... | collective-permute-start | bytes 24584 | tf_op jit(solution)/shard_map/ppermute | solution.py:671
  19.6 5.1 %collective-permute-start.9 = (f32[7,8,256]{2,1,0:T(8,128)S(1)}, f32[7,8,256]{2,1,0:T(8,128)S(1)}, u32[]{:S(2)}, u32[]{:S(2)}) collective-permute-start(f32[7,8,256]{2,1,0:T(8,128)S(1)} %get-tuple-element.97.refs_4_), channel_id=1, source_target_pairs={{0,24},{8,16},{16,8},{24,0},{1,25},{9,17},{17,9},{25,1},{2,26},{10... | collective-permute-start | bytes 172040 | tf_op jit(solution)/shard_map/ppermute | solution.py:701
  22.2 4.2 %collective-permute-start.8 = (f32[7,8,256]{2,1,0:T(8,128)S(1)}, f32[7,8,256]{2,1,0:T(8,128)S(1)}, u32[]{:S(2)}, u32[]{:S(2)}) collective-permute-start(f32[7,8,256]{2,1,0:T(8,128)S(1)} %get-tuple-element.97.refs_4_), channel_id=1, source_target_pairs={{0,16},{8,24},{16,0},{24,8},{1,17},{9,25},{17,1},{25,9},{2,18},{10... | collective-permute-start | bytes 172040 | tf_op jit(solution)/shard_map/ppermute | solution.py:701
  22.7 4.2 %collective-permute-start.7 = (f32[7,8,256]{2,1,0:T(8,128)S(1)}, f32[7,8,256]{2,1,0:T(8,128)S(1)}, u32[]{:S(2)}, u32[]{:S(2)}) collective-permute-start(f32[7,8,256]{2,1,0:T(8,128)S(1)} %get-tuple-element.97.refs_4_), channel_id=1, source_target_pairs={{0,8},{8,0},{16,24},{24,16},{1,9},{9,1},{17,25},{25,17},{2,10},{10... | collective-permute-start | bytes 172040 | tf_op jit(solution)/shard_map/ppermute | solution.py:701
  27.7 2.2 %collective-permute-start.10 = (f32[24,128]{1,0:T(8,128)S(1)}, f32[24,128]{1,0:T(8,128)S(1)}, u32[]{:S(2)}, u32[]{:S(2)}) collective-permute-start(f32[24,128]{1,0:T(8,128)S(1)} %get-tuple-element.118.refs_6_), channel_id=1, source_target_pairs={{0,1},{1,0},{2,3},{3,2},{4,5},{5,4},{6,7},{7,6},{8,9},{9,8},{10,11... | collective-permute-start | bytes 36872 | tf_op jit(solution)/shard_map/ppermute | solution.py:728
  30.0 5.9 %collective-permute-start.13 = (f32[5,8,256]{2,1,0:T(8,128)S(1)}, f32[5,8,256]{2,1,0:T(8,128)S(1)}, u32[]{:S(2)}, u32[]{:S(2)}) collective-permute-start(f32[5,8,256]{2,1,0:T(8,128)S(1)} %get-tuple-element.119.refs_8_), channel_id=1, source_target_pairs={{0,24},{8,16},{16,8},{24,0},{1,25},{9,17},{17,9},{25,1},{2,26},{10... | collective-permute-start | bytes 122888 | tf_op jit(solution)/shard_map/ppermute | solution.py:701
  31.6 4.4 %collective-permute-start.12 = (f32[5,8,256]{2,1,0:T(8,128)S(1)}, f32[5,8,256]{2,1,0:T(8,128)S(1)}, u32[]{:S(2)}, u32[]{:S(2)}) collective-permute-start(f32[5,8,256]{2,1,0:T(8,128)S(1)} %get-tuple-element.119.refs_8_), channel_id=1, source_target_pairs={{0,16},{8,24},{16,0},{24,8},{1,17},{9,25},{17,1},{25,9},{2,18},{10... | collective-permute-start | bytes 122888 | tf_op jit(solution)/shard_map/ppermute | solution.py:701
  32.0 4.0 %collective-permute-start.11 = (f32[5,8,256]{2,1,0:T(8,128)S(1)}, f32[5,8,256]{2,1,0:T(8,128)S(1)}, u32[]{:S(2)}, u32[]{:S(2)}) collective-permute-start(f32[5,8,256]{2,1,0:T(8,128)S(1)} %get-tuple-element.119.refs_8_), channel_id=1, source_target_pairs={{0,8},{8,0},{16,24},{24,16},{1,9},{9,1},{17,25},{25,17},{2,10},{10... | collective-permute-start | bytes 122888 | tf_op jit(solution)/shard_map/ppermute | solution.py:701
  36.8 1.4 %collective-permute-start.14 = (f32[24,128]{1,0:T(8,128)S(1)}, f32[24,128]{1,0:T(8,128)S(1)}, u32[]{:S(2)}, u32[]{:S(2)}) collective-permute-start(f32[24,128]{1,0:T(8,128)S(1)} %get-tuple-element.132.refs_6_), channel_id=1, source_target_pairs={{0,1},{1,0},{2,3},{3,2},{4,5},{5,4},{6,7},{7,6},{8,9},{9,8},{10,11... | collective-permute-start | bytes 36872 | tf_op jit(solution)/shard_map/ppermute | solution.py:728
  38.3 5.8 %collective-permute-start.17 = (f32[4,8,256]{2,1,0:T(8,128)S(1)}, f32[4,8,256]{2,1,0:T(8,128)S(1)}, u32[]{:S(2)}, u32[]{:S(2)}) collective-permute-start(f32[4,8,256]{2,1,0:T(8,128)S(1)} %get-tuple-element.133.refs_4_), channel_id=1, source_target_pairs={{0,24},{8,16},{16,8},{24,0},{1,25},{9,17},{17,9},{25,1},{2,26},{10... | collective-permute-start | bytes 98312 | tf_op jit(solution)/shard_map/ppermute | solution.py:701
  40.9 3.9 %collective-permute-start.16 = (f32[4,8,256]{2,1,0:T(8,128)S(1)}, f32[4,8,256]{2,1,0:T(8,128)S(1)}, u32[]{:S(2)}, u32[]{:S(2)}) collective-permute-start(f32[4,8,256]{2,1,0:T(8,128)S(1)} %get-tuple-element.133.refs_4_), channel_id=1, source_target_pairs={{0,16},{8,24},{16,0},{24,8},{1,17},{9,25},{17,1},{25,9},{2,18},{10... | collective-permute-start | bytes 98312 | tf_op jit(solution)/shard_map/ppermute | solution.py:701
  41.4 3.9 %collective-permute-start.15 = (f32[4,8,256]{2,1,0:T(8,128)S(1)}, f32[4,8,256]{2,1,0:T(8,128)S(1)}, u32[]{:S(2)}, u32[]{:S(2)}) collective-permute-start(f32[4,8,256]{2,1,0:T(8,128)S(1)} %get-tuple-element.133.refs_4_), channel_id=1, source_target_pairs={{0,8},{8,0},{16,24},{24,16},{1,9},{9,1},{17,25},{25,17},{2,10},{10... | collective-permute-start | bytes 98312 | tf_op jit(solution)/shard_map/ppermute | solution.py:701
  47.4 6.9 %collective-permute-start.18 = (f32[64,256]{1,0:T(8,128)S(1)}, f32[64,256]{1,0:T(8,128)S(1)}, u32[]{:S(2)}, u32[]{:S(2)}) collective-permute-start(f32[64,256]{1,0:T(8,128)S(1)} %get-tuple-element.151), channel_id=1, source_target_pairs={{0,2},{4,6},{2,0},{6,4},{1,3},{5,7},{3,1},{7,5},{8,10},{12,14},{10... | collective-permute-start | bytes 196616 | tf_op jit(solution)/shard_map/ppermute | solution.py:737
  51.8 2.5 %collective-permute-start.19 = (f32[64,256]{1,0:T(8,128)S(1)}, f32[64,256]{1,0:T(8,128)S(1)}, u32[]{:S(2)}, u32[]{:S(2)}) collective-permute-start(f32[64,256]{1,0:T(8,128)S(1)} %get-tuple-element.152), channel_id=1, source_target_pairs={{2,4},{4,2},{3,5},{5,3},{10,12},{12,10},{11,13},{13,11},{18,20},{2... | collective-permute-start | bytes 196616 | tf_op jit(solution)/shard_map/ppermute | solution.py:738
  52.5 1.8 %collective-permute-start.20 = (f32[16,128]{1,0:T(8,128)S(1)}, f32[16,128]{1,0:T(8,128)S(1)}, u32[]{:S(2)}, u32[]{:S(2)}) collective-permute-start(f32[16,128]{1,0:T(8,128)S(1)} %get-tuple-element.153), channel_id=1, source_target_pairs={{0,1},{1,0},{2,3},{3,2},{4,5},{5,4},{6,7},{7,6},{8,9},{9,8},{10,11... | collective-permute-start | bytes 24584 | tf_op jit(solution)/shard_map/ppermute | solution.py:739
  (5 other events, 20.6 us)

commit v3 on v2

--- a/solution.py
+++ b/solution.py
@@ -23,6 +23,8 @@
 LANES = 128
 SUB = 8
 F32 = jnp.float32
+
+U_FACTOR, U_SIDE, U_RIGHT, U_LAST, U_SOLVE, U_CREEP, U_FINAL, U_BACK = 8, 8, 16, 16, 64, 16, 16, 64
 
 
 def loop(count, body, init, unroll=16, reverse=False):
@@ -97,29 +99,39 @@
     return lax.rem(lax.axis_index(axis), 2) == 0
 
 
-def edge_rows(t_in, code_in, q_in, a_ref, b_ref, t, code, q, sem):
-    levels, x, width = t_in.shape
-    rows = (x - 1, x - 2, x - 3, 0, 1, 2)
-    copies = []
-    for j, row in enumerate(rows):
-        for entry, (source, held) in enumerate(((t_in, t), (code_in, code), (q_in, q))):
-            if entry < 2 or j % 3 < 2:
-                copies.append(pltpu.make_async_copy(source.at[:, row, :], held.at[j], sem.at[entry, j]))
-    for copy in copies:
+def edge_rows(t_in, code_in, q_in, a_ref, b_ref, made, t, code, sem_in, sem_out):
+    x = t_in.shape[1]
+    is_even = even("plane")
+    reads, writes = [], []
+    for j in range(2):
+        at_top = is_even if j == 0 else ~is_even
+        near, far, beyond = (jnp.where(at_top, x - 1 - d, d) for d in range(3))
+        for entry, (source, row, held) in enumerate(
+            (
+                (code_in, near, code.at[j, 0]),
+                (code_in, far, code.at[j, 1]),
+                (code_in, beyond, code.at[j, 2]),
+                (t_in, far, made.at[j, 1]),
+                (t_in, beyond, t.at[j]),
+                (q_in, far, made.at[j, 5]),
+                (t_in, near, made.at[j, 0]),
+                (q_in, near, made.at[j, 4]),
+            )
+        ):
+            reads.append(pltpu.make_async_copy(source.at[:, row, :], held, sem_in.at[j, entry]))
+    for copy in reads:
         copy.start()
-    for copy in copies:
+    for j, out in enumerate((a_ref, b_ref)):
+        for copy in reads[8 * j : 8 * j + 8]:
+            copy.wait()
+        made[j, 2] = by_code(code[j, 0], k_table)
+        k2, k3 = by_code(code[j, 1], k_table), by_code(code[j, 2], k_table)
+        made[j, 3] = k2
+        made[j, 5] = made[j, 5] + conductance(k2, k3, lat_unit) * (t[j] - made[j, 1])
+        writes.append(pltpu.make_async_copy(made.at[j], out, sem_out.at[j]))
+        writes[-1].start()
+    for copy in writes:
         copy.wait()
-    is_even = even("plane")
-
-    def side(near):
-        k1, k2, k3 = (by_code(code[near + j], k_table) for j in range(3))
-        flow = conductance(k2, k3, lat_unit) * (t[near + 2] - t[near + 1])
-        return (t[near], t[near + 1], k1, k2, q[near], q[near + 1] + flow)
-
-    top, bottom = side(0), side(3)
-    for i in range(6):
-        a_ref[i] = jnp.where(is_even, top[i], bottom[i])
-        b_ref[i] = jnp.where(is_even, bottom[i], top[i])
 
 
 def edge_layers(code, flag, dist, creep, hard, g, a_ref, b_ref):
@@ -167,39 +179,51 @@
     return jnp.concatenate(tiles, axis=1)
 
 
-def factor_main(code_ref, t_ref, q_ref, gx_ref, gy_ref, p_ref, pack_ref, k_ref, cap_ref, w_ref, r_ref, yr_ref, left_ref, g_ref):
+def from_beside(t, g, axis):
+    return g * pltpu.roll(t, t.shape[axis] - 1, axis) + pltpu.roll(g * t, 1, axis)
+
+
+def lateral_main(k_ref, t_ref, q_ref, gx_ref, gy_ref, diag_ref, p_ref):
     levels, x, width = t_ref.shape
     row = lax.broadcasted_iota(jnp.int32, (x, width), 0)
     lane = lax.broadcasted_iota(jnp.int32, (x, width), 1)
-    first_loss, last_loss = end_losses()
-
-    def lateral(i, carry):
-        pack_t, pack_k = carry
-        k = by_code(code_ref[i], k_table)
-        k_ref[i] = k
-        cap = by_code(code_ref[i], cap_table, cap_unit)
-        cap_ref[i] = cap
+
+    def level(i, carry):
+        k, t = k_ref[i], t_ref[i]
         gx = conductance(k, pltpu.roll(k, x - 1, 0), lat_unit)
         gx = jnp.where(row == x - 1, 0.0, gx)
         gx_ref[i] = gx
         gy = conductance(k, pltpu.roll(k, width - 1, 1), lat_unit)
         gy = jnp.where(lane == width - 1, 0.0, gy)
         gy_ref[i] = gy
-        t = t_ref[i]
-        fy = gy * (pltpu.roll(t, width - 1, 1) - t)
-        fx = gx * (pltpu.roll(t, x - 1, 0) - t)
-        p_ref[i] = cap * t + q_ref[i] + fx - pltpu.roll(fx, 1, 0) + fy - pltpu.roll(fy, 1, 1)
-        return (lane_edge_of(t, i, pack_t), lane_edge_of(k, i, pack_k))
+        diag = cap_by_k(k) - gx - pltpu.roll(gx, 1, 0) - gy - pltpu.roll(gy, 1, 1)
+        diag_ref[i] = diag
+        p_ref[i] = diag * t + q_ref[i] + from_beside(t, gx, 0) + from_beside(t, gy, 1)
+        return carry
+
+    loop(levels, level, 0, unroll=U_FACTOR)
+
+
+def factor_main(code_ref, t_ref, pack_ref, k_ref, w_ref, r_ref, yr_ref, left_ref, g_ref):
+    levels, x, width = t_ref.shape
+    first_loss, last_loss = end_losses()
+
+    def tables(i, carry):
+        pack_t, pack_k = carry
+        k = by_code(code_ref[i], k_table)
+        k_ref[i] = k
+        loss = jnp.where(i == 0, first_loss, 0.0) + jnp.where(i == levels - 1, last_loss, 0.0)
+        r_ref[i] = by_code(code_ref[i], cap_table, cap_unit) + loss
+        return (lane_edge_of(t_ref[i], i, pack_t), lane_edge_of(k, i, pack_k))
 
     tile = jnp.zeros((x, LANES), F32)
-    pack_ref[0], pack_ref[1] = loop(levels, lateral, (tile, tile), unroll=8)
+    pack_ref[0], pack_ref[1] = loop(levels, tables, (tile, tile))
     zero = jnp.zeros((x, width), F32)
 
     def forward(i, carry):
         ws, y, k_here = carry
         k_next = k_ref[jnp.minimum(i + 1, levels - 1)]
-        loss = jnp.where(i == 0, first_loss, 0.0) + jnp.where(i == levels - 1, last_loss, 0.0)
-        s = cap_ref[i] + loss + ws
+        s = r_ref[i] + ws
         u = jnp.where(i == levels - 1, 0.0, conductance(k_here, k_next))
         r = rcp(s + u)
         w = u * r
@@ -244,56 +268,51 @@
         return (lane_edge_of(halos[0], i, pack_t), lane_edge_of(halos[1], i, pack_k))
 
     zero = jnp.zeros((SUB, LANES), F32)
-    pack_ref[0], pack_ref[1] = loop(levels, level, (zero, zero))
-
-
-def first_side(p, t, k, w, r, left, th, kh, qh, gx_in, gx_ref, gxh, gyh, caph, wh, rh, yrh, lefth, z, zh, send, pack_ref):
+    pack_ref[0], pack_ref[1] = loop(levels, level, (zero, zero), unroll=64)
+
+
+def first_side(p, t, k, w, r, left, th, kh, qh, gxh, gyh, diagh, wh, rh, yrh, lefth, z, zh, send, pack_ref):
     levels, x, width = t.shape
     row = lax.broadcasted_iota(jnp.int32, (SUB, width), 0)
     lane = lax.broadcasted_iota(jnp.int32, (SUB, width), 1)
     first_loss, last_loss = end_losses()
 
     def forward(i, carry):
-        ws, yy, wy, k_here, wy_main, bf = carry
+        ws, yy, wy, here, wy_main, bf = carry
+        temp, t_main, k_main = th[i], t[i], k[i]
         k_next = kh[jnp.minimum(i + 1, levels - 1)]
-        cap = cap_by_k(k_here)
-        caph[i] = cap
+        cap = cap_by_k(here)
         loss = jnp.where(i == 0, first_loss, 0.0) + jnp.where(i == levels - 1, last_loss, 0.0)
         s = cap + loss + ws
-        u = jnp.where(i == levels - 1, 0.0, conductance(k_here, k_next))
+        u = jnp.where(i == levels - 1, 0.0, conductance(here, k_next))
         rr = rcp(s + u)
         ww = u * rr
-        wh[i] = ww
-        rh[i] = rr
-        yrh[i] = yy * rr
-
-        temp, t_main, k_main = th[i], t[i], k[i]
-        gx = conductance(k_here, jnp.where(row == SUB - 1, k_main[0:1], pltpu.roll(k_here, SUB - 1, 0)), lat_unit)
-        gxh[i] = gx
-        fx = gx * (jnp.where(row == SUB - 1, t_main[0:1], pltpu.roll(temp, SUB - 1, 0)) - temp)
-        g_top = conductance(k_main[x - SUB :], pltpu.roll(k_here, SUB - 1, 0), lat_unit)
-        gx_ref[i, x - 1 : x, :] = g_top[SUB - 1 :]
-        f_top = g_top * (pltpu.roll(temp, SUB - 1, 0) - t_main[x - SUB :])
-        gy = conductance(k_here, pltpu.roll(k_here, width - 1, 1), lat_unit)
+        wh[i], rh[i], yrh[i] = ww, rr, yy * rr
+
+        gx = conductance(here, jnp.where(row == SUB - 1, k_main[0:1], pltpu.roll(here, SUB - 1, 0)), lat_unit)
+        g_low = conductance(here, jnp.where(row == 0, k_main[x - 1 :], pltpu.roll(here, 1, 0)), lat_unit)
+        gy = conductance(here, pltpu.roll(here, width - 1, 1), lat_unit)
         gy = jnp.where(lane == width - 1, 0.0, gy)
-        gyh[i] = gy
-        fy = gy * (pltpu.roll(temp, width - 1, 1) - temp)
-        f_low = pltpu.roll(fx, 1, 0)
-        lateral = fx - jnp.where(row == 0, pltpu.roll(f_top, 1, 0), f_low) + fy - pltpu.roll(fy, 1, 1)
-        y = cap * temp + qh[i] + lateral + wy
+        gxh[i], gyh[i] = gx, gy
+        diag = cap - gx - g_low - gy - pltpu.roll(gy, 1, 1)
+        diagh[i] = diag
+        step_up = jnp.where(row == SUB - 1, t_main[0:1], pltpu.roll(temp, SUB - 1, 0))
+        step_low = jnp.where(row == 0, t_main[x - 1 :], pltpu.roll(temp, 1, 0))
+        y = diag * temp + qh[i] + gx * step_up + g_low * step_low + from_beside(temp, gy, 1) + wy
         zh[i] = y * rr
-
+        to_first = pltpu.roll(gx * (temp - step_up), 1, 0)
+        to_last = pltpu.roll(g_low * (temp - step_low), SUB - 1, 0)
         rhs = p[i]
         parts = [rhs[j : j + SUB] for j in range(0, x, SUB)]
-        parts[0] = parts[0] - jnp.where(row == 0, f_low, 0.0)
-        parts[-1] = parts[-1] + jnp.where(row == SUB - 1, f_top, 0.0)
+        parts[0] = parts[0] + jnp.where(row == 0, to_first, 0.0)
+        parts[-1] = parts[-1] + jnp.where(row == SUB - 1, to_last, 0.0)
         rhs = jnp.concatenate(parts, axis=0)
         y_main = rhs + wy_main
         z[i] = y_main * r[i]
         return (ww * s, yy * ww, ww * y, k_next, w[i] * y_main, bf + left[i] * rhs)
 
     zero, zero_main = jnp.zeros((SUB, width), F32), jnp.zeros((x, width), F32)
-    *_, bf = loop(levels, forward, (zero, zero + 1.0, zero, kh[0], zero_main, zero_main), unroll=8)
+    *_, bf = loop(levels, forward, (zero, zero + 1.0, zero, kh[0], zero_main, zero_main), unroll=U_SIDE)
 
     def backward(i, carry):
         ll, right, value, pack_l, pack_r = carry
@@ -304,7 +323,7 @@
         return (ll, right, zh[i] + ww * value, lane_edge_of(ll, i, pack_l), lane_edge_of(right, i, pack_r))
 
     tile = jnp.zeros((SUB, LANES), F32)
-    ll, _, bfh, pack_ref[0], pack_ref[1] = loop(levels, backward, (zero, zero, zero, tile, tile), reverse=True)
+    ll, _, bfh, pack_ref[0], pack_ref[1] = loop(levels, backward, (zero, zero, zero, tile, tile), unroll=U_BACK, reverse=True)
     for j in range(0, x, SUB):
         send[j // SUB] = bf[j : j + SUB]
         send[(x + j) // SUB] = z[levels - 1, j : j + SUB, :]
@@ -318,8 +337,22 @@
     return jnp.concatenate([main_ref[i], halo_ref[i]], axis=0)
 
 
+def join_rows(gxh, k, kh, gx_in, diag_in, gx_ref, diag_ref):
+    levels, x, _ = k.shape
+
+    def level(i, carry):
+        g_first = gxh[i, SUB - 1 : SUB, :]
+        g_last = conductance(k[i, x - 1 : x, :], kh[i, 0:1, :], lat_unit)
+        gx_ref[i, x - 1 : x, :] = g_last
+        diag_ref[i, 0:1, :] = diag_in[i, 0:1, :] - g_first
+        diag_ref[i, x - 1 : x, :] = diag_in[i, x - 1 : x, :] - g_last
+        return carry
+
+    loop(levels, level, 0, unroll=64)
+
+
 def right_side(last, *refs):
-    t, th, q, qh, cap, caph, gx, gxh, gy, gyh, w, wh, r, rh, left, lefth, *out = refs
+    t, th, q, qh, diag, diagh, gx, gxh, gy, gyh, w, wh, r, rh, left, lefth, *out = refs
     levels, x, width = t.shape
     z, send = out[0], out[-1]
     rows = x if last else x + SUB
@@ -331,10 +364,8 @@
         wy, bf = carry
         temp = both(t, th, i)
         here = temp[:rows]
-        fy = pick(gy, gyh, i) * (pltpu.roll(here, width - 1, 1) - here)
-        fx = both(gx, gxh, i) * (pltpu.roll(temp, x + SUB - 1, 0) - temp)
-        lateral = (fx - pltpu.roll(fx, 1, 0))[:rows] + fy - pltpu.roll(fy, 1, 1)
-        rhs = pick(cap, caph, i) * here + pick(q, qh, i) + lateral
+        rhs = pick(diag, diagh, i) * here + pick(q, qh, i) + from_beside(temp, both(gx, gxh, i), 0)[:rows]
+        rhs = rhs + from_beside(here, pick(gy, gyh, i), 1)
         y = rhs + wy
         zz = y * pick(r, rh, i)
         z[i] = zz[:x]
@@ -343,7 +374,7 @@
         return (pick(w, wh, i) * y, bf + pick(left, lefth, i) * rhs)
 
     zero = jnp.zeros((rows, width), F32)
-    _, bf = loop(levels, level, (zero, zero), unroll=16 if last else 8)
+    _, bf = loop(levels, level, (zero, zero), unroll=U_LAST if last else U_RIGHT)
     parts = [bf, pick(z, None if last else out[1], levels - 1)]
     groups = [part[j : j + SUB] for part in parts for j in range(0, x, SUB)]
     if not last:
@@ -394,7 +425,7 @@
             z[1][i, :, tile] = value[x:]
         return pick(w, i) * y
 
-    loop(levels, level, jnp.zeros(flow.shape, F32))
+    loop(levels, level, jnp.zeros(flow.shape, F32), unroll=64)
 
 
 def packed(a, b):
@@ -490,7 +521,7 @@
         return (both(w, wh, jnp.maximum(i - 1, 0)) * value, pack)
 
     init = (bottom * both(r, rh, levels - 1), jnp.zeros((rows, LANES), F32))
-    _, pack_ref[...] = loop(levels, level, init, reverse=True)
+    _, pack_ref[...] = loop(levels, level, init, unroll=U_SOLVE, reverse=True)
 
 
 def prepare_creep(code_ref, flag_ref, mod, exp, rate):
@@ -539,7 +570,7 @@
         _, out[0][i], out[1][i] = creep_cells(*[ref[i] for ref in main])
         return carry
 
-    loop(main[0].shape[0], level, 0, unroll=8)
+    loop(main[0].shape[0], level, 0, unroll=U_CREEP)
     for j, (_, creep, hard, _) in enumerate(creep_beside(main[0], flow, k, za, zb, state)):
         out[2][j] = creep
         out[2][2 + j] = hard
@@ -566,7 +597,7 @@
         return (w[jnp.maximum(i - 1, 0)] * value, pack)
 
     init = (bottom * r[levels - 1], jnp.zeros((x, LANES), F32))
-    _, pack_ref[...] = loop(levels, level, init, unroll=8, reverse=True)
+    _, pack_ref[...] = loop(levels, level, init, unroll=U_FINAL, reverse=True)
     place = lax.axis_index("stack")
     for j, (elastic, new, _, m) in enumerate(creep_beside(t, (top, bottom), k, za, zb, state)):
         zs[j] = jnp.where(place == (0, count - 1)[j], 0.0, m * (elastic - new))
@@ -647,44 +678,47 @@
         [edge] * 2,
         "edge_rows",
         cells,
-        [pltpu.VMEM(edge, F32), pltpu.VMEM(edge, jnp.int32), pltpu.VMEM(edge, F32), dma((3, 6))],
+        [
+            pltpu.VMEM((2, *edge), F32),
+            pltpu.VMEM((2, levels, width), F32),
+            pltpu.VMEM((2, 3, levels, width), jnp.int32),
+            dma((2, 8)),
+            dma((2,)),
+        ],
         in_hbm=3,
+        out_hbm=2,
         vmem=60,
     )
     rows_a = lax.ppermute(rows_a, "plane", plane_swaps[0])
     rows_b = lax.ppermute(rows_b, "plane", plane_swaps[1])
-    gx, gy, part, pack, k, cap, w, r, yr, left, g = call(
-        factor_main,
-        (code, temp, source),
-        [main] * 3 + [(4, x, LANES)] + [main] * 6 + [(3, x, width)],
-        "factor_main",
-        60 * cells,
+    pack, k, w, r, yr, left, g = call(
+        factor_main, (code, temp), [(4, x, LANES)] + [main] * 5 + [(3, x, width)], "factor_main", 30 * cells
     )
-    za, zb = call(edge_layers, (code, flag, distortion, creep, hard, g), [(8, x, width)] * 2, "edge_layers", cells)
+    gx, gy, diag, part = call(lateral_main, (k, temp, source), [main] * 4, "lateral_main", 40 * cells)
+    za, zb = call(edge_layers, (code, flag, distortion, creep, hard, g), [(8, x, width)] * 2, "edge_layers", cells, after=(part,))
     za, g_two, zb = lax.ppermute(za, "stack", peers[0]), lax.ppermute(g, "stack", peers[1]), lax.ppermute(zb, "stack", peers[2])
     g_sets = [g, za, g_two, zb]
     other_pack = lax.ppermute(pack[:2], "phys", swap)
 
     kh, th, qh, packh = call(
-        assemble_halo, (rows_a, rows_b), [halo] * 3 + [(2, SUB, LANES)], "assemble_halo", cells
+        assemble_halo, (rows_a, rows_b), [halo] * 3 + [(2, SUB, LANES)], "assemble_halo", cells, after=(part,)
     )
     other_packh = lax.ppermute(packh, "phys", swap)
     rows = x + SUB
     groups = 2 * x // SUB
-    gx, gxh, gyh, caph, wh, rh, yrh, lefth, z, zh, send, packh_lr = call(
+    gxh, gyh, diagh, wh, rh, yrh, lefth, z, zh, send, packh_lr = call(
         first_side,
-        (part, temp, k, w, r, left, th, kh, qh, gx),
-        [main] + [halo] * 7 + [main, halo, (groups + 3, SUB, width), (2, SUB, LANES)],
+        (part, temp, k, w, r, left, th, kh, qh),
+        [halo] * 7 + [main, halo, (groups + 3, SUB, width), (2, SUB, LANES)],
         "first_side",
         40 * cells,
-        aliases={9: 0},
     )
 
     own = other = state = None
     for step in range(TSTEPS):
         first, last = step == 0, step == TSTEPS - 1
         if not first:
-            ins = (temp, th, source, qh, cap, caph, gx, gxh, gy, gyh, w, wh, r, rh, left, lefth)
+            ins = (temp, th, source, qh, diag, diagh, gx, gxh, gy, gyh, w, wh, r, rh, left, lefth)
             send = (groups if last else groups + 1, SUB, width)
             z, *zh, send = call(
                 functools.partial(right_side, last), ins, [main, send] if last else [main, halo, send], "right_side", 30 * cells
@@ -707,6 +741,7 @@
         if first:
             h_sets = b_sets
             mod, exp, rate = call(prepare_creep, (code, flag), [main] * 3, "prepare_creep", 10 * cells, after=(z,))
+            gx, diag = call(join_rows, (gxh, k, kh, gx, diag), [main] * 2, "join_rows", cells, aliases={3: 0, 4: 1}, after=(rate,))
         else:
             creep, hard, state = call(
                 functools.partial(creep_step, step == 1),
@@ -723,7 +758,7 @@
             [main, halo, (rows, LANES), layers],
             "column_solve",
             10 * cells,
-            after=(rate,) if first else (creep,),
+            after=(rate, diag) if first else (creep,),
         )
         other = lax.ppermute(own, "phys", swap)
 

time: 56.4 us -> 53.9 us (0.956)
  Pallas kernels: 25.7 us -> 23.4 us
  local copies, waits for them, and re-layouts: 1.25 us -> 0.04 us
  waiting for transfers between devices: 3.71 us -> 4.83 us
    pallas_call x21 -> x23, Pallas kernels: 25.7 us -> 23.4 us  [call(): pl.pallas_call(kernel if after else body, in_specs=[HBM] * in_hbm + [VMEM...]
    unnamed x16 -> x14, local copies, waits for them, and re-layouts: 1.25 us -> 0.04 us
    ppermute x9, waiting for transfers between devices: 3.68 us -> 4.26 us  [per_device(): b_sets = [send] + [lax.ppermute(send, 'stack', peer) for peer in peers]]
  transfers between devices with their start and end apart: 21 -> 21, of which waited for: 5 -> 9; matrix products, arithmetic and copies ran while one was open for 0% -> 0% of each run, Pallas kernels for 32% -> 32%
where the time goes in v3:
time: 53.9 us; the launch traced here: 52.9 us
  starting transfers between devices  23.7 us (44%)
  Pallas kernels  23.4 us (43%)
  waiting for transfers between devices  4.83 us (9%)
  between operations  0.96 us (2%)
    pallas_call x23, Pallas kernels, call(): pl.pallas_call(kernel if after else body, in_specs=[HBM] * in_hbm + [VMEM...  23.4 us
    ppermute x9, starting transfers between devices, per_device(): b_sets = [send] + [lax.ppermute(send, 'stack', peer) for peer in peers]  10.5 us
    ppermute x1, starting transfers between devices, per_device(): xa = lax.ppermute(xa, 'plane', plane_swaps[0])  4.31 us
    ppermute x9, waiting for transfers between devices, per_device(): b_sets = [send] + [lax.ppermute(send, 'stack', peer) for peer in peers]  4.26 us
    ppermute x1, starting transfers between devices, per_device(): rows_a = lax.ppermute(rows_a, 'plane', plane_swaps[0])  3.09 us
    ppermute x1, starting transfers between devices, per_device(): lax.ppermute(za, 'stack', peers[0])  1.56 us
    ppermute x1, starting transfers between devices, per_device(): lax.ppermute(zb, 'stack', peers[2])  1.49 us
  transfers between devices with their start and end apart: 21, of which 9 were waited for; matrix products, arithmetic and copies ran while one was open for 0% of the time, Pallas kernels for 32%

profile of v3, /device:TPU:0, one launch (start us, length us, event | category | flops | bytes accessed | tf_op | source)
XLA Modules:
  0.0 52.9 jit_solution(1030289673400692845)
XLA Ops:
  0.7 2.5 %edge_rows.1 = (f32[6,64,256]{2,1,0:T(8,128)}, f32[6,64,256]{2,1,0:T(8,128)}) custom-call(f32[64,16,256]{2,1,0:T(8,128)} %t.1, s32[64,16,256]{2,1,0:T(8,128)} %refs_0_.3, f32[64,16,256]{2,1,0:T(8,128)} %refs_2_.5), custom_call_target="tpu_custom_call" | custom-call | flops 262144 | bytes 3932160 | tf_op jit(solution)/shard_map/edge_rows/pallas_call | solution.py:78
  3.2 3.1 %collective-permute-start.3 = (f32[6,64,256]{2,1,0:T(8,128)}, f32[6,64,256]{2,1,0:T(8,128)S(1)}, u32[]{:S(2)}, u32[]{:S(2)}) collective-permute-start(f32[6,64,256]{2,1,0:T(8,128)} %get-tuple-element.88), channel_id=1, source_target_pairs={{0,2},{4,6},{2,0},{6,4},{1,3},{5,7},{3,1},{7,5},{8,10},{12,14},{10... | collective-permute-start | bytes 1179656 | tf_op jit(solution)/shard_map/ppermute | solution.py:692
  6.3 0.8 %collective-permute-start.4 = (f32[6,64,256]{2,1,0:T(8,128)}, f32[6,64,256]{2,1,0:T(8,128)S(1)}, u32[]{:S(2)}, u32[]{:S(2)}) collective-permute-start(f32[6,64,256]{2,1,0:T(8,128)} %get-tuple-element.89), channel_id=1, source_target_pairs={{2,4},{4,2},{3,5},{5,3},{10,12},{12,10},{11,13},{13,11},{18,20},{2... | collective-permute-start | bytes 1179656 | tf_op jit(solution)/shard_map/ppermute | solution.py:693
  7.1 2.2 %factor_main.1 = (f32[4,16,128]{2,1,0:T(8,128)S(1)}, f32[64,16,256]{2,1,0:T(8,128)S(1)}, f32[64,16,256]{2,1,0:T(8,128)S(1)}, f32[64,16,256]{2,1,0:T(8,128)S(1)},...) custom-call(s32[64,16,256]{2,1,0:T(8,128)S(1)} %copy-done.3, ...), custom_call_target="tpu_custom_call" | custom-call | flops 7864320 | bytes 7421952 | tf_op jit(solution)/shard_map/factor_main/pallas_call | solution.py:78
  9.3 2.2 %lateral_main.1 = (f32[64,16,256]{2,1,0:T(8,128)S(1)}, f32[64,16,256]{2,1,0:T(8,128)S(1)}, f32[64,16,256]{2,1,0:T(8,128)S(1)}, f32[64,16,256]{2,1,0:T(8,128)S(1)}) custom-call(f32[64,16,256]{2,1,0:T(8,128)S(1)} %get-tuple-element.81.k_ref.k.refs_1_.refs_8_.refs_12_, f32[64,16,256]{2,1,0:T(8,128)S(1)} %copy-done.1, f32[64,16,256]{2,1,0:T(8,128)S(1)} %copy-done), custom_call_target="tpu_custom_call" | custom-call | flops 10485760 | bytes 7340032 | tf_op jit(solution)/shard_map/lateral_main/pallas_call | solution.py:78
  11.6 1.6 %collective-permute-start = (f32[8,16,256]{2,1,0:T(8,128)S(1)}, f32[8,16,256]{2,1,0:T(8,128)S(1)}, u32[]{:S(2)}, u32[]{:S(2)}) collective-permute-start(f32[8,16,256]{2,1,0:T(8,128)S(1)} %get-tuple-element.83), channel_id=1, source_target_pairs={{0,8},{8,0},{16,24},{24,16},{1,9},{9,1},{17,25},{25,17},{2,10},{10... | collective-permute-start | bytes 393224 | tf_op jit(solution)/shard_map/ppermute | solution.py:699
  13.1 1.5 %collective-permute-start.2 = (f32[8,16,256]{2,1,0:T(8,128)S(1)}, f32[8,16,256]{2,1,0:T(8,128)S(1)}, u32[]{:S(2)}, u32[]{:S(2)}) collective-permute-start(f32[8,16,256]{2,1,0:T(8,128)S(1)} %get-tuple-element.84), channel_id=1, source_target_pairs={{0,24},{8,16},{16,8},{24,0},{1,25},{9,17},{17,9},{25,1},{2,26},{10... | collective-permute-start | bytes 393224 | tf_op jit(solution)/shard_map/ppermute | solution.py:699
  16.6 2.1 %first_side.1 = (f32[64,8,256]{2,1,0:T(8,128)S(1)}, f32[64,8,256]{2,1,0:T(8,128)S(1)}, f32[64,8,256]{2,1,0:T(8,128)S(1)}, f32[64,8,256]{2,1,0:T(8,128)S(1)}, f32...) custom-call(f32[64,16,256]{2,1,0:T(8,128)S(1)} %get-tuple-element.82, ...), custom_call_target="tpu_custom_call" | custom-call | flops 10485760 | bytes 13172736 | tf_op jit(solution)/shard_map/first_side/pallas_call | solution.py:78
  18.7 2.6 %collective-permute-start.9 = (f32[7,8,256]{2,1,0:T(8,128)S(1)}, f32[7,8,256]{2,1,0:T(8,128)S(1)}, u32[]{:S(2)}, u32[]{:S(2)}) collective-permute-start(f32[7,8,256]{2,1,0:T(8,128)S(1)} %get-tuple-element.97.refs_4_), channel_id=1, source_target_pairs={{0,24},{8,16},{16,8},{24,0},{1,25},{9,17},{17,9},{25,1},{2,26},{10... | collective-permute-start | bytes 172040 | tf_op jit(solution)/shard_map/ppermute | solution.py:735
  22.7 0.6 %prepare_creep.1 = (f32[64,16,256]{2,1,0:T(8,128)S(1)}, f32[64,16,256]{2,1,0:T(8,128)S(1)}, f32[64,16,256]{2,1,0:T(8,128)S(1)}) custom-call(s32[64,16,256]{2,1,0:T(8,128)S(1)} %copy-done.3, s32[64,16,256]{2,1,0:T(8,128)S(1)} %copy-done.4, f32[64,16,256]{2,1,0:T(8,128)S(1)} %get-tuple-element.103.refs_2_.refs_8_), custom_call_target="tpu_custom_call" | custom-call | flops 2621440 | bytes 5242880 | tf_op jit(solution)/shard_map/prepare_creep/pallas_call | solution.py:78
  23.9 1.7 %collective-permute-done.8.refs_6_ = f32[7,8,256]{2,1,0:T(8,128)S(1)} collective-permute-done((f32[7,8,256]{2,1,0:T(8,128)S(1)}, f32[7,8,256]{2,1,0:T(8,128)S(1)}, u32[]{:S(2)}, u32[]{:S(2)}) %collective-permute-start.8) | collective-permute-done | bytes 57376 | tf_op jit(solution)/shard_map/ppermute | solution.py:735
  26.6 1.7 %right_side.2 = (f32[64,16,256]{2,1,0:T(8,128)S(1)}, f32[64,8,256]{2,1,0:T(8,128)S(1)}, f32[5,8,256]{2,1,0:T(8,128)S(1)}) custom-call(f32[64,16,256]{2,1,0:T(8,128)S(1)} %get-tuple-element.112.refs_0_, f32[64,8,256]{2,1,0:T(8,128)S(1)} %get-tuple-element.113.refs_1_, f32[64,16,256]{2,1,0:T(8,128)S(1)} %copy-done, ...), custom_call_target="tpu_custom_call" | custom-call | flops 7864320 | bytes 14196736 | tf_op jit(solution)/shard_map/right_side/pallas_call | solution.py:78
  28.4 1.5 %collective-permute-start.13 = (f32[5,8,256]{2,1,0:T(8,128)S(1)}, f32[5,8,256]{2,1,0:T(8,128)S(1)}, u32[]{:S(2)}, u32[]{:S(2)}) collective-permute-start(f32[5,8,256]{2,1,0:T(8,128)S(1)} %get-tuple-element.121.refs_8_), channel_id=1, source_target_pairs={{0,24},{8,16},{16,8},{24,0},{1,25},{9,17},{17,9},{25,1},{2,26},{10... | collective-permute-start | bytes 122888 | tf_op jit(solution)/shard_map/ppermute | solution.py:735
  30.3 1.6 %collective-permute-start.11 = (f32[5,8,256]{2,1,0:T(8,128)S(1)}, f32[5,8,256]{2,1,0:T(8,128)S(1)}, u32[]{:S(2)}, u32[]{:S(2)}) collective-permute-start(f32[5,8,256]{2,1,0:T(8,128)S(1)} %get-tuple-element.121.refs_8_), channel_id=1, source_target_pairs={{0,8},{8,0},{16,24},{24,16},{1,9},{9,1},{17,25},{25,17},{2,10},{10... | collective-permute-start | bytes 122888 | tf_op jit(solution)/shard_map/ppermute | solution.py:735
  31.9 1.6 %creep_step.2 = (f32[64,16,256]{2,1,0:T(8,128)S(1)}, f32[64,16,256]{2,1,0:T(8,128)S(1)}, f32[4,16,256]{2,1,0:T(8,128)S(1)}) custom-call(f32[64,16,256]{2,1,0:T(8,128)S(1)} %get-tuple-element.112.refs_0_, f32[64,16,256]{2,1,0:T(8,128)S(1)} %get-tuple-element.127.refs_1_.refs_16_, f32[64,16,256]{2,1,0:T(8,128)S(1)} %get-tuple-element.128.refs_2_.refs_17_, ...), custom_call_target="tpu_custom_call" | custom-call | flops 15728640 | bytes 10846208 | tf_op jit(solution)/shard_map/creep_step/pallas_call | solution.py:78
  34.8 1.1 %right_side.3 = (f32[64,16,256]{2,1,0:T(8,128)S(1)}, f32[4,8,256]{2,1,0:T(8,128)S(1)}) custom-call(f32[64,16,256]{2,1,0:T(8,128)S(1)} %get-tuple-element.131.refs_0_, f32[64,8,256]{2,1,0:T(8,128)S(1)} %get-tuple-element.132.refs_1_, f32[64,16,256]{2,1,0:T(8,128)S(1)} %copy-done, f32[64,8,256]{2,1,0:T(8,128)S(1)} %get-tuple-element.92.qh.refs_3_, ...), custom_call_target="tpu_custom_call" | custom-call | flops 7864320 | bytes 13664256 | tf_op jit(solution)/shard_map/right_side/pallas_call | solution.py:78
  36.1 2.6 %collective-permute-start.17 = (f32[4,8,256]{2,1,0:T(8,128)S(1)}, f32[4,8,256]{2,1,0:T(8,128)S(1)}, u32[]{:S(2)}, u32[]{:S(2)}) collective-permute-start(f32[4,8,256]{2,1,0:T(8,128)S(1)} %get-tuple-element.135.refs_4_), channel_id=1, source_target_pairs={{0,24},{8,16},{16,8},{24,0},{1,25},{9,17},{17,9},{25,1},{2,26},{10... | collective-permute-start | bytes 98312 | tf_op jit(solution)/shard_map/ppermute | solution.py:735
  39.5 1.6 %creep_step.3 = (f32[64,16,256]{2,1,0:T(8,128)S(1)}, f32[64,16,256]{2,1,0:T(8,128)S(1)}, f32[4,16,256]{2,1,0:T(8,128)S(1)}) custom-call(f32[64,16,256]{2,1,0:T(8,128)S(1)} %get-tuple-element.131.refs_0_, f32[64,16,256]{2,1,0:T(8,128)S(1)} %get-tuple-element.127.refs_1_.refs_16_, f32[64,16,256]{2,1,0:T(8,128)S(1)} %get-tuple-element.128.refs_2_.refs_17_, ...), custom_call_target="tpu_custom_call" | custom-call | flops 15728640 | bytes 10911744 | tf_op jit(solution)/shard_map/creep_step/pallas_call | solution.py:78
  41.5 1.1 %collective-permute-done.16.refs_6_ = f32[4,8,256]{2,1,0:T(8,128)S(1)} collective-permute-done((f32[4,8,256]{2,1,0:T(8,128)S(1)}, f32[4,8,256]{2,1,0:T(8,128)S(1)}, u32[]{:S(2)}, u32[]{:S(2)}) %collective-permute-start.16) | collective-permute-done | bytes 32800 | tf_op jit(solution)/shard_map/ppermute | solution.py:735
  43.1 1.9 %solve_and_creep.1 = (f32[64,16,256]{2,1,0:T(8,128)S(1)}, f32[64,16,256]{2,1,0:T(8,128)S(1)}, f32[64,16,256]{2,1,0:T(8,128)S(1)}, f32[64,16,256]{2,1,0:T(8,128)S...) custom-call(f32[3,16,256]{2,1,0:T(8,128)S(1)} %get-tuple-element.80.refs, ...), custom_call_target="tpu_custom_call" | custom-call | flops 18350080 | bytes 16719872 | tf_op jit(solution)/shard_map/solve_and_creep/pallas_call | solution.py:78
  45.0 4.3 %collective-permute-start.18 = (f32[64,256]{1,0:T(8,128)S(1)}, f32[64,256]{1,0:T(8,128)S(1)}, u32[]{:S(2)}, u32[]{:S(2)}) collective-permute-start(f32[64,256]{1,0:T(8,128)S(1)} %get-tuple-element.153), channel_id=1, source_target_pairs={{0,2},{4,6},{2,0},{6,4},{1,3},{5,7},{3,1},{7,5},{8,10},{12,14},{10... | collective-permute-start | bytes 196616 | tf_op jit(solution)/shard_map/ppermute | solution.py:772
  49.3 0.7 %collective-permute-start.19 = (f32[64,256]{1,0:T(8,128)S(1)}, f32[64,256]{1,0:T(8,128)S(1)}, u32[]{:S(2)}, u32[]{:S(2)}) collective-permute-start(f32[64,256]{1,0:T(8,128)S(1)} %get-tuple-element.154), channel_id=1, source_target_pairs={{2,4},{4,2},{3,5},{5,3},{10,12},{12,10},{11,13},{13,11},{18,20},{2... | collective-permute-start | bytes 196616 | tf_op jit(solution)/shard_map/ppermute | solution.py:773
  50.0 1.7 %balance_inside.1 = (f32[64,16,256]{2,1,0:T(8,128)}, f32[64,16,256]{2,1,0:T(8,128)}, f32[64,16,256]{2,1,0:T(8,128)}, f32[64,16,256]{2,1,0:T(8,128)S(1)}) custom-call(f32[64,16,256]{2,1,0:T(8,128)S(1)} %get-tuple-element.144.s, f32[2,16,256]{2,1,0:T(8,128)S(1)} %get-tuple-element.145.zs, f32[64,16,256]{2,1,0:T(8,128)S(1)} %get-tuple-element.146.t, ...), custom_call_target="tpu_custom_call" | custom-call | flops 5242880 | bytes 8421376 | tf_op jit(solution)/shard_map/balance_inside/pallas_call | solution.py:78
  51.8 1.1 %balance_edges.1 = f32[64,16,256]{2,1,0:T(8,128)} custom-call(f32[64,16,256]{2,1,0:T(8,128)S(1)} %get-tuple-element.152.inside, f32[64,256]{1,0:T(8,128)S(1)} %collective-permute-done.18.xa, f32[64,256]{1,0:T(8,128)S(1)} %collective-permute-done.19.xb, f32[16,128]{1,0:T(8,128)S(1)} %collective-permute-done.20.other), custom_call_target="tpu_custom_call" | custom-call | flops 2621440 | bytes 2236416 | tf_op jit(solution)/shard_map/balance_edges/pallas_call | solution.py:78
  (56 shorter events, 8.8 us)
Async XLA Ops:
  0.6 6.4 %copy-start.3 = (s32[64,16,256]{2,1,0:T(8,128)S(1)}, s32[64,16,256]{2,1,0:T(8,128)}, u32[]{:S(2)}) copy-start(s32[64,16,256]{2,1,0:T(8,128)} %refs_0_.3) | copy-start | bytes 3145732
  0.6 6.4 %copy-start.1 = (f32[64,16,256]{2,1,0:T(8,128)S(1)}, f32[64,16,256]{2,1,0:T(8,128)}, u32[]{:S(2)}) copy-start(f32[64,16,256]{2,1,0:T(8,128)} %t.1) | copy-start | bytes 3145732
  3.2 12.4 %collective-permute-start.3 = (f32[6,64,256]{2,1,0:T(8,128)}, f32[6,64,256]{2,1,0:T(8,128)S(1)}, u32[]{:S(2)}, u32[]{:S(2)}) collective-permute-start(f32[6,64,256]{2,1,0:T(8,128)} %get-tuple-element.88), channel_id=1, source_target_pairs={{0,2},{4,6},{2,0},{6,4},{1,3},{5,7},{3,1},{7,5},{8,10},{12,14},{10... | collective-permute-start | bytes 1179656 | tf_op jit(solution)/shard_map/ppermute | solution.py:692
  6.3 9.3 %collective-permute-start.4 = (f32[6,64,256]{2,1,0:T(8,128)}, f32[6,64,256]{2,1,0:T(8,128)S(1)}, u32[]{:S(2)}, u32[]{:S(2)}) collective-permute-start(f32[6,64,256]{2,1,0:T(8,128)} %get-tuple-element.89), channel_id=1, source_target_pairs={{2,4},{4,2},{3,5},{5,3},{10,12},{12,10},{11,13},{13,11},{18,20},{2... | collective-permute-start | bytes 1179656 | tf_op jit(solution)/shard_map/ppermute | solution.py:693
  7.1 4.4 %copy-start.6 = (f32[64,16,256]{2,1,0:T(8,128)S(1)}, f32[64,16,256]{2,1,0:T(8,128)}, u32[]{:S(2)}) copy-start(f32[64,16,256]{2,1,0:T(8,128)} %refs_6_.1) | copy-start | bytes 3145732
  11.6 12.1 %collective-permute-start = (f32[8,16,256]{2,1,0:T(8,128)S(1)}, f32[8,16,256]{2,1,0:T(8,128)S(1)}, u32[]{:S(2)}, u32[]{:S(2)}) collective-permute-start(f32[8,16,256]{2,1,0:T(8,128)S(1)} %get-tuple-element.83), channel_id=1, source_target_pairs={{0,8},{8,0},{16,24},{24,16},{1,9},{9,1},{17,25},{25,17},{2,10},{10... | collective-permute-start | bytes 393224 | tf_op jit(solution)/shard_map/ppermute | solution.py:699
  13.1 10.5 %collective-permute-start.2 = (f32[8,16,256]{2,1,0:T(8,128)S(1)}, f32[8,16,256]{2,1,0:T(8,128)S(1)}, u32[]{:S(2)}, u32[]{:S(2)}) collective-permute-start(f32[8,16,256]{2,1,0:T(8,128)S(1)} %get-tuple-element.84), channel_id=1, source_target_pairs={{0,24},{8,16},{16,8},{24,0},{1,25},{9,17},{17,9},{25,1},{2,26},{10... | collective-permute-start | bytes 393224 | tf_op jit(solution)/shard_map/ppermute | solution.py:699
  14.6 7.3 %collective-permute-start.1 = (f32[3,16,256]{2,1,0:T(8,128)S(1)}, f32[3,16,256]{2,1,0:T(8,128)S(1)}, u32[]{:S(2)}, u32[]{:S(2)}) collective-permute-start(f32[3,16,256]{2,1,0:T(8,128)S(1)} %get-tuple-element.80.refs_5_.refs_0_), channel_id=1, source_target_pairs={{0,16},{8,24},{16,0},{24,8},{1,17},{9,25},{17,1},{25,9},{2,18},{10... | collective-permute-start | bytes 147464 | tf_op jit(solution)/shard_map/ppermute | solution.py:699
  15.6 3.1 %collective-permute-start.5 = (f32[2,16,128]{2,1,0:T(8,128)S(1)}, f32[2,16,128]{2,1,0:T(8,128)S(1)}, u32[]{:S(2)}, u32[]{:S(2)}) collective-permute-start(f32[2,16,128]{2,1,0:T(8,128)S(1)} %slice.3), channel_id=1, source_target_pairs={{0,1},{1,0},{2,3},{3,2},{4,5},{5,4},{6,7},{7,6},{8,9},{9,8},{10,11... | collective-permute-start | bytes 49160 | tf_op jit(solution)/shard_map/ppermute | solution.py:701
  16.0 2.7 %collective-permute-start.6 = (f32[2,8,128]{2,1,0:T(8,128)S(1)}, f32[2,8,128]{2,1,0:T(8,128)S(1)}, u32[]{:S(2)}, u32[]{:S(2)}) collective-permute-start(f32[2,8,128]{2,1,0:T(8,128)S(1)} %get-tuple-element.95.refs_2_), channel_id=1, source_target_pairs={{0,1},{1,0},{2,3},{3,2},{4,5},{5,4},{6,7},{7,6},{8,9},{9,8},{10,11... | collective-permute-start | bytes 24584 | tf_op jit(solution)/shard_map/ppermute | solution.py:706
  18.7 5.1 %collective-permute-start.9 = (f32[7,8,256]{2,1,0:T(8,128)S(1)}, f32[7,8,256]{2,1,0:T(8,128)S(1)}, u32[]{:S(2)}, u32[]{:S(2)}) collective-permute-start(f32[7,8,256]{2,1,0:T(8,128)S(1)} %get-tuple-element.97.refs_4_), channel_id=1, source_target_pairs={{0,24},{8,16},{16,8},{24,0},{1,25},{9,17},{17,9},{25,1},{2,26},{10... | collective-permute-start | bytes 172040 | tf_op jit(solution)/shard_map/ppermute | solution.py:735
  21.4 4.2 %collective-permute-start.8 = (f32[7,8,256]{2,1,0:T(8,128)S(1)}, f32[7,8,256]{2,1,0:T(8,128)S(1)}, u32[]{:S(2)}, u32[]{:S(2)}) collective-permute-start(f32[7,8,256]{2,1,0:T(8,128)S(1)} %get-tuple-element.97.refs_4_), channel_id=1, source_target_pairs={{0,16},{8,24},{16,0},{24,8},{1,17},{9,25},{17,1},{25,9},{2,18},{10... | collective-permute-start | bytes 172040 | tf_op jit(solution)/shard_map/ppermute | solution.py:735
  21.9 4.2 %collective-permute-start.7 = (f32[7,8,256]{2,1,0:T(8,128)S(1)}, f32[7,8,256]{2,1,0:T(8,128)S(1)}, u32[]{:S(2)}, u32[]{:S(2)}) collective-permute-start(f32[7,8,256]{2,1,0:T(8,128)S(1)} %get-tuple-element.97.refs_4_), channel_id=1, source_target_pairs={{0,8},{8,0},{16,24},{24,16},{1,9},{9,1},{17,25},{25,17},{2,10},{10... | collective-permute-start | bytes 172040 | tf_op jit(solution)/shard_map/ppermute | solution.py:735
  26.6 1.7 %collective-permute-start.10 = (f32[24,128]{1,0:T(8,128)S(1)}, f32[24,128]{1,0:T(8,128)S(1)}, u32[]{:S(2)}, u32[]{:S(2)}) collective-permute-start(f32[24,128]{1,0:T(8,128)S(1)} %get-tuple-element.120.refs_6_), channel_id=1, source_target_pairs={{0,1},{1,0},{2,3},{3,2},{4,5},{5,4},{6,7},{7,6},{8,9},{9,8},{10,11... | collective-permute-start | bytes 36872 | tf_op jit(solution)/shard_map/ppermute | solution.py:763
  28.4 5.6 %collective-permute-start.13 = (f32[5,8,256]{2,1,0:T(8,128)S(1)}, f32[5,8,256]{2,1,0:T(8,128)S(1)}, u32[]{:S(2)}, u32[]{:S(2)}) collective-permute-start(f32[5,8,256]{2,1,0:T(8,128)S(1)} %get-tuple-element.121.refs_8_), channel_id=1, source_target_pairs={{0,24},{8,16},{16,8},{24,0},{1,25},{9,17},{17,9},{25,1},{2,26},{10... | collective-permute-start | bytes 122888 | tf_op jit(solution)/shard_map/ppermute | solution.py:735
  29.9 4.2 %collective-permute-start.12 = (f32[5,8,256]{2,1,0:T(8,128)S(1)}, f32[5,8,256]{2,1,0:T(8,128)S(1)}, u32[]{:S(2)}, u32[]{:S(2)}) collective-permute-start(f32[5,8,256]{2,1,0:T(8,128)S(1)} %get-tuple-element.121.refs_8_), channel_id=1, source_target_pairs={{0,16},{8,24},{16,0},{24,8},{1,17},{9,25},{17,1},{25,9},{2,18},{10... | collective-permute-start | bytes 122888 | tf_op jit(solution)/shard_map/ppermute | solution.py:735
  30.3 4.0 %collective-permute-start.11 = (f32[5,8,256]{2,1,0:T(8,128)S(1)}, f32[5,8,256]{2,1,0:T(8,128)S(1)}, u32[]{:S(2)}, u32[]{:S(2)}) collective-permute-start(f32[5,8,256]{2,1,0:T(8,128)S(1)} %get-tuple-element.121.refs_8_), channel_id=1, source_target_pairs={{0,8},{8,0},{16,24},{24,16},{1,9},{9,1},{17,25},{25,17},{2,10},{10... | collective-permute-start | bytes 122888 | tf_op jit(solution)/shard_map/ppermute | solution.py:735
  34.7 1.2 %collective-permute-start.14 = (f32[24,128]{1,0:T(8,128)S(1)}, f32[24,128]{1,0:T(8,128)S(1)}, u32[]{:S(2)}, u32[]{:S(2)}) collective-permute-start(f32[24,128]{1,0:T(8,128)S(1)} %get-tuple-element.134.refs_6_), channel_id=1, source_target_pairs={{0,1},{1,0},{2,3},{3,2},{4,5},{5,4},{6,7},{7,6},{8,9},{9,8},{10,11... | collective-permute-start | bytes 36872 | tf_op jit(solution)/shard_map/ppermute | solution.py:763
  36.1 5.5 %collective-permute-start.17 = (f32[4,8,256]{2,1,0:T(8,128)S(1)}, f32[4,8,256]{2,1,0:T(8,128)S(1)}, u32[]{:S(2)}, u32[]{:S(2)}) collective-permute-start(f32[4,8,256]{2,1,0:T(8,128)S(1)} %get-tuple-element.135.refs_4_), channel_id=1, source_target_pairs={{0,24},{8,16},{16,8},{24,0},{1,25},{9,17},{17,9},{25,1},{2,26},{10... | collective-permute-start | bytes 98312 | tf_op jit(solution)/shard_map/ppermute | solution.py:735
  38.7 3.9 %collective-permute-start.16 = (f32[4,8,256]{2,1,0:T(8,128)S(1)}, f32[4,8,256]{2,1,0:T(8,128)S(1)}, u32[]{:S(2)}, u32[]{:S(2)}) collective-permute-start(f32[4,8,256]{2,1,0:T(8,128)S(1)} %get-tuple-element.135.refs_4_), channel_id=1, source_target_pairs={{0,16},{8,24},{16,0},{24,8},{1,17},{9,25},{17,1},{25,9},{2,18},{10... | collective-permute-start | bytes 98312 | tf_op jit(solution)/shard_map/ppermute | solution.py:735
  39.2 3.9 %collective-permute-start.15 = (f32[4,8,256]{2,1,0:T(8,128)S(1)}, f32[4,8,256]{2,1,0:T(8,128)S(1)}, u32[]{:S(2)}, u32[]{:S(2)}) collective-permute-start(f32[4,8,256]{2,1,0:T(8,128)S(1)} %get-tuple-element.135.refs_4_), channel_id=1, source_target_pairs={{0,8},{8,0},{16,24},{24,16},{1,9},{9,1},{17,25},{25,17},{2,10},{10... | collective-permute-start | bytes 98312 | tf_op jit(solution)/shard_map/ppermute | solution.py:735
  45.0 6.8 %collective-permute-start.18 = (f32[64,256]{1,0:T(8,128)S(1)}, f32[64,256]{1,0:T(8,128)S(1)}, u32[]{:S(2)}, u32[]{:S(2)}) collective-permute-start(f32[64,256]{1,0:T(8,128)S(1)} %get-tuple-element.153), channel_id=1, source_target_pairs={{0,2},{4,6},{2,0},{6,4},{1,3},{5,7},{3,1},{7,5},{8,10},{12,14},{10... | collective-permute-start | bytes 196616 | tf_op jit(solution)/shard_map/ppermute | solution.py:772
  49.3 2.5 %collective-permute-start.19 = (f32[64,256]{1,0:T(8,128)S(1)}, f32[64,256]{1,0:T(8,128)S(1)}, u32[]{:S(2)}, u32[]{:S(2)}) collective-permute-start(f32[64,256]{1,0:T(8,128)S(1)} %get-tuple-element.154), channel_id=1, source_target_pairs={{2,4},{4,2},{3,5},{5,3},{10,12},{12,10},{11,13},{13,11},{18,20},{2... | collective-permute-start | bytes 196616 | tf_op jit(solution)/shard_map/ppermute | solution.py:773
  50.0 1.8 %collective-permute-start.20 = (f32[16,128]{1,0:T(8,128)S(1)}, f32[16,128]{1,0:T(8,128)S(1)}, u32[]{:S(2)}, u32[]{:S(2)}) collective-permute-start(f32[16,128]{1,0:T(8,128)S(1)} %get-tuple-element.155), channel_id=1, source_target_pairs={{0,1},{1,0},{2,3},{3,2},{4,5},{5,4},{6,7},{7,6},{8,9},{9,8},{10,11... | collective-permute-start | bytes 24584 | tf_op jit(solution)/shard_map/ppermute | solution.py:774
  (4 other events, 9.7 us)

commit v4 on v3

--- a/solution.py
+++ b/solution.py
@@ -88,11 +88,19 @@
     )(*ins, *after)
 
 
-def pair_swaps(axis):
-    count = lax.axis_size(axis)
-    first = [(i, i + 1) for i in range(0, count - 1, 2)]
-    second = [(i, i + 1) for i in range(1, count - 1, 2)]
-    return [pairs + [(b, a) for a, b in pairs] for pairs in (first, second)]
+def plane_exchange(a, b):
+    count, cores = lax.axis_size("plane"), lax.axis_size("phys")
+    pairs = [(i, i + 1) for i in range(0, count - 1, 2)]
+    a = lax.ppermute(a, "plane", pairs + [(j, i) for i, j in pairs])
+    pairs = [(i * cores + f, (i + 1) * cores + f) for i in range(1, count - 1, 2) for f in range(cores)]
+    pairs += [(i * cores, i * cores + 1) for i in (0, count - 1)]
+    b = lax.ppermute(b, ("plane", "phys"), pairs + [(j, i) for i, j in pairs])
+    return a, b
+
+
+def has_b():
+    place, count = lax.axis_index("plane"), lax.axis_size("plane")
+    return (place > 0) & (place < count - 1)
 
 
 def even(axis):
@@ -253,7 +261,7 @@
     levels, _, width = kh_ref.shape
     row = lax.broadcasted_iota(jnp.int32, (SUB, width), 0)
     a_rows = [row == jnp.where(is_even, j, SUB - 1 - j) for j in (0, 1)]
-    b_rows = [row == jnp.where(is_even, SUB - 1 - j, j) for j in (0, 1)]
+    b_rows = [(row == jnp.where(is_even, SUB - 1 - j, j)) & has_b() for j in (0, 1)]
 
     def level(i, carry):
         pack_t, pack_k = carry
@@ -638,7 +646,7 @@
     is_even = even("plane")
     row = lax.broadcasted_iota(jnp.int32, (x, width), 0)
     a_row = row == jnp.where(is_even, x - 1, 0)
-    b_row = row == jnp.where(is_even, 0, x - 1)
+    b_row = (row == jnp.where(is_even, 0, x - 1)) & has_b()
     chunks = sem.shape[0]
     part = levels // chunks
     copies = []
@@ -662,12 +670,11 @@
 def per_device(temp, source, code, flag, distortion, creep, hard):
     levels, x, width = temp.shape
     count = lax.axis_size("stack")
-    if lax.axis_size("phys") != 2 or count != 4 or levels > LANES or x % SUB or width % LANES:
+    if lax.axis_size("phys") != 2 or count != 4 or lax.axis_size("plane") % 2 or levels > LANES or x % SUB or width % LANES:
         raise ValueError("unsupported sizes")
     main, halo, layers = (levels, x, width), (levels, SUB, width), (2, x, width)
     cells = levels * x * width
     swap = [(0, 1), (1, 0)]
-    plane_swaps = pair_swaps("plane")
     peers = [[(i, i ^ j) for i in range(count)] for j in range(1, count)]
     dma = pltpu.SemaphoreType.DMA
 
@@ -689,8 +696,7 @@
         out_hbm=2,
         vmem=60,
     )
-    rows_a = lax.ppermute(rows_a, "plane", plane_swaps[0])
-    rows_b = lax.ppermute(rows_b, "plane", plane_swaps[1])
+    rows_a, rows_b = plane_exchange(rows_a, rows_b)
     pack, k, w, r, yr, left, g = call(
         factor_main, (code, temp), [(4, x, LANES)] + [main] * 5 + [(3, x, width)], "factor_main", 30 * cells
     )
@@ -769,8 +775,7 @@
         "solve_and_creep",
         70 * cells,
     )
-    xa = lax.ppermute(xa, "plane", plane_swaps[0])
-    xb = lax.ppermute(xb, "plane", plane_swaps[1])
+    xa, xb = plane_exchange(xa, xb)
     other = lax.ppermute(pack, "phys", swap)
     temp, creep, hard, inside = call(
         balance_inside, (stress, zs, temp, creep, hard), [main] * 4, "balance_inside", 20 * cells, [dma((3,))], out_hbm=3

time: 53.9 us -> 50.8 us (0.942); the launches traced: 52.9 us -> 50.6 us
  starting transfers between devices: 23.7 us -> 20.7 us
  waiting for transfers between devices: 4.83 us -> 5.68 us
    ppermute x4, starting transfers between devices: 8.85 us -> 5.38 us  [the longest x2 5.37 us: plane_exchange(): a = lax.ppermute(a, 'plane', pairs + [(j, i) for i, j in pairs])]
    ppermute x4, waiting for transfers between devices: 0.44 us -> 1.29 us  [the longest x2 1.29 us: plane_exchange(): a = lax.ppermute(a, 'plane', pairs + [(j, i) for i, j in pairs])]
  transfers between devices with their start and end apart: 21 -> 21, of which waited for: 9 -> 9; matrix products, arithmetic and copies ran while one was open for 0% -> 0% of each run, Pallas kernels for 32% -> 33%
where the time goes in v4:
time: 50.8 us; the launch traced here: 50.6 us
  Pallas kernels  23.4 us (46%)
  starting transfers between devices  20.7 us (41%)
  waiting for transfers between devices  5.68 us (11%)
  between operations  0.91 us (2%)
    pallas_call x23, Pallas kernels, call(): pl.pallas_call(kernel if after else body, in_specs=[HBM] * in_hbm + [VMEM...  23.4 us
    ppermute x9, starting transfers between devices, per_device(): b_sets = [send] + [lax.ppermute(send, 'stack', peer) for peer in peers]  10.5 us
    ppermute x2, starting transfers between devices, plane_exchange(): a = lax.ppermute(a, 'plane', pairs + [(j, i) for i, j in pairs])  5.37 us
    ppermute x9, waiting for transfers between devices, per_device(): b_sets = [send] + [lax.ppermute(send, 'stack', peer) for peer in peers]  4.26 us
    ppermute x1, starting transfers between devices, per_device(): lax.ppermute(za, 'stack', peers[0])  1.56 us
    ppermute x1, starting transfers between devices, per_device(): lax.ppermute(zb, 'stack', peers[2])  1.49 us
    ppermute x2, waiting for transfers between devices, plane_exchange(): a = lax.ppermute(a, 'plane', pairs + [(j, i) for i, j in pairs])  1.29 us
  transfers between devices with their start and end apart: 21, of which 9 were waited for; matrix products, arithmetic and copies ran while one was open for 0% of the time, Pallas kernels for 33%

profile of v4, /device:TPU:0, one launch (start us, length us, event | category | flops | bytes accessed | tf_op | source)
XLA Modules:
  0.0 50.6 jit_solution(17135932585612621997)
XLA Ops:
  0.7 2.5 %edge_rows.1 = (f32[6,64,256]{2,1,0:T(8,128)}, f32[6,64,256]{2,1,0:T(8,128)}) custom-call(f32[64,16,256]{2,1,0:T(8,128)} %t.1, s32[64,16,256]{2,1,0:T(8,128)} %refs_0_.3, f32[64,16,256]{2,1,0:T(8,128)} %refs_2_.5), custom_call_target="tpu_custom_call" | custom-call | flops 262144 | bytes 3932160 | tf_op jit(solution)/shard_map/edge_rows/pallas_call | solution.py:78
  3.2 3.1 %collective-permute-start.3 = (f32[6,64,256]{2,1,0:T(8,128)}, f32[6,64,256]{2,1,0:T(8,128)S(1)}, u32[]{:S(2)}, u32[]{:S(2)}) collective-permute-start(f32[6,64,256]{2,1,0:T(8,128)} %get-tuple-element.88), channel_id=1, source_target_pairs={{0,2},{4,6},{2,0},{6,4},{1,3},{5,7},{3,1},{7,5},{8,10},{12,14},{10... | collective-permute-start | bytes 1179656 | tf_op jit(solution)/shard_map/ppermute | solution.py:94
  6.3 2.2 %factor_main.1 = (f32[4,16,128]{2,1,0:T(8,128)S(1)}, f32[64,16,256]{2,1,0:T(8,128)S(1)}, f32[64,16,256]{2,1,0:T(8,128)S(1)}, f32[64,16,256]{2,1,0:T(8,128)S(1)},...) custom-call(s32[64,16,256]{2,1,0:T(8,128)S(1)} %copy-done.3, ...), custom_call_target="tpu_custom_call" | custom-call | flops 7864320 | bytes 7421952 | tf_op jit(solution)/shard_map/factor_main/pallas_call | solution.py:78
  8.5 2.2 %lateral_main.1 = (f32[64,16,256]{2,1,0:T(8,128)S(1)}, f32[64,16,256]{2,1,0:T(8,128)S(1)}, f32[64,16,256]{2,1,0:T(8,128)S(1)}, f32[64,16,256]{2,1,0:T(8,128)S(1)}) custom-call(f32[64,16,256]{2,1,0:T(8,128)S(1)} %get-tuple-element.81.k_ref.k.refs_1_.refs_8_.refs_12_, f32[64,16,256]{2,1,0:T(8,128)S(1)} %copy-done.1, f32[64,16,256]{2,1,0:T(8,128)S(1)} %copy-done), custom_call_target="tpu_custom_call" | custom-call | flops 10485760 | bytes 7340032 | tf_op jit(solution)/shard_map/lateral_main/pallas_call | solution.py:78
  10.8 1.6 %collective-permute-start = (f32[8,16,256]{2,1,0:T(8,128)S(1)}, f32[8,16,256]{2,1,0:T(8,128)S(1)}, u32[]{:S(2)}, u32[]{:S(2)}) collective-permute-start(f32[8,16,256]{2,1,0:T(8,128)S(1)} %get-tuple-element.83), channel_id=1, source_target_pairs={{0,8},{8,0},{16,24},{24,16},{1,9},{9,1},{17,25},{25,17},{2,10},{10... | collective-permute-start | bytes 393224 | tf_op jit(solution)/shard_map/ppermute | solution.py:705
  12.3 1.5 %collective-permute-start.2 = (f32[8,16,256]{2,1,0:T(8,128)S(1)}, f32[8,16,256]{2,1,0:T(8,128)S(1)}, u32[]{:S(2)}, u32[]{:S(2)}) collective-permute-start(f32[8,16,256]{2,1,0:T(8,128)S(1)} %get-tuple-element.84), channel_id=1, source_target_pairs={{0,24},{8,16},{16,8},{24,0},{1,25},{9,17},{17,9},{25,1},{2,26},{10... | collective-permute-start | bytes 393224 | tf_op jit(solution)/shard_map/ppermute | solution.py:705
  14.3 1.3 %collective-permute-done.3.refs_0_ = f32[6,64,256]{2,1,0:T(8,128)S(1)} collective-permute-done((f32[6,64,256]{2,1,0:T(8,128)}, f32[6,64,256]{2,1,0:T(8,128)S(1)}, u32[]{:S(2)}, u32[]{:S(2)}) %collective-permute-start.3) | collective-permute-done | bytes 393248 | tf_op jit(solution)/shard_map/ppermute | solution.py:94
  16.0 0.6 %collective-permute-start.6 = (f32[2,8,128]{2,1,0:T(8,128)S(1)}, f32[2,8,128]{2,1,0:T(8,128)S(1)}, u32[]{:S(2)}, u32[]{:S(2)}) collective-permute-start(f32[2,8,128]{2,1,0:T(8,128)S(1)} %get-tuple-element.95.refs_2_), channel_id=1, source_target_pairs={{0,1},{1,0},{2,3},{3,2},{4,5},{5,4},{6,7},{7,6},{8,9},{9,8},{10,11... | collective-permute-start | bytes 24584 | tf_op jit(solution)/shard_map/ppermute | solution.py:712
  16.6 2.1 %first_side.1 = (f32[64,8,256]{2,1,0:T(8,128)S(1)}, f32[64,8,256]{2,1,0:T(8,128)S(1)}, f32[64,8,256]{2,1,0:T(8,128)S(1)}, f32[64,8,256]{2,1,0:T(8,128)S(1)}, f32...) custom-call(f32[64,16,256]{2,1,0:T(8,128)S(1)} %get-tuple-element.82, ...), custom_call_target="tpu_custom_call" | custom-call | flops 10485760 | bytes 13172736 | tf_op jit(solution)/shard_map/first_side/pallas_call | solution.py:78
  18.7 2.6 %collective-permute-start.9 = (f32[7,8,256]{2,1,0:T(8,128)S(1)}, f32[7,8,256]{2,1,0:T(8,128)S(1)}, u32[]{:S(2)}, u32[]{:S(2)}) collective-permute-start(f32[7,8,256]{2,1,0:T(8,128)S(1)} %get-tuple-element.97.refs_4_), channel_id=1, source_target_pairs={{0,24},{8,16},{16,8},{24,0},{1,25},{9,17},{17,9},{25,1},{2,26},{10... | collective-permute-start | bytes 172040 | tf_op jit(solution)/shard_map/ppermute | solution.py:741
  22.7 0.6 %prepare_creep.1 = (f32[64,16,256]{2,1,0:T(8,128)S(1)}, f32[64,16,256]{2,1,0:T(8,128)S(1)}, f32[64,16,256]{2,1,0:T(8,128)S(1)}) custom-call(s32[64,16,256]{2,1,0:T(8,128)S(1)} %copy-done.3, s32[64,16,256]{2,1,0:T(8,128)S(1)} %copy-done.4, f32[64,16,256]{2,1,0:T(8,128)S(1)} %get-tuple-element.103.refs_2_.refs_8_), custom_call_target="tpu_custom_call" | custom-call | flops 2621440 | bytes 5242880 | tf_op jit(solution)/shard_map/prepare_creep/pallas_call | solution.py:78
  23.9 1.7 %collective-permute-done.8.refs_6_ = f32[7,8,256]{2,1,0:T(8,128)S(1)} collective-permute-done((f32[7,8,256]{2,1,0:T(8,128)S(1)}, f32[7,8,256]{2,1,0:T(8,128)S(1)}, u32[]{:S(2)}, u32[]{:S(2)}) %collective-permute-start.8) | collective-permute-done | bytes 57376 | tf_op jit(solution)/shard_map/ppermute | solution.py:741
  26.6 1.7 %right_side.2 = (f32[64,16,256]{2,1,0:T(8,128)S(1)}, f32[64,8,256]{2,1,0:T(8,128)S(1)}, f32[5,8,256]{2,1,0:T(8,128)S(1)}) custom-call(f32[64,16,256]{2,1,0:T(8,128)S(1)} %get-tuple-element.112.refs_0_, f32[64,8,256]{2,1,0:T(8,128)S(1)} %get-tuple-element.113.refs_1_, f32[64,16,256]{2,1,0:T(8,128)S(1)} %copy-done, ...), custom_call_target="tpu_custom_call" | custom-call | flops 7864320 | bytes 14196736 | tf_op jit(solution)/shard_map/right_side/pallas_call | solution.py:78
  28.4 1.5 %collective-permute-start.13 = (f32[5,8,256]{2,1,0:T(8,128)S(1)}, f32[5,8,256]{2,1,0:T(8,128)S(1)}, u32[]{:S(2)}, u32[]{:S(2)}) collective-permute-start(f32[5,8,256]{2,1,0:T(8,128)S(1)} %get-tuple-element.121.refs_8_), channel_id=1, source_target_pairs={{0,24},{8,16},{16,8},{24,0},{1,25},{9,17},{17,9},{25,1},{2,26},{10... | collective-permute-start | bytes 122888 | tf_op jit(solution)/shard_map/ppermute | solution.py:741
  30.3 1.6 %collective-permute-start.11 = (f32[5,8,256]{2,1,0:T(8,128)S(1)}, f32[5,8,256]{2,1,0:T(8,128)S(1)}, u32[]{:S(2)}, u32[]{:S(2)}) collective-permute-start(f32[5,8,256]{2,1,0:T(8,128)S(1)} %get-tuple-element.121.refs_8_), channel_id=1, source_target_pairs={{0,8},{8,0},{16,24},{24,16},{1,9},{9,1},{17,25},{25,17},{2,10},{10... | collective-permute-start | bytes 122888 | tf_op jit(solution)/shard_map/ppermute | solution.py:741
  31.9 1.6 %creep_step.2 = (f32[64,16,256]{2,1,0:T(8,128)S(1)}, f32[64,16,256]{2,1,0:T(8,128)S(1)}, f32[4,16,256]{2,1,0:T(8,128)S(1)}) custom-call(f32[64,16,256]{2,1,0:T(8,128)S(1)} %get-tuple-element.112.refs_0_, f32[64,16,256]{2,1,0:T(8,128)S(1)} %get-tuple-element.127.refs_1_.refs_16_, f32[64,16,256]{2,1,0:T(8,128)S(1)} %get-tuple-element.128.refs_2_.refs_17_, ...), custom_call_target="tpu_custom_call" | custom-call | flops 15728640 | bytes 10846208 | tf_op jit(solution)/shard_map/creep_step/pallas_call | solution.py:78
  34.8 1.1 %right_side.3 = (f32[64,16,256]{2,1,0:T(8,128)S(1)}, f32[4,8,256]{2,1,0:T(8,128)S(1)}) custom-call(f32[64,16,256]{2,1,0:T(8,128)S(1)} %get-tuple-element.131.refs_0_, f32[64,8,256]{2,1,0:T(8,128)S(1)} %get-tuple-element.132.refs_1_, f32[64,16,256]{2,1,0:T(8,128)S(1)} %copy-done, f32[64,8,256]{2,1,0:T(8,128)S(1)} %get-tuple-element.92.qh.refs_3_, ...), custom_call_target="tpu_custom_call" | custom-call | flops 7864320 | bytes 13664256 | tf_op jit(solution)/shard_map/right_side/pallas_call | solution.py:78
  36.1 2.6 %collective-permute-start.17 = (f32[4,8,256]{2,1,0:T(8,128)S(1)}, f32[4,8,256]{2,1,0:T(8,128)S(1)}, u32[]{:S(2)}, u32[]{:S(2)}) collective-permute-start(f32[4,8,256]{2,1,0:T(8,128)S(1)} %get-tuple-element.135.refs_4_), channel_id=1, source_target_pairs={{0,24},{8,16},{16,8},{24,0},{1,25},{9,17},{17,9},{25,1},{2,26},{10... | collective-permute-start | bytes 98312 | tf_op jit(solution)/shard_map/ppermute | solution.py:741
  39.5 1.6 %creep_step.3 = (f32[64,16,256]{2,1,0:T(8,128)S(1)}, f32[64,16,256]{2,1,0:T(8,128)S(1)}, f32[4,16,256]{2,1,0:T(8,128)S(1)}) custom-call(f32[64,16,256]{2,1,0:T(8,128)S(1)} %get-tuple-element.131.refs_0_, f32[64,16,256]{2,1,0:T(8,128)S(1)} %get-tuple-element.127.refs_1_.refs_16_, f32[64,16,256]{2,1,0:T(8,128)S(1)} %get-tuple-element.128.refs_2_.refs_17_, ...), custom_call_target="tpu_custom_call" | custom-call | flops 15728640 | bytes 10911744 | tf_op jit(solution)/shard_map/creep_step/pallas_call | solution.py:78
  41.5 1.1 %collective-permute-done.16.refs_6_ = f32[4,8,256]{2,1,0:T(8,128)S(1)} collective-permute-done((f32[4,8,256]{2,1,0:T(8,128)S(1)}, f32[4,8,256]{2,1,0:T(8,128)S(1)}, u32[]{:S(2)}, u32[]{:S(2)}) %collective-permute-start.16) | collective-permute-done | bytes 32800 | tf_op jit(solution)/shard_map/ppermute | solution.py:741
  43.1 1.9 %solve_and_creep.1 = (f32[64,16,256]{2,1,0:T(8,128)S(1)}, f32[64,16,256]{2,1,0:T(8,128)S(1)}, f32[64,16,256]{2,1,0:T(8,128)S(1)}, f32[64,16,256]{2,1,0:T(8,128)S...) custom-call(f32[3,16,256]{2,1,0:T(8,128)S(1)} %get-tuple-element.80.refs, ...), custom_call_target="tpu_custom_call" | custom-call | flops 18350080 | bytes 16719872 | tf_op jit(solution)/shard_map/solve_and_creep/pallas_call | solution.py:78
  45.0 2.3 %collective-permute-start.18 = (f32[64,256]{1,0:T(8,128)S(1)}, f32[64,256]{1,0:T(8,128)S(1)}, u32[]{:S(2)}, u32[]{:S(2)}) collective-permute-start(f32[64,256]{1,0:T(8,128)S(1)} %get-tuple-element.153), channel_id=1, source_target_pairs={{0,2},{4,6},{2,0},{6,4},{1,3},{5,7},{3,1},{7,5},{8,10},{12,14},{10... | collective-permute-start | bytes 196616 | tf_op jit(solution)/shard_map/ppermute | solution.py:94
  47.8 1.7 %balance_inside.1 = (f32[64,16,256]{2,1,0:T(8,128)}, f32[64,16,256]{2,1,0:T(8,128)}, f32[64,16,256]{2,1,0:T(8,128)}, f32[64,16,256]{2,1,0:T(8,128)S(1)}) custom-call(f32[64,16,256]{2,1,0:T(8,128)S(1)} %get-tuple-element.144.s, f32[2,16,256]{2,1,0:T(8,128)S(1)} %get-tuple-element.145.zs, f32[64,16,256]{2,1,0:T(8,128)S(1)} %get-tuple-element.146.t, ...), custom_call_target="tpu_custom_call" | custom-call | flops 5242880 | bytes 8421376 | tf_op jit(solution)/shard_map/balance_inside/pallas_call | solution.py:78
  49.5 1.1 %balance_edges.1 = f32[64,16,256]{2,1,0:T(8,128)} custom-call(f32[64,16,256]{2,1,0:T(8,128)S(1)} %get-tuple-element.152.inside, f32[64,256]{1,0:T(8,128)S(1)} %collective-permute-done.18.xa, f32[64,256]{1,0:T(8,128)S(1)} %collective-permute-done.19.xb, f32[16,128]{1,0:T(8,128)S(1)} %collective-permute-done.20.other), custom_call_target="tpu_custom_call" | custom-call | flops 2621440 | bytes 2236416 | tf_op jit(solution)/shard_map/balance_edges/pallas_call | solution.py:78
  (56 shorter events, 8.2 us)
Async XLA Ops:
  0.6 5.6 %copy-start.3 = (s32[64,16,256]{2,1,0:T(8,128)S(1)}, s32[64,16,256]{2,1,0:T(8,128)}, u32[]{:S(2)}) copy-start(s32[64,16,256]{2,1,0:T(8,128)} %refs_0_.3) | copy-start | bytes 3145732
  0.6 5.6 %copy-start.1 = (f32[64,16,256]{2,1,0:T(8,128)S(1)}, f32[64,16,256]{2,1,0:T(8,128)}, u32[]{:S(2)}) copy-start(f32[64,16,256]{2,1,0:T(8,128)} %t.1) | copy-start | bytes 3145732
  3.2 12.4 %collective-permute-start.3 = (f32[6,64,256]{2,1,0:T(8,128)}, f32[6,64,256]{2,1,0:T(8,128)S(1)}, u32[]{:S(2)}, u32[]{:S(2)}) collective-permute-start(f32[6,64,256]{2,1,0:T(8,128)} %get-tuple-element.88), channel_id=1, source_target_pairs={{0,2},{4,6},{2,0},{6,4},{1,3},{5,7},{3,1},{7,5},{8,10},{12,14},{10... | collective-permute-start | bytes 1179656 | tf_op jit(solution)/shard_map/ppermute | solution.py:94
  6.3 9.3 %collective-permute-start.4 = (f32[6,64,256]{2,1,0:T(8,128)}, f32[6,64,256]{2,1,0:T(8,128)S(1)}, u32[]{:S(2)}, u32[]{:S(2)}) collective-permute-start(f32[6,64,256]{2,1,0:T(8,128)} %get-tuple-element.89), channel_id=1, source_target_pairs={{2,4},{3,5},{0,1},{6,7},{4,2},{5,3},{1,0},{7,6},{10,12},{11,13},{8... | collective-permute-start | bytes 1179656 | tf_op jit(solution)/shard_map/ppermute | solution.py:97
  6.3 4.4 %copy-start.6 = (f32[64,16,256]{2,1,0:T(8,128)S(1)}, f32[64,16,256]{2,1,0:T(8,128)}, u32[]{:S(2)}) copy-start(f32[64,16,256]{2,1,0:T(8,128)} %refs_6_.1) | copy-start | bytes 3145732
  10.8 12.9 %collective-permute-start = (f32[8,16,256]{2,1,0:T(8,128)S(1)}, f32[8,16,256]{2,1,0:T(8,128)S(1)}, u32[]{:S(2)}, u32[]{:S(2)}) collective-permute-start(f32[8,16,256]{2,1,0:T(8,128)S(1)} %get-tuple-element.83), channel_id=1, source_target_pairs={{0,8},{8,0},{16,24},{24,16},{1,9},{9,1},{17,25},{25,17},{2,10},{10... | collective-permute-start | bytes 393224 | tf_op jit(solution)/shard_map/ppermute | solution.py:705
  12.3 11.4 %collective-permute-start.2 = (f32[8,16,256]{2,1,0:T(8,128)S(1)}, f32[8,16,256]{2,1,0:T(8,128)S(1)}, u32[]{:S(2)}, u32[]{:S(2)}) collective-permute-start(f32[8,16,256]{2,1,0:T(8,128)S(1)} %get-tuple-element.84), channel_id=1, source_target_pairs={{0,24},{8,16},{16,8},{24,0},{1,25},{9,17},{17,9},{25,1},{2,26},{10... | collective-permute-start | bytes 393224 | tf_op jit(solution)/shard_map/ppermute | solution.py:705
  13.8 8.1 %collective-permute-start.1 = (f32[3,16,256]{2,1,0:T(8,128)S(1)}, f32[3,16,256]{2,1,0:T(8,128)S(1)}, u32[]{:S(2)}, u32[]{:S(2)}) collective-permute-start(f32[3,16,256]{2,1,0:T(8,128)S(1)} %get-tuple-element.80.refs_5_.refs_0_), channel_id=1, source_target_pairs={{0,16},{8,24},{16,0},{24,8},{1,17},{9,25},{17,1},{25,9},{2,18},{10... | collective-permute-start | bytes 147464 | tf_op jit(solution)/shard_map/ppermute | solution.py:705
  15.6 3.1 %collective-permute-start.5 = (f32[2,16,128]{2,1,0:T(8,128)S(1)}, f32[2,16,128]{2,1,0:T(8,128)S(1)}, u32[]{:S(2)}, u32[]{:S(2)}) collective-permute-start(f32[2,16,128]{2,1,0:T(8,128)S(1)} %slice.3), channel_id=1, source_target_pairs={{0,1},{1,0},{2,3},{3,2},{4,5},{5,4},{6,7},{7,6},{8,9},{9,8},{10,11... | collective-permute-start | bytes 49160 | tf_op jit(solution)/shard_map/ppermute | solution.py:707
  16.0 2.7 %collective-permute-start.6 = (f32[2,8,128]{2,1,0:T(8,128)S(1)}, f32[2,8,128]{2,1,0:T(8,128)S(1)}, u32[]{:S(2)}, u32[]{:S(2)}) collective-permute-start(f32[2,8,128]{2,1,0:T(8,128)S(1)} %get-tuple-element.95.refs_2_), channel_id=1, source_target_pairs={{0,1},{1,0},{2,3},{3,2},{4,5},{5,4},{6,7},{7,6},{8,9},{9,8},{10,11... | collective-permute-start | bytes 24584 | tf_op jit(solution)/shard_map/ppermute | solution.py:712
  18.7 5.1 %collective-permute-start.9 = (f32[7,8,256]{2,1,0:T(8,128)S(1)}, f32[7,8,256]{2,1,0:T(8,128)S(1)}, u32[]{:S(2)}, u32[]{:S(2)}) collective-permute-start(f32[7,8,256]{2,1,0:T(8,128)S(1)} %get-tuple-element.97.refs_4_), channel_id=1, source_target_pairs={{0,24},{8,16},{16,8},{24,0},{1,25},{9,17},{17,9},{25,1},{2,26},{10... | collective-permute-start | bytes 172040 | tf_op jit(solution)/shard_map/ppermute | solution.py:741
  21.4 4.2 %collective-permute-start.8 = (f32[7,8,256]{2,1,0:T(8,128)S(1)}, f32[7,8,256]{2,1,0:T(8,128)S(1)}, u32[]{:S(2)}, u32[]{:S(2)}) collective-permute-start(f32[7,8,256]{2,1,0:T(8,128)S(1)} %get-tuple-element.97.refs_4_), channel_id=1, source_target_pairs={{0,16},{8,24},{16,0},{24,8},{1,17},{9,25},{17,1},{25,9},{2,18},{10... | collective-permute-start | bytes 172040 | tf_op jit(solution)/shard_map/ppermute | solution.py:741
  21.9 4.2 %collective-permute-start.7 = (f32[7,8,256]{2,1,0:T(8,128)S(1)}, f32[7,8,256]{2,1,0:T(8,128)S(1)}, u32[]{:S(2)}, u32[]{:S(2)}) collective-permute-start(f32[7,8,256]{2,1,0:T(8,128)S(1)} %get-tuple-element.97.refs_4_), channel_id=1, source_target_pairs={{0,8},{8,0},{16,24},{24,16},{1,9},{9,1},{17,25},{25,17},{2,10},{10... | collective-permute-start | bytes 172040 | tf_op jit(solution)/shard_map/ppermute | solution.py:741
  26.6 1.7 %collective-permute-start.10 = (f32[24,128]{1,0:T(8,128)S(1)}, f32[24,128]{1,0:T(8,128)S(1)}, u32[]{:S(2)}, u32[]{:S(2)}) collective-permute-start(f32[24,128]{1,0:T(8,128)S(1)} %get-tuple-element.120.refs_6_), channel_id=1, source_target_pairs={{0,1},{1,0},{2,3},{3,2},{4,5},{5,4},{6,7},{7,6},{8,9},{9,8},{10,11... | collective-permute-start | bytes 36872 | tf_op jit(solution)/shard_map/ppermute | solution.py:769
  28.4 5.6 %collective-permute-start.13 = (f32[5,8,256]{2,1,0:T(8,128)S(1)}, f32[5,8,256]{2,1,0:T(8,128)S(1)}, u32[]{:S(2)}, u32[]{:S(2)}) collective-permute-start(f32[5,8,256]{2,1,0:T(8,128)S(1)} %get-tuple-element.121.refs_8_), channel_id=1, source_target_pairs={{0,24},{8,16},{16,8},{24,0},{1,25},{9,17},{17,9},{25,1},{2,26},{10... | collective-permute-start | bytes 122888 | tf_op jit(solution)/shard_map/ppermute | solution.py:741
  29.9 4.2 %collective-permute-start.12 = (f32[5,8,256]{2,1,0:T(8,128)S(1)}, f32[5,8,256]{2,1,0:T(8,128)S(1)}, u32[]{:S(2)}, u32[]{:S(2)}) collective-permute-start(f32[5,8,256]{2,1,0:T(8,128)S(1)} %get-tuple-element.121.refs_8_), channel_id=1, source_target_pairs={{0,16},{8,24},{16,0},{24,8},{1,17},{9,25},{17,1},{25,9},{2,18},{10... | collective-permute-start | bytes 122888 | tf_op jit(solution)/shard_map/ppermute | solution.py:741
  30.3 4.0 %collective-permute-start.11 = (f32[5,8,256]{2,1,0:T(8,128)S(1)}, f32[5,8,256]{2,1,0:T(8,128)S(1)}, u32[]{:S(2)}, u32[]{:S(2)}) collective-permute-start(f32[5,8,256]{2,1,0:T(8,128)S(1)} %get-tuple-element.121.refs_8_), channel_id=1, source_target_pairs={{0,8},{8,0},{16,24},{24,16},{1,9},{9,1},{17,25},{25,17},{2,10},{10... | collective-permute-start | bytes 122888 | tf_op jit(solution)/shard_map/ppermute | solution.py:741
  34.7 1.2 %collective-permute-start.14 = (f32[24,128]{1,0:T(8,128)S(1)}, f32[24,128]{1,0:T(8,128)S(1)}, u32[]{:S(2)}, u32[]{:S(2)}) collective-permute-start(f32[24,128]{1,0:T(8,128)S(1)} %get-tuple-element.134.refs_6_), channel_id=1, source_target_pairs={{0,1},{1,0},{2,3},{3,2},{4,5},{5,4},{6,7},{7,6},{8,9},{9,8},{10,11... | collective-permute-start | bytes 36872 | tf_op jit(solution)/shard_map/ppermute | solution.py:769
  36.1 5.5 %collective-permute-start.17 = (f32[4,8,256]{2,1,0:T(8,128)S(1)}, f32[4,8,256]{2,1,0:T(8,128)S(1)}, u32[]{:S(2)}, u32[]{:S(2)}) collective-permute-start(f32[4,8,256]{2,1,0:T(8,128)S(1)} %get-tuple-element.135.refs_4_), channel_id=1, source_target_pairs={{0,24},{8,16},{16,8},{24,0},{1,25},{9,17},{17,9},{25,1},{2,26},{10... | collective-permute-start | bytes 98312 | tf_op jit(solution)/shard_map/ppermute | solution.py:741
  38.7 3.9 %collective-permute-start.16 = (f32[4,8,256]{2,1,0:T(8,128)S(1)}, f32[4,8,256]{2,1,0:T(8,128)S(1)}, u32[]{:S(2)}, u32[]{:S(2)}) collective-permute-start(f32[4,8,256]{2,1,0:T(8,128)S(1)} %get-tuple-element.135.refs_4_), channel_id=1, source_target_pairs={{0,16},{8,24},{16,0},{24,8},{1,17},{9,25},{17,1},{25,9},{2,18},{10... | collective-permute-start | bytes 98312 | tf_op jit(solution)/shard_map/ppermute | solution.py:741
  39.2 3.9 %collective-permute-start.15 = (f32[4,8,256]{2,1,0:T(8,128)S(1)}, f32[4,8,256]{2,1,0:T(8,128)S(1)}, u32[]{:S(2)}, u32[]{:S(2)}) collective-permute-start(f32[4,8,256]{2,1,0:T(8,128)S(1)} %get-tuple-element.135.refs_4_), channel_id=1, source_target_pairs={{0,8},{8,0},{16,24},{24,16},{1,9},{9,1},{17,25},{25,17},{2,10},{10... | collective-permute-start | bytes 98312 | tf_op jit(solution)/shard_map/ppermute | solution.py:741
  45.0 4.5 %collective-permute-start.18 = (f32[64,256]{1,0:T(8,128)S(1)}, f32[64,256]{1,0:T(8,128)S(1)}, u32[]{:S(2)}, u32[]{:S(2)}) collective-permute-start(f32[64,256]{1,0:T(8,128)S(1)} %get-tuple-element.153), channel_id=1, source_target_pairs={{0,2},{4,6},{2,0},{6,4},{1,3},{5,7},{3,1},{7,5},{8,10},{12,14},{10... | collective-permute-start | bytes 196616 | tf_op jit(solution)/shard_map/ppermute | solution.py:94
  47.3 2.2 %collective-permute-start.19 = (f32[64,256]{1,0:T(8,128)S(1)}, f32[64,256]{1,0:T(8,128)S(1)}, u32[]{:S(2)}, u32[]{:S(2)}) collective-permute-start(f32[64,256]{1,0:T(8,128)S(1)} %get-tuple-element.154), channel_id=1, source_target_pairs={{2,4},{3,5},{0,1},{6,7},{4,2},{5,3},{1,0},{7,6},{10,12},{11,13},{8... | collective-permute-start | bytes 196616 | tf_op jit(solution)/shard_map/ppermute | solution.py:97
  47.3 2.2 %collective-permute-start.20 = (f32[16,128]{1,0:T(8,128)S(1)}, f32[16,128]{1,0:T(8,128)S(1)}, u32[]{:S(2)}, u32[]{:S(2)}) collective-permute-start(f32[16,128]{1,0:T(8,128)S(1)} %get-tuple-element.155), channel_id=1, source_target_pairs={{0,1},{1,0},{2,3},{3,2},{4,5},{5,4},{6,7},{7,6},{8,9},{9,8},{10,11... | collective-permute-start | bytes 24584 | tf_op jit(solution)/shard_map/ppermute | solution.py:779
  (4 other events, 8.9 us)

commit v5 on v4

--- a/solution.py
+++ b/solution.py
@@ -24,7 +24,7 @@
 SUB = 8
 F32 = jnp.float32
 
-U_FACTOR, U_SIDE, U_RIGHT, U_LAST, U_SOLVE, U_CREEP, U_FINAL, U_BACK = 8, 8, 16, 16, 64, 16, 16, 64
+U_FACTOR, U_SIDE, U_RIGHT, U_LAST, U_SOLVE, U_CREEP, U_FINAL, U_BACK, U_SWEEP = 8, 16, 64, 16, 64, 32, 64, 64, 64
 
 
 def loop(count, body, init, unroll=16, reverse=False):
@@ -212,7 +212,7 @@
     loop(levels, level, 0, unroll=U_FACTOR)
 
 
-def factor_main(code_ref, t_ref, pack_ref, k_ref, w_ref, r_ref, yr_ref, left_ref, g_ref):
+def factor_main(code_ref, t_ref, pack_ref, k_ref, w_ref, r_ref, yr_ref, left_ref, right_ref, g_ref):
     levels, x, width = t_ref.shape
     first_loss, last_loss = end_losses()
 
@@ -247,7 +247,7 @@
         w = w_ref[i]
         left = yr_ref[i] + w * left
         right = jnp.where(i == levels - 1, r_ref[i], w * right)
-        left_ref[i] = left
+        left_ref[i], right_ref[i] = left, right
         return (left, right, lane_edge_of(left, i, pack_l), lane_edge_of(right, i, pack_r))
 
     left, _, pack_ref[2], pack_ref[3] = loop(levels, backward, (zero, zero, tile, tile), reverse=True)
@@ -279,14 +279,14 @@
     pack_ref[0], pack_ref[1] = loop(levels, level, (zero, zero), unroll=64)
 
 
-def first_side(p, t, k, w, r, left, th, kh, qh, gxh, gyh, diagh, wh, rh, yrh, lefth, z, zh, send, pack_ref):
+def first_side(p, t, k, left, right, th, kh, qh, gxh, gyh, diagh, wh, rh, yrh, lefth, righth, rhs_ref, rhsh, send, pack_ref):
     levels, x, width = t.shape
     row = lax.broadcasted_iota(jnp.int32, (SUB, width), 0)
     lane = lax.broadcasted_iota(jnp.int32, (SUB, width), 1)
     first_loss, last_loss = end_losses()
 
     def forward(i, carry):
-        ws, yy, wy, here, wy_main, bf = carry
+        ws, yy, here, bf, bl = carry
         temp, t_main, k_main = th[i], t[i], k[i]
         k_next = kh[jnp.minimum(i + 1, levels - 1)]
         cap = cap_by_k(here)
@@ -306,8 +306,7 @@
         diagh[i] = diag
         step_up = jnp.where(row == SUB - 1, t_main[0:1], pltpu.roll(temp, SUB - 1, 0))
         step_low = jnp.where(row == 0, t_main[x - 1 :], pltpu.roll(temp, 1, 0))
-        y = diag * temp + qh[i] + gx * step_up + g_low * step_low + from_beside(temp, gy, 1) + wy
-        zh[i] = y * rr
+        rhsh[i] = diag * temp + qh[i] + gx * step_up + g_low * step_low + from_beside(temp, gy, 1)
         to_first = pltpu.roll(gx * (temp - step_up), 1, 0)
         to_last = pltpu.roll(g_low * (temp - step_low), SUB - 1, 0)
         rhs = p[i]
@@ -315,27 +314,27 @@
         parts[0] = parts[0] + jnp.where(row == 0, to_first, 0.0)
         parts[-1] = parts[-1] + jnp.where(row == SUB - 1, to_last, 0.0)
         rhs = jnp.concatenate(parts, axis=0)
-        y_main = rhs + wy_main
-        z[i] = y_main * r[i]
-        return (ww * s, yy * ww, ww * y, k_next, w[i] * y_main, bf + left[i] * rhs)
+        rhs_ref[i] = rhs
+        return (ww * s, yy * ww, k_next, bf + left[i] * rhs, bl + right[i] * rhs)
 
     zero, zero_main = jnp.zeros((SUB, width), F32), jnp.zeros((x, width), F32)
-    *_, bf = loop(levels, forward, (zero, zero + 1.0, zero, kh[0], zero_main, zero_main), unroll=U_SIDE)
+    *_, bf, bl = loop(levels, forward, (zero, zero + 1.0, kh[0], zero_main, zero_main), unroll=U_SIDE)
 
     def backward(i, carry):
-        ll, right, value, pack_l, pack_r = carry
-        ww = wh[i]
+        ll, rr, bfh, blh, pack_l, pack_r = carry
+        ww, rhs = wh[i], rhsh[i]
         ll = yrh[i] + ww * ll
-        right = jnp.where(i == levels - 1, rh[i], ww * right)
-        lefth[i] = ll
-        return (ll, right, zh[i] + ww * value, lane_edge_of(ll, i, pack_l), lane_edge_of(right, i, pack_r))
+        rr = jnp.where(i == levels - 1, rh[i], ww * rr)
+        lefth[i], righth[i] = ll, rr
+        return (ll, rr, bfh + ll * rhs, blh + rr * rhs, lane_edge_of(ll, i, pack_l), lane_edge_of(rr, i, pack_r))
 
     tile = jnp.zeros((SUB, LANES), F32)
-    ll, _, bfh, pack_ref[0], pack_ref[1] = loop(levels, backward, (zero, zero, zero, tile, tile), unroll=U_BACK, reverse=True)
+    init = (zero, zero, zero, zero, tile, tile)
+    ll, _, bfh, blh, pack_ref[0], pack_ref[1] = loop(levels, backward, init, unroll=U_BACK, reverse=True)
     for j in range(0, x, SUB):
         send[j // SUB] = bf[j : j + SUB]
-        send[(x + j) // SUB] = z[levels - 1, j : j + SUB, :]
-    send[2 * x // SUB] = packed(bfh, zh[levels - 1])
+        send[(x + j) // SUB] = bl[j : j + SUB]
+    send[2 * x // SUB] = packed(bfh, blh)
     half = [0.5 * rcp(jnp.maximum(kh[i], 1e-3)) for i in (0, levels - 1)]
     send[2 * x // SUB + 1] = packed(ll + half[0], yrh[levels - 1])
     send[2 * x // SUB + 2] = packed(rh[levels - 1] + half[1], rh[levels - 1])
@@ -360,30 +359,27 @@
 
 
 def right_side(last, *refs):
-    t, th, q, qh, diag, diagh, gx, gxh, gy, gyh, w, wh, r, rh, left, lefth, *out = refs
+    t, th, q, qh, diag, diagh, gx, gxh, gy, gyh, left, lefth, right, righth, *out = refs
     levels, x, width = t.shape
-    z, send = out[0], out[-1]
+    send = out[-1]
     rows = x if last else x + SUB
 
     def pick(main_ref, halo_ref, i):
         return main_ref[i] if last else both(main_ref, halo_ref, i)
 
     def level(i, carry):
-        wy, bf = carry
+        bf, bl = carry
         temp = both(t, th, i)
         here = temp[:rows]
         rhs = pick(diag, diagh, i) * here + pick(q, qh, i) + from_beside(temp, both(gx, gxh, i), 0)[:rows]
         rhs = rhs + from_beside(here, pick(gy, gyh, i), 1)
-        y = rhs + wy
-        zz = y * pick(r, rh, i)
-        z[i] = zz[:x]
+        out[0][i] = rhs[:x]
         if not last:
-            out[1][i] = zz[x:]
-        return (pick(w, wh, i) * y, bf + pick(left, lefth, i) * rhs)
+            out[1][i] = rhs[x:]
+        return (bf + pick(left, lefth, i) * rhs, bl + pick(right, righth, i) * rhs)
 
     zero = jnp.zeros((rows, width), F32)
-    _, bf = loop(levels, level, (zero, zero), unroll=U_LAST if last else U_RIGHT)
-    parts = [bf, pick(z, None if last else out[1], levels - 1)]
+    parts = loop(levels, level, (zero, zero), unroll=U_LAST if last else U_RIGHT)
     groups = [part[j : j + SUB] for part in parts for j in range(0, x, SUB)]
     if not last:
         groups.append(packed(*[part[x:] for part in parts]))
@@ -415,25 +411,23 @@
         send[j] = add_at_edge(raw[j], groups[j]) if j < len(groups) else raw[j]
 
 
-def fix_sweep(flow, *refs):
-    half = (len(refs) - 0) // 4
-    w, r, z_in, z = (refs[j * half : (j + 1) * half] for j in range(4))
+def forward_sweep(flow, *refs):
+    count = len(refs) // 4
+    w, r, rhs, z = (refs[j * count : (j + 1) * count] for j in range(4))
     levels, x, width = z[0].shape
-    start = pl.multiple_of(jnp.where(lax.axis_index("phys") == 1, 0, width - LANES), LANES)
-    tile = pl.ds(start, LANES)
 
     def pick(pair, i):
-        return jnp.concatenate([ref[i, :, tile] for ref in pair], axis=0)
+        return jnp.concatenate([ref[i] for ref in pair], axis=0)
 
     def level(i, wy):
-        y = lane_unedge(flow[...], i) + wy
-        value = pick(z_in, i) + pick(r, i) * y
-        z[0][i, :, tile] = value[:x]
-        if half > 1:
-            z[1][i, :, tile] = value[x:]
+        y = add_at_edge(pick(rhs, i) + wy, lane_unedge(flow[...], i))
+        value = pick(r, i) * y
+        z[0][i] = value[:x]
+        if count > 1:
+            z[1][i] = value[x:]
         return pick(w, i) * y
 
-    loop(levels, level, jnp.zeros(flow.shape, F32), unroll=64)
+    loop(levels, level, jnp.zeros((flow.shape[0], width), F32), unroll=U_SWEEP)
 
 
 def packed(a, b):
@@ -586,9 +580,8 @@
 
 def solve_and_creep(count, *refs):
     g_sets, b_sets, refs = refs[:count], refs[count : 2 * count], refs[2 * count :]
-    z, w, r, yr, k, za, zb, state = refs[:8]
-    mod, exp, rate, dist, creep, hard = refs[8:14]
-    t, creep_out, hard_out, s, zs, xa, xb, pack_ref = refs[14:]
+    z, w, r, yr, mod, exp, rate, dist, creep, hard = refs[:10]
+    t, creep_out, hard_out, s, flow_ref, xa, xb, pack_ref = refs[10:]
     levels, x, width = z.shape
     top, bottom = block_flows(g_sets, None, b_sets, x, x)
 
@@ -606,16 +599,14 @@
 
     init = (bottom * r[levels - 1], jnp.zeros((x, LANES), F32))
     _, pack_ref[...] = loop(levels, level, init, unroll=U_FINAL, reverse=True)
-    place = lax.axis_index("stack")
-    for j, (elastic, new, _, m) in enumerate(creep_beside(t, (top, bottom), k, za, zb, state)):
-        zs[j] = jnp.where(place == (0, count - 1)[j], 0.0, m * (elastic - new))
+    flow_ref[0], flow_ref[1] = top, bottom
     is_even = even("plane")
     upper, lower = s[:, x - 1, :], s[:, 0, :]
     xa[...] = jnp.where(is_even, upper, lower)
     xb[...] = jnp.where(is_even, lower, upper)
 
 
-def balance_inside(s, zs, t, creep, hard, t_out, creep_out, hard_out, inside, sem):
+def balance_inside(s, t, creep, hard, flow, k, za, zb, state, t_out, creep_out, hard_out, inside, sem):
     copies = [
         pltpu.make_async_copy(held, out, sem.at[j])
         for j, (held, out) in enumerate(((t, t_out), (creep, creep_out), (hard, hard_out)))
@@ -625,6 +616,11 @@
     levels, x, width = s.shape
     row = lax.broadcasted_iota(jnp.int32, (x, width), 0)
     lane = lax.broadcasted_iota(jnp.int32, (x, width), 1)
+    place, count = lax.axis_index("stack"), lax.axis_size("stack")
+    zs = [
+        jnp.where(place == end, 0.0, m * (elastic - new))
+        for end, (elastic, new, _, m) in zip((0, count - 1), creep_beside(t, flow, k, za, zb, state))
+    ]
 
     def level(i, before):
         here = s[i]
@@ -636,7 +632,7 @@
         inside[i] = total + jnp.where(lane == width - 1, 0.0, pltpu.roll(here, width - 1, 1))
         return here
 
-    loop(levels, level, zs[0])
+    loop(levels, level, zs[0], unroll=8)
     for copy in copies:
         copy.wait()
 
@@ -697,8 +693,8 @@
         vmem=60,
     )
     rows_a, rows_b = plane_exchange(rows_a, rows_b)
-    pack, k, w, r, yr, left, g = call(
-        factor_main, (code, temp), [(4, x, LANES)] + [main] * 5 + [(3, x, width)], "factor_main", 30 * cells
+    pack, k, w, r, yr, left, right, g = call(
+        factor_main, (code, temp), [(4, x, LANES)] + [main] * 6 + [(3, x, width)], "factor_main", 30 * cells
     )
     gx, gy, diag, part = call(lateral_main, (k, temp, source), [main] * 4, "lateral_main", 40 * cells)
     za, zb = call(edge_layers, (code, flag, distortion, creep, hard, g), [(8, x, width)] * 2, "edge_layers", cells, after=(part,))
@@ -712,10 +708,10 @@
     other_packh = lax.ppermute(packh, "phys", swap)
     rows = x + SUB
     groups = 2 * x // SUB
-    gxh, gyh, diagh, wh, rh, yrh, lefth, z, zh, send, packh_lr = call(
+    gxh, gyh, diagh, wh, rh, yrh, lefth, righth, rhs, rhsh, send, packh_lr = call(
         first_side,
-        (part, temp, k, w, r, left, th, kh, qh),
-        [halo] * 7 + [main, halo, (groups + 3, SUB, width), (2, SUB, LANES)],
+        (part, temp, k, left, right, th, kh, qh),
+        [halo] * 8 + [main, halo, (groups + 3, SUB, width), (2, SUB, LANES)],
         "first_side",
         40 * cells,
     )
@@ -724,12 +720,12 @@
     for step in range(TSTEPS):
         first, last = step == 0, step == TSTEPS - 1
         if not first:
-            ins = (temp, th, source, qh, diag, diagh, gx, gxh, gy, gyh, w, wh, r, rh, left, lefth)
+            ins = (temp, th, source, qh, diag, diagh, gx, gxh, gy, gyh, left, lefth, right, righth)
             send = (groups if last else groups + 1, SUB, width)
-            z, *zh, send = call(
+            rhs, *rhsh, send = call(
                 functools.partial(right_side, last), ins, [main, send] if last else [main, halo, send], "right_side", 30 * cells
             )
-            zh = zh[0] if zh else None
+            rhsh = rhsh[0] if rhsh else None
         flow_rows = x if last else rows
         lane_flow, send = call(
             functools.partial(edge_flow, first, x, flow_rows),
@@ -739,11 +735,11 @@
             cells // 8,
         )
         b_sets = [send] + [lax.ppermute(send, "stack", peer) for peer in peers]
-        ins = [lane_flow, w, r, z] if last else [lane_flow, w, wh, r, rh, z, zh]
-        fixed = call(
-            fix_sweep, ins, [main] if last else [main, halo], "fix_sweep", cells, aliases={3: 0} if last else {5: 0, 6: 1}
+        ins = [lane_flow, w, r, rhs] if last else [lane_flow, w, wh, r, rh, rhs, rhsh]
+        z, *zh = call(
+            forward_sweep, ins, [main] if last else [main, halo], "forward_sweep", cells, aliases={3: 0} if last else {5: 0, 6: 1}
         )
-        z, zh = (fixed[0], None) if last else fixed
+        zh = zh[0] if zh else None
         if first:
             h_sets = b_sets
             mod, exp, rate = call(prepare_creep, (code, flag), [main] * 3, "prepare_creep", 10 * cells, after=(z,))
@@ -768,9 +764,9 @@
         )
         other = lax.ppermute(own, "phys", swap)
 
-    temp, creep, hard, stress, zs, xa, xb, pack = call(
+    temp, creep, hard, stress, flow, xa, xb, pack = call(
         functools.partial(solve_and_creep, count),
-        g_sets + b_sets + [z, w, r, yr, k, za, zb, state, mod, exp, rate, distortion, creep, hard],
+        g_sets + b_sets + [z, w, r, yr, mod, exp, rate, distortion, creep, hard],
         [main] * 4 + [layers] + [(levels, width)] * 2 + [(x, LANES)],
         "solve_and_creep",
         70 * cells,
@@ -778,7 +774,13 @@
     xa, xb = plane_exchange(xa, xb)
     other = lax.ppermute(pack, "phys", swap)
     temp, creep, hard, inside = call(
-        balance_inside, (stress, zs, temp, creep, hard), [main] * 4, "balance_inside", 20 * cells, [dma((3,))], out_hbm=3
+        balance_inside,
+        (stress, temp, creep, hard, flow, k, za, zb, state),
+        [main] * 4,
+        "balance_inside",
+        20 * cells,
+        [dma((3,))],
+        out_hbm=3,
     )
     (residual,) = call(
         balance_edges,

time: 50.8 us -> 50.4 us (level)
  transfers between devices with their start and end apart: 21 -> 21, of which waited for: 9 -> 8; matrix products, arithmetic and copies ran while one was open for 0% -> 0% of each run, Pallas kernels for 33% -> 33%
where the time goes in v5:
time: 50.4 us; the launch traced here: 50.2 us
  Pallas kernels  23.1 us (46%)
  starting transfers between devices  20.7 us (41%)
  waiting for transfers between devices  5.46 us (11%)
  between operations  0.91 us (2%)
    pallas_call x23, Pallas kernels, call(): pl.pallas_call(kernel if after else body, in_specs=[HBM] * in_hbm + [VMEM...  23.1 us
    ppermute x9, starting transfers between devices, per_device(): b_sets = [send] + [lax.ppermute(send, 'stack', peer) for peer in peers]  10.6 us
    ppermute x2, starting transfers between devices, plane_exchange(): a = lax.ppermute(a, 'plane', pairs + [(j, i) for i, j in pairs])  5.36 us
    ppermute x9, waiting for transfers between devices, per_device(): b_sets = [send] + [lax.ppermute(send, 'stack', peer) for peer in peers]  4.06 us
    ppermute x1, starting transfers between devices, per_device(): lax.ppermute(za, 'stack', peers[0])  1.56 us
    ppermute x1, starting transfers between devices, per_device(): lax.ppermute(zb, 'stack', peers[2])  1.49 us
    ppermute x2, waiting for transfers between devices, plane_exchange(): a = lax.ppermute(a, 'plane', pairs + [(j, i) for i, j in pairs])  1.29 us
  transfers between devices with their start and end apart: 21, of which 8 were waited for; matrix products, arithmetic and copies ran while one was open for 0% of the time, Pallas kernels for 33%

profile of v5, /device:TPU:0, one launch (start us, length us, event | category | flops | bytes accessed | tf_op | source)
XLA Modules:
  0.0 50.2 jit_solution(17444233431796018921)
XLA Ops:
  0.7 2.5 %edge_rows.1 = (f32[6,64,256]{2,1,0:T(8,128)}, f32[6,64,256]{2,1,0:T(8,128)}) custom-call(f32[64,16,256]{2,1,0:T(8,128)} %t.1, s32[64,16,256]{2,1,0:T(8,128)} %refs_0_.3, f32[64,16,256]{2,1,0:T(8,128)} %refs_2_.5), custom_call_target="tpu_custom_call" | custom-call | flops 262144 | bytes 3932160 | tf_op jit(solution)/shard_map/edge_rows/pallas_call | solution.py:78
  3.2 3.1 %collective-permute-start.3 = (f32[6,64,256]{2,1,0:T(8,128)}, f32[6,64,256]{2,1,0:T(8,128)S(1)}, u32[]{:S(2)}, u32[]{:S(2)}) collective-permute-start(f32[6,64,256]{2,1,0:T(8,128)} %get-tuple-element.89), channel_id=1, source_target_pairs={{0,2},{4,6},{2,0},{6,4},{1,3},{5,7},{3,1},{7,5},{8,10},{12,14},{10... | collective-permute-start | bytes 1179656 | tf_op jit(solution)/shard_map/ppermute | solution.py:94
  6.3 2.2 %factor_main.1 = (f32[4,16,128]{2,1,0:T(8,128)S(1)}, f32[64,16,256]{2,1,0:T(8,128)S(1)}, f32[64,16,256]{2,1,0:T(8,128)S(1)}, f32[64,16,256]{2,1,0:T(8,128)S(1)},...) custom-call(s32[64,16,256]{2,1,0:T(8,128)S(1)} %copy-done.1, ...), custom_call_target="tpu_custom_call" | custom-call | flops 7864320 | bytes 8470528 | tf_op jit(solution)/shard_map/factor_main/pallas_call | solution.py:78
  8.5 2.2 %lateral_main.1 = (f32[64,16,256]{2,1,0:T(8,128)S(1)}, f32[64,16,256]{2,1,0:T(8,128)S(1)}, f32[64,16,256]{2,1,0:T(8,128)S(1)}, f32[64,16,256]{2,1,0:T(8,128)S(1)}) custom-call(f32[64,16,256]{2,1,0:T(8,128)S(1)} %get-tuple-element.83.k_ref.k.refs_1_.refs_8_, f32[64,16,256]{2,1,0:T(8,128)S(1)} %copy-done, f32[64,16,256]{2,1,0:T(8,128)S(1)} %copy-done.3), custom_call_target="tpu_custom_call" | custom-call | flops 10485760 | bytes 7340032 | tf_op jit(solution)/shard_map/lateral_main/pallas_call | solution.py:78
  10.8 1.6 %collective-permute-start = (f32[8,16,256]{2,1,0:T(8,128)S(1)}, f32[8,16,256]{2,1,0:T(8,128)S(1)}, u32[]{:S(2)}, u32[]{:S(2)}) collective-permute-start(f32[8,16,256]{2,1,0:T(8,128)S(1)} %get-tuple-element.85), channel_id=1, source_target_pairs={{0,8},{8,0},{16,24},{24,16},{1,9},{9,1},{17,25},{25,17},{2,10},{10... | collective-permute-start | bytes 393224 | tf_op jit(solution)/shard_map/ppermute | solution.py:701
  12.3 1.5 %collective-permute-start.2 = (f32[8,16,256]{2,1,0:T(8,128)S(1)}, f32[8,16,256]{2,1,0:T(8,128)S(1)}, u32[]{:S(2)}, u32[]{:S(2)}) collective-permute-start(f32[8,16,256]{2,1,0:T(8,128)S(1)} %get-tuple-element.86), channel_id=1, source_target_pairs={{0,24},{8,16},{16,8},{24,0},{1,25},{9,17},{17,9},{25,1},{2,26},{10... | collective-permute-start | bytes 393224 | tf_op jit(solution)/shard_map/ppermute | solution.py:701
  14.3 1.3 %collective-permute-done.3.refs_0_ = f32[6,64,256]{2,1,0:T(8,128)S(1)} collective-permute-done((f32[6,64,256]{2,1,0:T(8,128)}, f32[6,64,256]{2,1,0:T(8,128)S(1)}, u32[]{:S(2)}, u32[]{:S(2)}) %collective-permute-start.3) | collective-permute-done | bytes 393248 | tf_op jit(solution)/shard_map/ppermute | solution.py:94
  16.6 1.9 %first_side.1 = (f32[64,8,256]{2,1,0:T(8,128)S(1)}, f32[64,8,256]{2,1,0:T(8,128)S(1)}, f32[64,8,256]{2,1,0:T(8,128)S(1)}, f32[64,8,256]{2,1,0:T(8,128)S(1)}, f32...) custom-call(f32[64,16,256]{2,1,0:T(8,128)S(1)} %get-tuple-element.84, ...), custom_call_target="tpu_custom_call" | custom-call | flops 10485760 | bytes 12648448 | tf_op jit(solution)/shard_map/first_side/pallas_call | solution.py:78
  18.6 2.6 %collective-permute-start.9 = (f32[7,8,256]{2,1,0:T(8,128)S(1)}, f32[7,8,256]{2,1,0:T(8,128)S(1)}, u32[]{:S(2)}, u32[]{:S(2)}) collective-permute-start(f32[7,8,256]{2,1,0:T(8,128)S(1)} %get-tuple-element.98.refs_4_), channel_id=1, source_target_pairs={{0,24},{8,16},{16,8},{24,0},{1,25},{9,17},{17,9},{25,1},{2,26},{10... | collective-permute-start | bytes 172040 | tf_op jit(solution)/shard_map/ppermute | solution.py:737
  22.7 0.6 %prepare_creep.1 = (f32[64,16,256]{2,1,0:T(8,128)S(1)}, f32[64,16,256]{2,1,0:T(8,128)S(1)}, f32[64,16,256]{2,1,0:T(8,128)S(1)}) custom-call(s32[64,16,256]{2,1,0:T(8,128)S(1)} %copy-done.1, s32[64,16,256]{2,1,0:T(8,128)S(1)} %copy-done.4, f32[64,16,256]{2,1,0:T(8,128)S(1)} %get-tuple-element.106.refs_2_.refs_8_), custom_call_target="tpu_custom_call" | custom-call | flops 2621440 | bytes 5242880 | tf_op jit(solution)/shard_map/prepare_creep/pallas_call | solution.py:78
  23.7 1.7 %collective-permute-done.8.refs_6_ = f32[7,8,256]{2,1,0:T(8,128)S(1)} collective-permute-done((f32[7,8,256]{2,1,0:T(8,128)S(1)}, f32[7,8,256]{2,1,0:T(8,128)S(1)}, u32[]{:S(2)}, u32[]{:S(2)}) %collective-permute-start.8) | collective-permute-done | bytes 57376 | tf_op jit(solution)/shard_map/ppermute | solution.py:737
  26.5 1.5 %right_side.2 = (f32[64,16,256]{2,1,0:T(8,128)S(1)}, f32[64,8,256]{2,1,0:T(8,128)S(1)}, f32[5,8,256]{2,1,0:T(8,128)S(1)}) custom-call(f32[64,16,256]{2,1,0:T(8,128)S(1)} %get-tuple-element.115.refs_0_, f32[64,8,256]{2,1,0:T(8,128)S(1)} %get-tuple-element.116.refs_1_, f32[64,16,256]{2,1,0:T(8,128)S(1)} %copy-done.3, ...), custom_call_target="tpu_custom_call" | custom-call | flops 7864320 | bytes 12623872 | tf_op jit(solution)/shard_map/right_side/pallas_call | solution.py:78
  28.1 1.5 %collective-permute-start.13 = (f32[5,8,256]{2,1,0:T(8,128)S(1)}, f32[5,8,256]{2,1,0:T(8,128)S(1)}, u32[]{:S(2)}, u32[]{:S(2)}) collective-permute-start(f32[5,8,256]{2,1,0:T(8,128)S(1)} %get-tuple-element.125.refs_8_), channel_id=1, source_target_pairs={{0,24},{8,16},{16,8},{24,0},{1,25},{9,17},{17,9},{25,1},{2,26},{10... | collective-permute-start | bytes 122888 | tf_op jit(solution)/shard_map/ppermute | solution.py:737
  30.0 1.6 %collective-permute-start.11 = (f32[5,8,256]{2,1,0:T(8,128)S(1)}, f32[5,8,256]{2,1,0:T(8,128)S(1)}, u32[]{:S(2)}, u32[]{:S(2)}) collective-permute-start(f32[5,8,256]{2,1,0:T(8,128)S(1)} %get-tuple-element.125.refs_8_), channel_id=1, source_target_pairs={{0,8},{8,0},{16,24},{24,16},{1,9},{9,1},{17,25},{25,17},{2,10},{10... | collective-permute-start | bytes 122888 | tf_op jit(solution)/shard_map/ppermute | solution.py:737
  31.6 1.5 %creep_step.2 = (f32[64,16,256]{2,1,0:T(8,128)S(1)}, f32[64,16,256]{2,1,0:T(8,128)S(1)}, f32[4,16,256]{2,1,0:T(8,128)S(1)}) custom-call(f32[64,16,256]{2,1,0:T(8,128)S(1)} %get-tuple-element.115.refs_0_, f32[64,16,256]{2,1,0:T(8,128)S(1)} %get-tuple-element.131.refs_1_.refs_12_, f32[64,16,256]{2,1,0:T(8,128)S(1)} %get-tuple-element.132.refs_2_.refs_13_, ...), custom_call_target="tpu_custom_call" | custom-call | flops 15728640 | bytes 10846208 | tf_op jit(solution)/shard_map/creep_step/pallas_call | solution.py:78
  33.1 0.6 %forward_sweep.4 = (f32[64,16,256]{2,1,0:T(8,128)S(1)}, f32[64,8,256]{2,1,0:T(8,128)S(1)}) custom-call(f32[24,128]{1,0:T(8,128)S(1)} %get-tuple-element.126.flow, f32[64,16,256]{2,1,0:T(8,128)S(1)} %get-tuple-element.100.refs_0_.refs_10_.refs_14_.refs_9_, ...), custom_call_target="tpu_custom_call", output_to_operand_aliasing={{0}: (5, {}), {1}: (6, {})} | custom-call | flops 262144 | bytes 6303744 | tf_op jit(solution)/shard_map/forward_sweep/pallas_call | solution.py:78
  34.6 1.1 %right_side.3 = (f32[64,16,256]{2,1,0:T(8,128)S(1)}, f32[4,8,256]{2,1,0:T(8,128)S(1)}) custom-call(f32[64,16,256]{2,1,0:T(8,128)S(1)} %get-tuple-element.135.refs_0_, f32[64,8,256]{2,1,0:T(8,128)S(1)} %get-tuple-element.136.refs_1_, f32[64,16,256]{2,1,0:T(8,128)S(1)} %copy-done.3, f32[64,8,256]{2,1,0:T(8,128)S(1)} %get-tuple-element.93.qh.refs_3_, ...), custom_call_target="tpu_custom_call" | custom-call | flops 7864320 | bytes 12091392 | tf_op jit(solution)/shard_map/right_side/pallas_call | solution.py:78
  35.8 2.6 %collective-permute-start.17 = (f32[4,8,256]{2,1,0:T(8,128)S(1)}, f32[4,8,256]{2,1,0:T(8,128)S(1)}, u32[]{:S(2)}, u32[]{:S(2)}) collective-permute-start(f32[4,8,256]{2,1,0:T(8,128)S(1)} %get-tuple-element.139.refs_4_), channel_id=1, source_target_pairs={{0,24},{8,16},{16,8},{24,0},{1,25},{9,17},{17,9},{25,1},{2,26},{10... | collective-permute-start | bytes 98312 | tf_op jit(solution)/shard_map/ppermute | solution.py:737
  39.3 1.5 %creep_step.3 = (f32[64,16,256]{2,1,0:T(8,128)S(1)}, f32[64,16,256]{2,1,0:T(8,128)S(1)}, f32[4,16,256]{2,1,0:T(8,128)S(1)}) custom-call(f32[64,16,256]{2,1,0:T(8,128)S(1)} %get-tuple-element.135.refs_0_, f32[64,16,256]{2,1,0:T(8,128)S(1)} %get-tuple-element.131.refs_1_.refs_12_, f32[64,16,256]{2,1,0:T(8,128)S(1)} %get-tuple-element.132.refs_2_.refs_13_, ...), custom_call_target="tpu_custom_call" | custom-call | flops 15728640 | bytes 10911744 | tf_op jit(solution)/shard_map/creep_step/pallas_call | solution.py:78
  41.2 1.1 %collective-permute-done.16.refs_6_ = f32[4,8,256]{2,1,0:T(8,128)S(1)} collective-permute-done((f32[4,8,256]{2,1,0:T(8,128)S(1)}, f32[4,8,256]{2,1,0:T(8,128)S(1)}, u32[]{:S(2)}, u32[]{:S(2)}) %collective-permute-start.16) | collective-permute-done | bytes 32800 | tf_op jit(solution)/shard_map/ppermute | solution.py:737
  42.8 1.8 %solve_and_creep.1 = (f32[64,16,256]{2,1,0:T(8,128)S(1)}, f32[64,16,256]{2,1,0:T(8,128)S(1)}, f32[64,16,256]{2,1,0:T(8,128)S(1)}, f32[64,16,256]{2,1,0:T(8,128)S...) custom-call(f32[3,16,256]{2,1,0:T(8,128)S(1)} %get-tuple-element.82.refs, ...), custom_call_target="tpu_custom_call" | custom-call | flops 18350080 | bytes 15343616 | tf_op jit(solution)/shard_map/solve_and_creep/pallas_call | solution.py:78
  44.6 2.3 %collective-permute-start.18 = (f32[64,256]{1,0:T(8,128)S(1)}, f32[64,256]{1,0:T(8,128)S(1)}, u32[]{:S(2)}, u32[]{:S(2)}) collective-permute-start(f32[64,256]{1,0:T(8,128)S(1)} %get-tuple-element.157), channel_id=1, source_target_pairs={{0,2},{4,6},{2,0},{6,4},{1,3},{5,7},{3,1},{7,5},{8,10},{12,14},{10... | collective-permute-start | bytes 196616 | tf_op jit(solution)/shard_map/ppermute | solution.py:94
  47.4 1.7 %balance_inside.1 = (f32[64,16,256]{2,1,0:T(8,128)}, f32[64,16,256]{2,1,0:T(8,128)}, f32[64,16,256]{2,1,0:T(8,128)}, f32[64,16,256]{2,1,0:T(8,128)S(1)}) custom-call(f32[64,16,256]{2,1,0:T(8,128)S(1)} %get-tuple-element.147.s, f32[64,16,256]{2,1,0:T(8,128)S(1)} %get-tuple-element.148.t, f32[64,16,256]{2,1,0:T(8,128)S(1)} %get-tuple-element.149.creep, ...), custom_call_target="tpu_custom_call" | custom-call | flops 5242880 | bytes 9797632 | tf_op jit(solution)/shard_map/balance_inside/pallas_call | solution.py:78
  49.1 1.1 %balance_edges.1 = f32[64,16,256]{2,1,0:T(8,128)} custom-call(f32[64,16,256]{2,1,0:T(8,128)S(1)} %get-tuple-element.156.inside, f32[64,256]{1,0:T(8,128)S(1)} %collective-permute-done.18.xa, f32[64,256]{1,0:T(8,128)S(1)} %collective-permute-done.19.xb, f32[16,128]{1,0:T(8,128)S(1)} %collective-permute-done.20.other), custom_call_target="tpu_custom_call" | custom-call | flops 2621440 | bytes 2236416 | tf_op jit(solution)/shard_map/balance_edges/pallas_call | solution.py:78
  (56 shorter events, 8.5 us)
Async XLA Ops:
  0.6 5.6 %copy-start.1 = (s32[64,16,256]{2,1,0:T(8,128)S(1)}, s32[64,16,256]{2,1,0:T(8,128)}, u32[]{:S(2)}) copy-start(s32[64,16,256]{2,1,0:T(8,128)} %refs_0_.3) | copy-start | bytes 3145732
  0.6 5.6 %copy-start = (f32[64,16,256]{2,1,0:T(8,128)S(1)}, f32[64,16,256]{2,1,0:T(8,128)}, u32[]{:S(2)}) copy-start(f32[64,16,256]{2,1,0:T(8,128)} %t.1) | copy-start | bytes 3145732
  3.2 12.4 %collective-permute-start.3 = (f32[6,64,256]{2,1,0:T(8,128)}, f32[6,64,256]{2,1,0:T(8,128)S(1)}, u32[]{:S(2)}, u32[]{:S(2)}) collective-permute-start(f32[6,64,256]{2,1,0:T(8,128)} %get-tuple-element.89), channel_id=1, source_target_pairs={{0,2},{4,6},{2,0},{6,4},{1,3},{5,7},{3,1},{7,5},{8,10},{12,14},{10... | collective-permute-start | bytes 1179656 | tf_op jit(solution)/shard_map/ppermute | solution.py:94
  6.3 9.3 %collective-permute-start.4 = (f32[6,64,256]{2,1,0:T(8,128)}, f32[6,64,256]{2,1,0:T(8,128)S(1)}, u32[]{:S(2)}, u32[]{:S(2)}) collective-permute-start(f32[6,64,256]{2,1,0:T(8,128)} %get-tuple-element.90), channel_id=1, source_target_pairs={{2,4},{3,5},{0,1},{6,7},{4,2},{5,3},{1,0},{7,6},{10,12},{11,13},{8... | collective-permute-start | bytes 1179656 | tf_op jit(solution)/shard_map/ppermute | solution.py:97
  6.3 4.4 %copy-start.6 = (f32[64,16,256]{2,1,0:T(8,128)S(1)}, f32[64,16,256]{2,1,0:T(8,128)}, u32[]{:S(2)}) copy-start(f32[64,16,256]{2,1,0:T(8,128)} %refs_6_.1) | copy-start | bytes 3145732
  10.8 12.9 %collective-permute-start = (f32[8,16,256]{2,1,0:T(8,128)S(1)}, f32[8,16,256]{2,1,0:T(8,128)S(1)}, u32[]{:S(2)}, u32[]{:S(2)}) collective-permute-start(f32[8,16,256]{2,1,0:T(8,128)S(1)} %get-tuple-element.85), channel_id=1, source_target_pairs={{0,8},{8,0},{16,24},{24,16},{1,9},{9,1},{17,25},{25,17},{2,10},{10... | collective-permute-start | bytes 393224 | tf_op jit(solution)/shard_map/ppermute | solution.py:701
  12.3 11.4 %collective-permute-start.2 = (f32[8,16,256]{2,1,0:T(8,128)S(1)}, f32[8,16,256]{2,1,0:T(8,128)S(1)}, u32[]{:S(2)}, u32[]{:S(2)}) collective-permute-start(f32[8,16,256]{2,1,0:T(8,128)S(1)} %get-tuple-element.86), channel_id=1, source_target_pairs={{0,24},{8,16},{16,8},{24,0},{1,25},{9,17},{17,9},{25,1},{2,26},{10... | collective-permute-start | bytes 393224 | tf_op jit(solution)/shard_map/ppermute | solution.py:701
  13.8 7.9 %collective-permute-start.1 = (f32[3,16,256]{2,1,0:T(8,128)S(1)}, f32[3,16,256]{2,1,0:T(8,128)S(1)}, u32[]{:S(2)}, u32[]{:S(2)}) collective-permute-start(f32[3,16,256]{2,1,0:T(8,128)S(1)} %get-tuple-element.82.refs_5_.refs_0_), channel_id=1, source_target_pairs={{0,16},{8,24},{16,0},{24,8},{1,17},{9,25},{17,1},{25,9},{2,18},{10... | collective-permute-start | bytes 147464 | tf_op jit(solution)/shard_map/ppermute | solution.py:701
  15.6 2.9 %collective-permute-start.5 = (f32[2,16,128]{2,1,0:T(8,128)S(1)}, f32[2,16,128]{2,1,0:T(8,128)S(1)}, u32[]{:S(2)}, u32[]{:S(2)}) collective-permute-start(f32[2,16,128]{2,1,0:T(8,128)S(1)} %slice.3), channel_id=1, source_target_pairs={{0,1},{1,0},{2,3},{3,2},{4,5},{5,4},{6,7},{7,6},{8,9},{9,8},{10,11... | collective-permute-start | bytes 49160 | tf_op jit(solution)/shard_map/ppermute | solution.py:703
  16.0 2.5 %collective-permute-start.6 = (f32[2,8,128]{2,1,0:T(8,128)S(1)}, f32[2,8,128]{2,1,0:T(8,128)S(1)}, u32[]{:S(2)}, u32[]{:S(2)}) collective-permute-start(f32[2,8,128]{2,1,0:T(8,128)S(1)} %get-tuple-element.96.refs_2_), channel_id=1, source_target_pairs={{0,1},{1,0},{2,3},{3,2},{4,5},{5,4},{6,7},{7,6},{8,9},{9,8},{10,11... | collective-permute-start | bytes 24584 | tf_op jit(solution)/shard_map/ppermute | solution.py:708
  18.6 5.1 %collective-permute-start.9 = (f32[7,8,256]{2,1,0:T(8,128)S(1)}, f32[7,8,256]{2,1,0:T(8,128)S(1)}, u32[]{:S(2)}, u32[]{:S(2)}) collective-permute-start(f32[7,8,256]{2,1,0:T(8,128)S(1)} %get-tuple-element.98.refs_4_), channel_id=1, source_target_pairs={{0,24},{8,16},{16,8},{24,0},{1,25},{9,17},{17,9},{25,1},{2,26},{10... | collective-permute-start | bytes 172040 | tf_op jit(solution)/shard_map/ppermute | solution.py:737
  21.2 4.2 %collective-permute-start.8 = (f32[7,8,256]{2,1,0:T(8,128)S(1)}, f32[7,8,256]{2,1,0:T(8,128)S(1)}, u32[]{:S(2)}, u32[]{:S(2)}) collective-permute-start(f32[7,8,256]{2,1,0:T(8,128)S(1)} %get-tuple-element.98.refs_4_), channel_id=1, source_target_pairs={{0,16},{8,24},{16,0},{24,8},{1,17},{9,25},{17,1},{25,9},{2,18},{10... | collective-permute-start | bytes 172040 | tf_op jit(solution)/shard_map/ppermute | solution.py:737
  21.7 4.2 %collective-permute-start.7 = (f32[7,8,256]{2,1,0:T(8,128)S(1)}, f32[7,8,256]{2,1,0:T(8,128)S(1)}, u32[]{:S(2)}, u32[]{:S(2)}) collective-permute-start(f32[7,8,256]{2,1,0:T(8,128)S(1)} %get-tuple-element.98.refs_4_), channel_id=1, source_target_pairs={{0,8},{8,0},{16,24},{24,16},{1,9},{9,1},{17,25},{25,17},{2,10},{10... | collective-permute-start | bytes 172040 | tf_op jit(solution)/shard_map/ppermute | solution.py:737
  26.4 1.6 %collective-permute-start.10 = (f32[24,128]{1,0:T(8,128)S(1)}, f32[24,128]{1,0:T(8,128)S(1)}, u32[]{:S(2)}, u32[]{:S(2)}) collective-permute-start(f32[24,128]{1,0:T(8,128)S(1)} %get-tuple-element.124.refs_6_), channel_id=1, source_target_pairs={{0,1},{1,0},{2,3},{3,2},{4,5},{5,4},{6,7},{7,6},{8,9},{9,8},{10,11... | collective-permute-start | bytes 36872 | tf_op jit(solution)/shard_map/ppermute | solution.py:765
  28.1 5.6 %collective-permute-start.13 = (f32[5,8,256]{2,1,0:T(8,128)S(1)}, f32[5,8,256]{2,1,0:T(8,128)S(1)}, u32[]{:S(2)}, u32[]{:S(2)}) collective-permute-start(f32[5,8,256]{2,1,0:T(8,128)S(1)} %get-tuple-element.125.refs_8_), channel_id=1, source_target_pairs={{0,24},{8,16},{16,8},{24,0},{1,25},{9,17},{17,9},{25,1},{2,26},{10... | collective-permute-start | bytes 122888 | tf_op jit(solution)/shard_map/ppermute | solution.py:737
  29.6 4.2 %collective-permute-start.12 = (f32[5,8,256]{2,1,0:T(8,128)S(1)}, f32[5,8,256]{2,1,0:T(8,128)S(1)}, u32[]{:S(2)}, u32[]{:S(2)}) collective-permute-start(f32[5,8,256]{2,1,0:T(8,128)S(1)} %get-tuple-element.125.refs_8_), channel_id=1, source_target_pairs={{0,16},{8,24},{16,0},{24,8},{1,17},{9,25},{17,1},{25,9},{2,18},{10... | collective-permute-start | bytes 122888 | tf_op jit(solution)/shard_map/ppermute | solution.py:737
  30.0 4.0 %collective-permute-start.11 = (f32[5,8,256]{2,1,0:T(8,128)S(1)}, f32[5,8,256]{2,1,0:T(8,128)S(1)}, u32[]{:S(2)}, u32[]{:S(2)}) collective-permute-start(f32[5,8,256]{2,1,0:T(8,128)S(1)} %get-tuple-element.125.refs_8_), channel_id=1, source_target_pairs={{0,8},{8,0},{16,24},{24,16},{1,9},{9,1},{17,25},{25,17},{2,10},{10... | collective-permute-start | bytes 122888 | tf_op jit(solution)/shard_map/ppermute | solution.py:737
  34.5 1.2 %collective-permute-start.14 = (f32[24,128]{1,0:T(8,128)S(1)}, f32[24,128]{1,0:T(8,128)S(1)}, u32[]{:S(2)}, u32[]{:S(2)}) collective-permute-start(f32[24,128]{1,0:T(8,128)S(1)} %get-tuple-element.138.refs_6_), channel_id=1, source_target_pairs={{0,1},{1,0},{2,3},{3,2},{4,5},{5,4},{6,7},{7,6},{8,9},{9,8},{10,11... | collective-permute-start | bytes 36872 | tf_op jit(solution)/shard_map/ppermute | solution.py:765
  35.8 5.4 %collective-permute-start.17 = (f32[4,8,256]{2,1,0:T(8,128)S(1)}, f32[4,8,256]{2,1,0:T(8,128)S(1)}, u32[]{:S(2)}, u32[]{:S(2)}) collective-permute-start(f32[4,8,256]{2,1,0:T(8,128)S(1)} %get-tuple-element.139.refs_4_), channel_id=1, source_target_pairs={{0,24},{8,16},{16,8},{24,0},{1,25},{9,17},{17,9},{25,1},{2,26},{10... | collective-permute-start | bytes 98312 | tf_op jit(solution)/shard_map/ppermute | solution.py:737
  38.4 3.9 %collective-permute-start.16 = (f32[4,8,256]{2,1,0:T(8,128)S(1)}, f32[4,8,256]{2,1,0:T(8,128)S(1)}, u32[]{:S(2)}, u32[]{:S(2)}) collective-permute-start(f32[4,8,256]{2,1,0:T(8,128)S(1)} %get-tuple-element.139.refs_4_), channel_id=1, source_target_pairs={{0,16},{8,24},{16,0},{24,8},{1,17},{9,25},{17,1},{25,9},{2,18},{10... | collective-permute-start | bytes 98312 | tf_op jit(solution)/shard_map/ppermute | solution.py:737
  38.9 3.9 %collective-permute-start.15 = (f32[4,8,256]{2,1,0:T(8,128)S(1)}, f32[4,8,256]{2,1,0:T(8,128)S(1)}, u32[]{:S(2)}, u32[]{:S(2)}) collective-permute-start(f32[4,8,256]{2,1,0:T(8,128)S(1)} %get-tuple-element.139.refs_4_), channel_id=1, source_target_pairs={{0,8},{8,0},{16,24},{24,16},{1,9},{9,1},{17,25},{25,17},{2,10},{10... | collective-permute-start | bytes 98312 | tf_op jit(solution)/shard_map/ppermute | solution.py:737
  44.6 4.5 %collective-permute-start.18 = (f32[64,256]{1,0:T(8,128)S(1)}, f32[64,256]{1,0:T(8,128)S(1)}, u32[]{:S(2)}, u32[]{:S(2)}) collective-permute-start(f32[64,256]{1,0:T(8,128)S(1)} %get-tuple-element.157), channel_id=1, source_target_pairs={{0,2},{4,6},{2,0},{6,4},{1,3},{5,7},{3,1},{7,5},{8,10},{12,14},{10... | collective-permute-start | bytes 196616 | tf_op jit(solution)/shard_map/ppermute | solution.py:94
  46.9 2.2 %collective-permute-start.19 = (f32[64,256]{1,0:T(8,128)S(1)}, f32[64,256]{1,0:T(8,128)S(1)}, u32[]{:S(2)}, u32[]{:S(2)}) collective-permute-start(f32[64,256]{1,0:T(8,128)S(1)} %get-tuple-element.158), channel_id=1, source_target_pairs={{2,4},{3,5},{0,1},{6,7},{4,2},{5,3},{1,0},{7,6},{10,12},{11,13},{8... | collective-permute-start | bytes 196616 | tf_op jit(solution)/shard_map/ppermute | solution.py:97
  46.9 2.2 %collective-permute-start.20 = (f32[16,128]{1,0:T(8,128)S(1)}, f32[16,128]{1,0:T(8,128)S(1)}, u32[]{:S(2)}, u32[]{:S(2)}) collective-permute-start(f32[16,128]{1,0:T(8,128)S(1)} %get-tuple-element.159), channel_id=1, source_target_pairs={{0,1},{1,0},{2,3},{3,2},{4,5},{5,4},{6,7},{7,6},{8,9},{9,8},{10,11... | collective-permute-start | bytes 24584 | tf_op jit(solution)/shard_map/ppermute | solution.py:775
  (4 other events, 8.9 us)

commit v6 on v5

--- a/solution.py
+++ b/solution.py
@@ -24,7 +24,7 @@
 SUB = 8
 F32 = jnp.float32
 
-U_FACTOR, U_SIDE, U_RIGHT, U_LAST, U_SOLVE, U_CREEP, U_FINAL, U_BACK, U_SWEEP = 8, 16, 64, 16, 64, 32, 64, 64, 64
+U_FACTOR, U_SIDE, U_RIGHT, U_LAST, U_SOLVE, U_CREEP, U_FINAL, U_BACK, U_SWEEP = 8, 16, 64, 16, 64, 32, 32, 64, 64
 
 
 def loop(count, body, init, unroll=16, reverse=False):
@@ -500,7 +500,7 @@
 
 
 def rate_by_flag(active):
-    return jnp.where(active, F32(0.5 * creep_rate * inv_e), F32(0.0))
+    return jnp.where(active, F32(creep_rate * inv_e), F32(0.0))
 
 
 def column_solve(count, first, *refs):
@@ -539,15 +539,15 @@
 
 def creep_cells(temp, mod, exp, rate, dist, creep, hard):
     elastic = dist - exp * temp
-    drive = jnp.exp2((0.5 * log2e) * mod * (elastic - creep) * rcp(hard))
-    drive = drive - rcp(drive)
-    size = jnp.abs(drive)
-    rate = rate * jnp.exp2(-log2e * rcp(jnp.exp2((0.5 * log2e) * temp + 1.0) + 1.0))
-    gap = 1.0 - hard * jnp.exp2(-0.1 * jnp.log2(1.0 + size) - 0.9)
+    strain = elastic - creep
+    drive = jnp.exp2((0.5 * log2e) * mod * jnp.abs(strain) * rcp(hard) - 1.0)
+    drive = drive - 0.25 * rcp(drive)
+    rate = rate * jnp.exp2(-log2e * rcp(jnp.exp2((0.5 * log2e) * temp + 1.0) + 1.0)) * drive
+    gap = 1.0 - hard * jnp.exp2(-0.1 * jnp.log2(0.5 + drive) - 1.0)
     gap_size = jnp.abs(gap)
     root = gap_size * lax.rsqrt(jnp.maximum(gap_size, 1e-30))
-    creep = creep + rate * drive
-    hard = hard + gap * root * (rate * size)
+    creep = creep + jnp.where(strain < 0.0, -rate, rate)
+    hard = hard + gap * root * rate
     return (elastic, creep, hard)
 
 

time: 50.4 us -> 50.5 us (level)
  no operation moved by 1% of the time
where the time goes in v6:
time: 50.5 us; the launch traced here: 50.4 us
  Pallas kernels  23.4 us (46%)
  starting transfers between devices  20.7 us (41%)
  waiting for transfers between devices  5.36 us (11%)
  between operations  0.92 us (2%)
    pallas_call x23, Pallas kernels, call(): pl.pallas_call(kernel if after else body, in_specs=[HBM] * in_hbm + [VMEM...  23.4 us
    ppermute x9, starting transfers between devices, per_device(): b_sets = [send] + [lax.ppermute(send, 'stack', peer) for peer in peers]  10.6 us
    ppermute x2, starting transfers between devices, plane_exchange(): a = lax.ppermute(a, 'plane', pairs + [(j, i) for i, j in pairs])  5.38 us
    ppermute x9, waiting for transfers between devices, per_device(): b_sets = [send] + [lax.ppermute(send, 'stack', peer) for peer in peers]  3.96 us
    ppermute x1, starting transfers between devices, per_device(): lax.ppermute(za, 'stack', peers[0])  1.56 us
    ppermute x1, starting transfers between devices, per_device(): lax.ppermute(zb, 'stack', peers[2])  1.49 us
    ppermute x2, waiting for transfers between devices, plane_exchange(): a = lax.ppermute(a, 'plane', pairs + [(j, i) for i, j in pairs])  1.29 us
  transfers between devices with their start and end apart: 21, of which 8 were waited for; matrix products, arithmetic and copies ran while one was open for 0% of the time, Pallas kernels for 33%

profile of v6, /device:TPU:0, one launch (start us, length us, event | category | flops | bytes accessed | tf_op | source)
XLA Modules:
  0.0 50.4 jit_solution(3267161215323852689)
XLA Ops:
  0.7 2.5 %edge_rows.1 = (f32[6,64,256]{2,1,0:T(8,128)}, f32[6,64,256]{2,1,0:T(8,128)}) custom-call(f32[64,16,256]{2,1,0:T(8,128)} %t.1, s32[64,16,256]{2,1,0:T(8,128)} %refs_0_.3, f32[64,16,256]{2,1,0:T(8,128)} %refs_2_.5), custom_call_target="tpu_custom_call" | custom-call | flops 262144 | bytes 3932160 | tf_op jit(solution)/shard_map/edge_rows/pallas_call | solution.py:78
  3.2 3.1 %collective-permute-start.3 = (f32[6,64,256]{2,1,0:T(8,128)}, f32[6,64,256]{2,1,0:T(8,128)S(1)}, u32[]{:S(2)}, u32[]{:S(2)}) collective-permute-start(f32[6,64,256]{2,1,0:T(8,128)} %get-tuple-element.89), channel_id=1, source_target_pairs={{0,2},{4,6},{2,0},{6,4},{1,3},{5,7},{3,1},{7,5},{8,10},{12,14},{10... | collective-permute-start | bytes 1179656 | tf_op jit(solution)/shard_map/ppermute | solution.py:94
  6.3 2.2 %factor_main.1 = (f32[4,16,128]{2,1,0:T(8,128)S(1)}, f32[64,16,256]{2,1,0:T(8,128)S(1)}, f32[64,16,256]{2,1,0:T(8,128)S(1)}, f32[64,16,256]{2,1,0:T(8,128)S(1)},...) custom-call(s32[64,16,256]{2,1,0:T(8,128)S(1)} %copy-done.1, ...), custom_call_target="tpu_custom_call" | custom-call | flops 7864320 | bytes 8470528 | tf_op jit(solution)/shard_map/factor_main/pallas_call | solution.py:78
  8.5 2.2 %lateral_main.1 = (f32[64,16,256]{2,1,0:T(8,128)S(1)}, f32[64,16,256]{2,1,0:T(8,128)S(1)}, f32[64,16,256]{2,1,0:T(8,128)S(1)}, f32[64,16,256]{2,1,0:T(8,128)S(1)}) custom-call(f32[64,16,256]{2,1,0:T(8,128)S(1)} %get-tuple-element.83.k_ref.k.refs_1_.refs_8_, f32[64,16,256]{2,1,0:T(8,128)S(1)} %copy-done, f32[64,16,256]{2,1,0:T(8,128)S(1)} %copy-done.3), custom_call_target="tpu_custom_call" | custom-call | flops 10485760 | bytes 7340032 | tf_op jit(solution)/shard_map/lateral_main/pallas_call | solution.py:78
  10.8 1.6 %collective-permute-start = (f32[8,16,256]{2,1,0:T(8,128)S(1)}, f32[8,16,256]{2,1,0:T(8,128)S(1)}, u32[]{:S(2)}, u32[]{:S(2)}) collective-permute-start(f32[8,16,256]{2,1,0:T(8,128)S(1)} %get-tuple-element.85), channel_id=1, source_target_pairs={{0,8},{8,0},{16,24},{24,16},{1,9},{9,1},{17,25},{25,17},{2,10},{10... | collective-permute-start | bytes 393224 | tf_op jit(solution)/shard_map/ppermute | solution.py:701
  12.3 1.5 %collective-permute-start.2 = (f32[8,16,256]{2,1,0:T(8,128)S(1)}, f32[8,16,256]{2,1,0:T(8,128)S(1)}, u32[]{:S(2)}, u32[]{:S(2)}) collective-permute-start(f32[8,16,256]{2,1,0:T(8,128)S(1)} %get-tuple-element.86), channel_id=1, source_target_pairs={{0,24},{8,16},{16,8},{24,0},{1,25},{9,17},{17,9},{25,1},{2,26},{10... | collective-permute-start | bytes 393224 | tf_op jit(solution)/shard_map/ppermute | solution.py:701
  14.3 1.3 %collective-permute-done.3.refs_0_ = f32[6,64,256]{2,1,0:T(8,128)S(1)} collective-permute-done((f32[6,64,256]{2,1,0:T(8,128)}, f32[6,64,256]{2,1,0:T(8,128)S(1)}, u32[]{:S(2)}, u32[]{:S(2)}) %collective-permute-start.3) | collective-permute-done | bytes 393248 | tf_op jit(solution)/shard_map/ppermute | solution.py:94
  16.6 1.9 %first_side.1 = (f32[64,8,256]{2,1,0:T(8,128)S(1)}, f32[64,8,256]{2,1,0:T(8,128)S(1)}, f32[64,8,256]{2,1,0:T(8,128)S(1)}, f32[64,8,256]{2,1,0:T(8,128)S(1)}, f32...) custom-call(f32[64,16,256]{2,1,0:T(8,128)S(1)} %get-tuple-element.84, ...), custom_call_target="tpu_custom_call" | custom-call | flops 10485760 | bytes 12648448 | tf_op jit(solution)/shard_map/first_side/pallas_call | solution.py:78
  18.6 2.6 %collective-permute-start.9 = (f32[7,8,256]{2,1,0:T(8,128)S(1)}, f32[7,8,256]{2,1,0:T(8,128)S(1)}, u32[]{:S(2)}, u32[]{:S(2)}) collective-permute-start(f32[7,8,256]{2,1,0:T(8,128)S(1)} %get-tuple-element.98.refs_4_), channel_id=1, source_target_pairs={{0,24},{8,16},{16,8},{24,0},{1,25},{9,17},{17,9},{25,1},{2,26},{10... | collective-permute-start | bytes 172040 | tf_op jit(solution)/shard_map/ppermute | solution.py:737
  22.7 0.6 %prepare_creep.1 = (f32[64,16,256]{2,1,0:T(8,128)S(1)}, f32[64,16,256]{2,1,0:T(8,128)S(1)}, f32[64,16,256]{2,1,0:T(8,128)S(1)}) custom-call(s32[64,16,256]{2,1,0:T(8,128)S(1)} %copy-done.1, s32[64,16,256]{2,1,0:T(8,128)S(1)} %copy-done.4, f32[64,16,256]{2,1,0:T(8,128)S(1)} %get-tuple-element.106.refs_2_.refs_8_), custom_call_target="tpu_custom_call" | custom-call | flops 2621440 | bytes 5242880 | tf_op jit(solution)/shard_map/prepare_creep/pallas_call | solution.py:78
  23.7 1.7 %collective-permute-done.8.refs_6_ = f32[7,8,256]{2,1,0:T(8,128)S(1)} collective-permute-done((f32[7,8,256]{2,1,0:T(8,128)S(1)}, f32[7,8,256]{2,1,0:T(8,128)S(1)}, u32[]{:S(2)}, u32[]{:S(2)}) %collective-permute-start.8) | collective-permute-done | bytes 57376 | tf_op jit(solution)/shard_map/ppermute | solution.py:737
  26.5 1.5 %right_side.2 = (f32[64,16,256]{2,1,0:T(8,128)S(1)}, f32[64,8,256]{2,1,0:T(8,128)S(1)}, f32[5,8,256]{2,1,0:T(8,128)S(1)}) custom-call(f32[64,16,256]{2,1,0:T(8,128)S(1)} %get-tuple-element.115.refs_0_, f32[64,8,256]{2,1,0:T(8,128)S(1)} %get-tuple-element.116.refs_1_, f32[64,16,256]{2,1,0:T(8,128)S(1)} %copy-done.3, ...), custom_call_target="tpu_custom_call" | custom-call | flops 7864320 | bytes 12623872 | tf_op jit(solution)/shard_map/right_side/pallas_call | solution.py:78
  28.1 1.5 %collective-permute-start.13 = (f32[5,8,256]{2,1,0:T(8,128)S(1)}, f32[5,8,256]{2,1,0:T(8,128)S(1)}, u32[]{:S(2)}, u32[]{:S(2)}) collective-permute-start(f32[5,8,256]{2,1,0:T(8,128)S(1)} %get-tuple-element.125.refs_8_), channel_id=1, source_target_pairs={{0,24},{8,16},{16,8},{24,0},{1,25},{9,17},{17,9},{25,1},{2,26},{10... | collective-permute-start | bytes 122888 | tf_op jit(solution)/shard_map/ppermute | solution.py:737
  30.0 1.6 %collective-permute-start.11 = (f32[5,8,256]{2,1,0:T(8,128)S(1)}, f32[5,8,256]{2,1,0:T(8,128)S(1)}, u32[]{:S(2)}, u32[]{:S(2)}) collective-permute-start(f32[5,8,256]{2,1,0:T(8,128)S(1)} %get-tuple-element.125.refs_8_), channel_id=1, source_target_pairs={{0,8},{8,0},{16,24},{24,16},{1,9},{9,1},{17,25},{25,17},{2,10},{10... | collective-permute-start | bytes 122888 | tf_op jit(solution)/shard_map/ppermute | solution.py:737
  31.6 1.6 %creep_step.2 = (f32[64,16,256]{2,1,0:T(8,128)S(1)}, f32[64,16,256]{2,1,0:T(8,128)S(1)}, f32[4,16,256]{2,1,0:T(8,128)S(1)}) custom-call(f32[64,16,256]{2,1,0:T(8,128)S(1)} %get-tuple-element.115.refs_0_, f32[64,16,256]{2,1,0:T(8,128)S(1)} %get-tuple-element.131.refs_1_.refs_12_, f32[64,16,256]{2,1,0:T(8,128)S(1)} %get-tuple-element.132.refs_2_.refs_13_, ...), custom_call_target="tpu_custom_call" | custom-call | flops 15728640 | bytes 10846208 | tf_op jit(solution)/shard_map/creep_step/pallas_call | solution.py:78
  33.1 0.6 %forward_sweep.4 = (f32[64,16,256]{2,1,0:T(8,128)S(1)}, f32[64,8,256]{2,1,0:T(8,128)S(1)}) custom-call(f32[24,128]{1,0:T(8,128)S(1)} %get-tuple-element.126.flow, f32[64,16,256]{2,1,0:T(8,128)S(1)} %get-tuple-element.100.refs_0_.refs_10_.refs_14_.refs_9_, ...), custom_call_target="tpu_custom_call", output_to_operand_aliasing={{0}: (5, {}), {1}: (6, {})} | custom-call | flops 262144 | bytes 6303744 | tf_op jit(solution)/shard_map/forward_sweep/pallas_call | solution.py:78
  34.6 1.1 %right_side.3 = (f32[64,16,256]{2,1,0:T(8,128)S(1)}, f32[4,8,256]{2,1,0:T(8,128)S(1)}) custom-call(f32[64,16,256]{2,1,0:T(8,128)S(1)} %get-tuple-element.135.refs_0_, f32[64,8,256]{2,1,0:T(8,128)S(1)} %get-tuple-element.136.refs_1_, f32[64,16,256]{2,1,0:T(8,128)S(1)} %copy-done.3, f32[64,8,256]{2,1,0:T(8,128)S(1)} %get-tuple-element.93.qh.refs_3_, ...), custom_call_target="tpu_custom_call" | custom-call | flops 7864320 | bytes 12091392 | tf_op jit(solution)/shard_map/right_side/pallas_call | solution.py:78
  35.8 2.6 %collective-permute-start.17 = (f32[4,8,256]{2,1,0:T(8,128)S(1)}, f32[4,8,256]{2,1,0:T(8,128)S(1)}, u32[]{:S(2)}, u32[]{:S(2)}) collective-permute-start(f32[4,8,256]{2,1,0:T(8,128)S(1)} %get-tuple-element.139.refs_4_), channel_id=1, source_target_pairs={{0,24},{8,16},{16,8},{24,0},{1,25},{9,17},{17,9},{25,1},{2,26},{10... | collective-permute-start | bytes 98312 | tf_op jit(solution)/shard_map/ppermute | solution.py:737
  39.3 1.6 %creep_step.3 = (f32[64,16,256]{2,1,0:T(8,128)S(1)}, f32[64,16,256]{2,1,0:T(8,128)S(1)}, f32[4,16,256]{2,1,0:T(8,128)S(1)}) custom-call(f32[64,16,256]{2,1,0:T(8,128)S(1)} %get-tuple-element.135.refs_0_, f32[64,16,256]{2,1,0:T(8,128)S(1)} %get-tuple-element.131.refs_1_.refs_12_, f32[64,16,256]{2,1,0:T(8,128)S(1)} %get-tuple-element.132.refs_2_.refs_13_, ...), custom_call_target="tpu_custom_call" | custom-call | flops 15728640 | bytes 10911744 | tf_op jit(solution)/shard_map/creep_step/pallas_call | solution.py:78
  41.3 1.0 %collective-permute-done.16.refs_6_ = f32[4,8,256]{2,1,0:T(8,128)S(1)} collective-permute-done((f32[4,8,256]{2,1,0:T(8,128)S(1)}, f32[4,8,256]{2,1,0:T(8,128)S(1)}, u32[]{:S(2)}, u32[]{:S(2)}) %collective-permute-start.16) | collective-permute-done | bytes 32800 | tf_op jit(solution)/shard_map/ppermute | solution.py:737
  42.8 1.9 %solve_and_creep.1 = (f32[64,16,256]{2,1,0:T(8,128)S(1)}, f32[64,16,256]{2,1,0:T(8,128)S(1)}, f32[64,16,256]{2,1,0:T(8,128)S(1)}, f32[64,16,256]{2,1,0:T(8,128)S...) custom-call(f32[3,16,256]{2,1,0:T(8,128)S(1)} %get-tuple-element.82.refs, ...), custom_call_target="tpu_custom_call" | custom-call | flops 18350080 | bytes 15343616 | tf_op jit(solution)/shard_map/solve_and_creep/pallas_call | solution.py:78
  44.7 2.3 %collective-permute-start.18 = (f32[64,256]{1,0:T(8,128)S(1)}, f32[64,256]{1,0:T(8,128)S(1)}, u32[]{:S(2)}, u32[]{:S(2)}) collective-permute-start(f32[64,256]{1,0:T(8,128)S(1)} %get-tuple-element.157), channel_id=1, source_target_pairs={{0,2},{4,6},{2,0},{6,4},{1,3},{5,7},{3,1},{7,5},{8,10},{12,14},{10... | collective-permute-start | bytes 196616 | tf_op jit(solution)/shard_map/ppermute | solution.py:94
  47.5 1.7 %balance_inside.1 = (f32[64,16,256]{2,1,0:T(8,128)}, f32[64,16,256]{2,1,0:T(8,128)}, f32[64,16,256]{2,1,0:T(8,128)}, f32[64,16,256]{2,1,0:T(8,128)S(1)}) custom-call(f32[64,16,256]{2,1,0:T(8,128)S(1)} %get-tuple-element.147.s, f32[64,16,256]{2,1,0:T(8,128)S(1)} %get-tuple-element.148.t, f32[64,16,256]{2,1,0:T(8,128)S(1)} %get-tuple-element.149.creep, ...), custom_call_target="tpu_custom_call" | custom-call | flops 5242880 | bytes 9797632 | tf_op jit(solution)/shard_map/balance_inside/pallas_call | solution.py:78
  49.3 1.1 %balance_edges.1 = f32[64,16,256]{2,1,0:T(8,128)} custom-call(f32[64,16,256]{2,1,0:T(8,128)S(1)} %get-tuple-element.156.inside, f32[64,256]{1,0:T(8,128)S(1)} %collective-permute-done.18.xa, f32[64,256]{1,0:T(8,128)S(1)} %collective-permute-done.19.xb, f32[16,128]{1,0:T(8,128)S(1)} %collective-permute-done.20.other), custom_call_target="tpu_custom_call" | custom-call | flops 2621440 | bytes 2236416 | tf_op jit(solution)/shard_map/balance_edges/pallas_call | solution.py:78
  (56 shorter events, 8.4 us)
Async XLA Ops:
  0.6 5.6 %copy-start.1 = (s32[64,16,256]{2,1,0:T(8,128)S(1)}, s32[64,16,256]{2,1,0:T(8,128)}, u32[]{:S(2)}) copy-start(s32[64,16,256]{2,1,0:T(8,128)} %refs_0_.3) | copy-start | bytes 3145732
  0.6 5.6 %copy-start = (f32[64,16,256]{2,1,0:T(8,128)S(1)}, f32[64,16,256]{2,1,0:T(8,128)}, u32[]{:S(2)}) copy-start(f32[64,16,256]{2,1,0:T(8,128)} %t.1) | copy-start | bytes 3145732
  3.2 12.4 %collective-permute-start.3 = (f32[6,64,256]{2,1,0:T(8,128)}, f32[6,64,256]{2,1,0:T(8,128)S(1)}, u32[]{:S(2)}, u32[]{:S(2)}) collective-permute-start(f32[6,64,256]{2,1,0:T(8,128)} %get-tuple-element.89), channel_id=1, source_target_pairs={{0,2},{4,6},{2,0},{6,4},{1,3},{5,7},{3,1},{7,5},{8,10},{12,14},{10... | collective-permute-start | bytes 1179656 | tf_op jit(solution)/shard_map/ppermute | solution.py:94
  6.3 9.3 %collective-permute-start.4 = (f32[6,64,256]{2,1,0:T(8,128)}, f32[6,64,256]{2,1,0:T(8,128)S(1)}, u32[]{:S(2)}, u32[]{:S(2)}) collective-permute-start(f32[6,64,256]{2,1,0:T(8,128)} %get-tuple-element.90), channel_id=1, source_target_pairs={{2,4},{3,5},{0,1},{6,7},{4,2},{5,3},{1,0},{7,6},{10,12},{11,13},{8... | collective-permute-start | bytes 1179656 | tf_op jit(solution)/shard_map/ppermute | solution.py:97
  6.3 4.4 %copy-start.6 = (f32[64,16,256]{2,1,0:T(8,128)S(1)}, f32[64,16,256]{2,1,0:T(8,128)}, u32[]{:S(2)}) copy-start(f32[64,16,256]{2,1,0:T(8,128)} %refs_6_.1) | copy-start | bytes 3145732
  10.8 12.9 %collective-permute-start = (f32[8,16,256]{2,1,0:T(8,128)S(1)}, f32[8,16,256]{2,1,0:T(8,128)S(1)}, u32[]{:S(2)}, u32[]{:S(2)}) collective-permute-start(f32[8,16,256]{2,1,0:T(8,128)S(1)} %get-tuple-element.85), channel_id=1, source_target_pairs={{0,8},{8,0},{16,24},{24,16},{1,9},{9,1},{17,25},{25,17},{2,10},{10... | collective-permute-start | bytes 393224 | tf_op jit(solution)/shard_map/ppermute | solution.py:701
  12.3 11.4 %collective-permute-start.2 = (f32[8,16,256]{2,1,0:T(8,128)S(1)}, f32[8,16,256]{2,1,0:T(8,128)S(1)}, u32[]{:S(2)}, u32[]{:S(2)}) collective-permute-start(f32[8,16,256]{2,1,0:T(8,128)S(1)} %get-tuple-element.86), channel_id=1, source_target_pairs={{0,24},{8,16},{16,8},{24,0},{1,25},{9,17},{17,9},{25,1},{2,26},{10... | collective-permute-start | bytes 393224 | tf_op jit(solution)/shard_map/ppermute | solution.py:701
  13.8 7.9 %collective-permute-start.1 = (f32[3,16,256]{2,1,0:T(8,128)S(1)}, f32[3,16,256]{2,1,0:T(8,128)S(1)}, u32[]{:S(2)}, u32[]{:S(2)}) collective-permute-start(f32[3,16,256]{2,1,0:T(8,128)S(1)} %get-tuple-element.82.refs_5_.refs_0_), channel_id=1, source_target_pairs={{0,16},{8,24},{16,0},{24,8},{1,17},{9,25},{17,1},{25,9},{2,18},{10... | collective-permute-start | bytes 147464 | tf_op jit(solution)/shard_map/ppermute | solution.py:701
  15.6 2.9 %collective-permute-start.5 = (f32[2,16,128]{2,1,0:T(8,128)S(1)}, f32[2,16,128]{2,1,0:T(8,128)S(1)}, u32[]{:S(2)}, u32[]{:S(2)}) collective-permute-start(f32[2,16,128]{2,1,0:T(8,128)S(1)} %slice.3), channel_id=1, source_target_pairs={{0,1},{1,0},{2,3},{3,2},{4,5},{5,4},{6,7},{7,6},{8,9},{9,8},{10,11... | collective-permute-start | bytes 49160 | tf_op jit(solution)/shard_map/ppermute | solution.py:703
  16.0 2.5 %collective-permute-start.6 = (f32[2,8,128]{2,1,0:T(8,128)S(1)}, f32[2,8,128]{2,1,0:T(8,128)S(1)}, u32[]{:S(2)}, u32[]{:S(2)}) collective-permute-start(f32[2,8,128]{2,1,0:T(8,128)S(1)} %get-tuple-element.96.refs_2_), channel_id=1, source_target_pairs={{0,1},{1,0},{2,3},{3,2},{4,5},{5,4},{6,7},{7,6},{8,9},{9,8},{10,11... | collective-permute-start | bytes 24584 | tf_op jit(solution)/shard_map/ppermute | solution.py:708
  18.6 5.1 %collective-permute-start.9 = (f32[7,8,256]{2,1,0:T(8,128)S(1)}, f32[7,8,256]{2,1,0:T(8,128)S(1)}, u32[]{:S(2)}, u32[]{:S(2)}) collective-permute-start(f32[7,8,256]{2,1,0:T(8,128)S(1)} %get-tuple-element.98.refs_4_), channel_id=1, source_target_pairs={{0,24},{8,16},{16,8},{24,0},{1,25},{9,17},{17,9},{25,1},{2,26},{10... | collective-permute-start | bytes 172040 | tf_op jit(solution)/shard_map/ppermute | solution.py:737
  21.2 4.2 %collective-permute-start.8 = (f32[7,8,256]{2,1,0:T(8,128)S(1)}, f32[7,8,256]{2,1,0:T(8,128)S(1)}, u32[]{:S(2)}, u32[]{:S(2)}) collective-permute-start(f32[7,8,256]{2,1,0:T(8,128)S(1)} %get-tuple-element.98.refs_4_), channel_id=1, source_target_pairs={{0,16},{8,24},{16,0},{24,8},{1,17},{9,25},{17,1},{25,9},{2,18},{10... | collective-permute-start | bytes 172040 | tf_op jit(solution)/shard_map/ppermute | solution.py:737
  21.7 4.2 %collective-permute-start.7 = (f32[7,8,256]{2,1,0:T(8,128)S(1)}, f32[7,8,256]{2,1,0:T(8,128)S(1)}, u32[]{:S(2)}, u32[]{:S(2)}) collective-permute-start(f32[7,8,256]{2,1,0:T(8,128)S(1)} %get-tuple-element.98.refs_4_), channel_id=1, source_target_pairs={{0,8},{8,0},{16,24},{24,16},{1,9},{9,1},{17,25},{25,17},{2,10},{10... | collective-permute-start | bytes 172040 | tf_op jit(solution)/shard_map/ppermute | solution.py:737
  26.4 1.6 %collective-permute-start.10 = (f32[24,128]{1,0:T(8,128)S(1)}, f32[24,128]{1,0:T(8,128)S(1)}, u32[]{:S(2)}, u32[]{:S(2)}) collective-permute-start(f32[24,128]{1,0:T(8,128)S(1)} %get-tuple-element.124.refs_6_), channel_id=1, source_target_pairs={{0,1},{1,0},{2,3},{3,2},{4,5},{5,4},{6,7},{7,6},{8,9},{9,8},{10,11... | collective-permute-start | bytes 36872 | tf_op jit(solution)/shard_map/ppermute | solution.py:765
  28.1 5.7 %collective-permute-start.13 = (f32[5,8,256]{2,1,0:T(8,128)S(1)}, f32[5,8,256]{2,1,0:T(8,128)S(1)}, u32[]{:S(2)}, u32[]{:S(2)}) collective-permute-start(f32[5,8,256]{2,1,0:T(8,128)S(1)} %get-tuple-element.125.refs_8_), channel_id=1, source_target_pairs={{0,24},{8,16},{16,8},{24,0},{1,25},{9,17},{17,9},{25,1},{2,26},{10... | collective-permute-start | bytes 122888 | tf_op jit(solution)/shard_map/ppermute | solution.py:737
  29.6 4.2 %collective-permute-start.12 = (f32[5,8,256]{2,1,0:T(8,128)S(1)}, f32[5,8,256]{2,1,0:T(8,128)S(1)}, u32[]{:S(2)}, u32[]{:S(2)}) collective-permute-start(f32[5,8,256]{2,1,0:T(8,128)S(1)} %get-tuple-element.125.refs_8_), channel_id=1, source_target_pairs={{0,16},{8,24},{16,0},{24,8},{1,17},{9,25},{17,1},{25,9},{2,18},{10... | collective-permute-start | bytes 122888 | tf_op jit(solution)/shard_map/ppermute | solution.py:737
  30.0 4.0 %collective-permute-start.11 = (f32[5,8,256]{2,1,0:T(8,128)S(1)}, f32[5,8,256]{2,1,0:T(8,128)S(1)}, u32[]{:S(2)}, u32[]{:S(2)}) collective-permute-start(f32[5,8,256]{2,1,0:T(8,128)S(1)} %get-tuple-element.125.refs_8_), channel_id=1, source_target_pairs={{0,8},{8,0},{16,24},{24,16},{1,9},{9,1},{17,25},{25,17},{2,10},{10... | collective-permute-start | bytes 122888 | tf_op jit(solution)/shard_map/ppermute | solution.py:737
  34.5 1.2 %collective-permute-start.14 = (f32[24,128]{1,0:T(8,128)S(1)}, f32[24,128]{1,0:T(8,128)S(1)}, u32[]{:S(2)}, u32[]{:S(2)}) collective-permute-start(f32[24,128]{1,0:T(8,128)S(1)} %get-tuple-element.138.refs_6_), channel_id=1, source_target_pairs={{0,1},{1,0},{2,3},{3,2},{4,5},{5,4},{6,7},{7,6},{8,9},{9,8},{10,11... | collective-permute-start | bytes 36872 | tf_op jit(solution)/shard_map/ppermute | solution.py:765
  35.8 5.4 %collective-permute-start.17 = (f32[4,8,256]{2,1,0:T(8,128)S(1)}, f32[4,8,256]{2,1,0:T(8,128)S(1)}, u32[]{:S(2)}, u32[]{:S(2)}) collective-permute-start(f32[4,8,256]{2,1,0:T(8,128)S(1)} %get-tuple-element.139.refs_4_), channel_id=1, source_target_pairs={{0,24},{8,16},{16,8},{24,0},{1,25},{9,17},{17,9},{25,1},{2,26},{10... | collective-permute-start | bytes 98312 | tf_op jit(solution)/shard_map/ppermute | solution.py:737
  38.4 3.9 %collective-permute-start.16 = (f32[4,8,256]{2,1,0:T(8,128)S(1)}, f32[4,8,256]{2,1,0:T(8,128)S(1)}, u32[]{:S(2)}, u32[]{:S(2)}) collective-permute-start(f32[4,8,256]{2,1,0:T(8,128)S(1)} %get-tuple-element.139.refs_4_), channel_id=1, source_target_pairs={{0,16},{8,24},{16,0},{24,8},{1,17},{9,25},{17,1},{25,9},{2,18},{10... | collective-permute-start | bytes 98312 | tf_op jit(solution)/shard_map/ppermute | solution.py:737
  38.9 3.9 %collective-permute-start.15 = (f32[4,8,256]{2,1,0:T(8,128)S(1)}, f32[4,8,256]{2,1,0:T(8,128)S(1)}, u32[]{:S(2)}, u32[]{:S(2)}) collective-permute-start(f32[4,8,256]{2,1,0:T(8,128)S(1)} %get-tuple-element.139.refs_4_), channel_id=1, source_target_pairs={{0,8},{8,0},{16,24},{24,16},{1,9},{9,1},{17,25},{25,17},{2,10},{10... | collective-permute-start | bytes 98312 | tf_op jit(solution)/shard_map/ppermute | solution.py:737
  44.7 4.5 %collective-permute-start.18 = (f32[64,256]{1,0:T(8,128)S(1)}, f32[64,256]{1,0:T(8,128)S(1)}, u32[]{:S(2)}, u32[]{:S(2)}) collective-permute-start(f32[64,256]{1,0:T(8,128)S(1)} %get-tuple-element.157), channel_id=1, source_target_pairs={{0,2},{4,6},{2,0},{6,4},{1,3},{5,7},{3,1},{7,5},{8,10},{12,14},{10... | collective-permute-start | bytes 196616 | tf_op jit(solution)/shard_map/ppermute | solution.py:94
  47.0 2.2 %collective-permute-start.19 = (f32[64,256]{1,0:T(8,128)S(1)}, f32[64,256]{1,0:T(8,128)S(1)}, u32[]{:S(2)}, u32[]{:S(2)}) collective-permute-start(f32[64,256]{1,0:T(8,128)S(1)} %get-tuple-element.158), channel_id=1, source_target_pairs={{2,4},{3,5},{0,1},{6,7},{4,2},{5,3},{1,0},{7,6},{10,12},{11,13},{8... | collective-permute-start | bytes 196616 | tf_op jit(solution)/shard_map/ppermute | solution.py:97
  47.0 2.2 %collective-permute-start.20 = (f32[16,128]{1,0:T(8,128)S(1)}, f32[16,128]{1,0:T(8,128)S(1)}, u32[]{:S(2)}, u32[]{:S(2)}) collective-permute-start(f32[16,128]{1,0:T(8,128)S(1)} %get-tuple-element.159), channel_id=1, source_target_pairs={{0,1},{1,0},{2,3},{3,2},{4,5},{5,4},{6,7},{7,6},{8,9},{9,8},{10,11... | collective-permute-start | bytes 24584 | tf_op jit(solution)/shard_map/ppermute | solution.py:775
  (4 other events, 8.9 us)

commit v7 on v6

--- a/solution.py
+++ b/solution.py
@@ -24,7 +24,7 @@
 SUB = 8
 F32 = jnp.float32
 
-U_FACTOR, U_SIDE, U_RIGHT, U_LAST, U_SOLVE, U_CREEP, U_FINAL, U_BACK, U_SWEEP = 8, 16, 64, 16, 64, 32, 32, 64, 64
+U_FACTOR, U_SIDE, U_RIGHT, U_LAST, U_SOLVE, U_CREEP, U_FINAL, U_BACK, U_SWEEP = 8, 8, 32, 16, 32, 32, 16, 32, 32
 
 
 def loop(count, body, init, unroll=16, reverse=False):
@@ -212,7 +212,22 @@
     loop(levels, level, 0, unroll=U_FACTOR)
 
 
-def factor_main(code_ref, t_ref, pack_ref, k_ref, w_ref, r_ref, yr_ref, left_ref, right_ref, g_ref):
+def eliminate(excess, u, y):
+    r = rcp(excess + u)
+    w = u * r
+    return r, w, y * r, w * excess, w * y
+
+
+def middle(s, sb, u, r, rb):
+    return rcp((s * sb + u * (s + sb)) * r * rb)
+
+
+def middle_responses(yr, yrb, w, wb, d):
+    left, rightb = d * yr, d * yrb
+    return (wb * left, rightb, left, w * rightb)
+
+
+def factor_main(code_ref, t_ref, pack_ref, k_ref, w_ref, r_ref, yr_ref, left_ref, right_ref, g_ref, d_ref):
     levels, x, width = t_ref.shape
     first_loss, last_loss = end_losses()
 
@@ -228,32 +243,39 @@
     pack_ref[0], pack_ref[1] = loop(levels, tables, (tile, tile))
     zero = jnp.zeros((x, width), F32)
 
-    def forward(i, carry):
-        ws, y, k_here = carry
-        k_next = k_ref[jnp.minimum(i + 1, levels - 1)]
-        s = r_ref[i] + ws
-        u = jnp.where(i == levels - 1, 0.0, conductance(k_here, k_next))
-        r = rcp(s + u)
-        w = u * r
-        w_ref[i] = w
-        r_ref[i] = r
-        yr_ref[i] = y * r
-        return (w * s, y * w, k_next)
-
-    loop(levels, forward, (zero, zero + 1.0, k_ref[0]))
-
-    def backward(i, carry):
-        left, right, pack_l, pack_r = carry
-        w = w_ref[i]
-        left = yr_ref[i] + w * left
-        right = jnp.where(i == levels - 1, r_ref[i], w * right)
-        left_ref[i], right_ref[i] = left, right
-        return (left, right, lane_edge_of(left, i, pack_l), lane_edge_of(right, i, pack_r))
-
-    left, _, pack_ref[2], pack_ref[3] = loop(levels, backward, (zero, zero, tile, tile), reverse=True)
+    half = levels // 2
+
+    def inward(i, carry):
+        ws, y, wsb, yb, *_ = carry
+        b = levels - 1 - i
+        u, ub = conductance(k_ref[i], k_ref[i + 1]), conductance(k_ref[b], k_ref[b - 1])
+        s, sb = r_ref[i] + ws, r_ref[b] + wsb
+        r, w, yr_ref[i], ws, y = eliminate(s, u, y)
+        rb, wb, yr_ref[b], wsb, yb = eliminate(sb, ub, yb)
+        r_ref[i], w_ref[i], r_ref[b], w_ref[b] = r, w, rb, wb
+        return (ws, y, wsb, yb, s, sb, u, r, rb)
+
+    one = zero + 1.0
+    *_, s, sb, u, r, rb = loop(half, inward, (zero, one, zero, one) + (zero,) * 5)
+    d = middle(s, sb, u, r, rb)
+    d_ref[...] = d
+
+    def outward(i, carry):
+        left, right, leftb, rightb, pack_l, pack_r = carry
+        b = levels - 1 - i
+        w, wb = w_ref[i], w_ref[b]
+        left, right = yr_ref[i] + w * left, w * right
+        leftb, rightb = wb * leftb, yr_ref[b] + wb * rightb
+        left_ref[i], right_ref[i], left_ref[b], right_ref[b] = left, right, leftb, rightb
+        pack_l = lane_edge_of(leftb, b, lane_edge_of(left, i, pack_l))
+        pack_r = lane_edge_of(rightb, b, lane_edge_of(right, i, pack_r))
+        return (left, right, leftb, rightb, pack_l, pack_r)
+
+    init = middle_responses(yr_ref[half - 1], yr_ref[half], w_ref[half - 1], w_ref[half], d)
+    left, right, _, rightb, pack_ref[2], pack_ref[3] = loop(half, outward, init + (tile, tile), reverse=True)
     g_ref[0] = left + 0.5 * rcp(k_ref[0])
-    g_ref[1] = yr_ref[levels - 1]
-    g_ref[2] = r_ref[levels - 1] + 0.5 * rcp(k_ref[levels - 1])
+    g_ref[1] = right
+    g_ref[2] = rightb + 0.5 * rcp(k_ref[levels - 1])
 
 
 def assemble_halo(a_ref, b_ref, kh_ref, th_ref, qh_ref, pack_ref):
@@ -279,24 +301,18 @@
     pack_ref[0], pack_ref[1] = loop(levels, level, (zero, zero), unroll=64)
 
 
-def first_side(p, t, k, left, right, th, kh, qh, gxh, gyh, diagh, wh, rh, yrh, lefth, righth, rhs_ref, rhsh, send, pack_ref):
+def first_side(p, t, k, left, right, th, kh, qh, gxh, gyh, diagh, wh, rh, yrh, lefth, righth, dh, rhs_ref, rhsh, send, pack_ref):
     levels, x, width = t.shape
     row = lax.broadcasted_iota(jnp.int32, (SUB, width), 0)
     lane = lax.broadcasted_iota(jnp.int32, (SUB, width), 1)
     first_loss, last_loss = end_losses()
 
-    def forward(i, carry):
-        ws, yy, here, bf, bl = carry
+    half = levels // 2
+
+    def lateral(i, here, carry):
+        bf, bl = carry
         temp, t_main, k_main = th[i], t[i], k[i]
-        k_next = kh[jnp.minimum(i + 1, levels - 1)]
         cap = cap_by_k(here)
-        loss = jnp.where(i == 0, first_loss, 0.0) + jnp.where(i == levels - 1, last_loss, 0.0)
-        s = cap + loss + ws
-        u = jnp.where(i == levels - 1, 0.0, conductance(here, k_next))
-        rr = rcp(s + u)
-        ww = u * rr
-        wh[i], rh[i], yrh[i] = ww, rr, yy * rr
-
         gx = conductance(here, jnp.where(row == SUB - 1, k_main[0:1], pltpu.roll(here, SUB - 1, 0)), lat_unit)
         g_low = conductance(here, jnp.where(row == 0, k_main[x - 1 :], pltpu.roll(here, 1, 0)), lat_unit)
         gy = conductance(here, pltpu.roll(here, width - 1, 1), lat_unit)
@@ -315,29 +331,50 @@
         parts[-1] = parts[-1] + jnp.where(row == SUB - 1, to_last, 0.0)
         rhs = jnp.concatenate(parts, axis=0)
         rhs_ref[i] = rhs
-        return (ww * s, yy * ww, k_next, bf + left[i] * rhs, bl + right[i] * rhs)
+        return cap, (bf + left[i] * rhs, bl + right[i] * rhs)
+
+    def inward(i, carry):
+        ws, y, wsb, yb, here, hereb, ends = carry[:7]
+        b = levels - 1 - i
+        after, before = kh[i + 1], kh[b - 1]
+        u, ub = conductance(here, after), conductance(hereb, before)
+        cap, ends = lateral(i, here, ends)
+        capb, ends = lateral(b, hereb, ends)
+        s = cap + jnp.where(i == 0, first_loss, 0.0) + ws
+        sb = capb + jnp.where(i == 0, last_loss, 0.0) + wsb
+        r, w, yrh[i], ws, y = eliminate(s, u, y)
+        rb, wb, yrh[b], wsb, yb = eliminate(sb, ub, yb)
+        rh[i], wh[i], rh[b], wh[b] = r, w, rb, wb
+        return (ws, y, wsb, yb, after, before, ends, s, sb, u, r, rb)
 
     zero, zero_main = jnp.zeros((SUB, width), F32), jnp.zeros((x, width), F32)
-    *_, bf, bl = loop(levels, forward, (zero, zero + 1.0, kh[0], zero_main, zero_main), unroll=U_SIDE)
-
-    def backward(i, carry):
-        ll, rr, bfh, blh, pack_l, pack_r = carry
-        ww, rhs = wh[i], rhsh[i]
-        ll = yrh[i] + ww * ll
-        rr = jnp.where(i == levels - 1, rh[i], ww * rr)
-        lefth[i], righth[i] = ll, rr
-        return (ll, rr, bfh + ll * rhs, blh + rr * rhs, lane_edge_of(ll, i, pack_l), lane_edge_of(rr, i, pack_r))
+    one = zero + 1.0
+    init = (zero, one, zero, one, kh[0], kh[levels - 1], (zero_main, zero_main)) + (zero,) * 5
+    *_, (bf, bl), s, sb, u, r, rb = loop(half, inward, init, unroll=U_SIDE)
+    d = middle(s, sb, u, r, rb)
+    dh[...] = d
+
+    def outward(i, carry):
+        ll, rr, llb, rrb, bfh, blh, pack_l, pack_r = carry
+        b = levels - 1 - i
+        w, wb, rhs, rhsb = wh[i], wh[b], rhsh[i], rhsh[b]
+        ll, rr = yrh[i] + w * ll, w * rr
+        llb, rrb = wb * llb, yrh[b] + wb * rrb
+        lefth[i], righth[i], lefth[b], righth[b] = ll, rr, llb, rrb
+        pack_l = lane_edge_of(llb, b, lane_edge_of(ll, i, pack_l))
+        pack_r = lane_edge_of(rrb, b, lane_edge_of(rr, i, pack_r))
+        return (ll, rr, llb, rrb, bfh + ll * rhs + llb * rhsb, blh + rr * rhs + rrb * rhsb, pack_l, pack_r)
 
     tile = jnp.zeros((SUB, LANES), F32)
-    init = (zero, zero, zero, zero, tile, tile)
-    ll, _, bfh, blh, pack_ref[0], pack_ref[1] = loop(levels, backward, init, unroll=U_BACK, reverse=True)
+    init = middle_responses(yrh[half - 1], yrh[half], wh[half - 1], wh[half], d) + (zero, zero, tile, tile)
+    ll, rr, _, rrb, bfh, blh, pack_ref[0], pack_ref[1] = loop(half, outward, init, unroll=U_BACK, reverse=True)
     for j in range(0, x, SUB):
         send[j // SUB] = bf[j : j + SUB]
         send[(x + j) // SUB] = bl[j : j + SUB]
     send[2 * x // SUB] = packed(bfh, blh)
-    half = [0.5 * rcp(jnp.maximum(kh[i], 1e-3)) for i in (0, levels - 1)]
-    send[2 * x // SUB + 1] = packed(ll + half[0], yrh[levels - 1])
-    send[2 * x // SUB + 2] = packed(rh[levels - 1] + half[1], rh[levels - 1])
+    edges = [0.5 * rcp(jnp.maximum(kh[i], 1e-3)) for i in (0, levels - 1)]
+    send[2 * x // SUB + 1] = packed(ll + edges[0], rr)
+    send[2 * x // SUB + 2] = packed(rrb + edges[1], rrb)
 
 
 def both(main_ref, halo_ref, i):
@@ -419,7 +456,7 @@
     def pick(pair, i):
         return jnp.concatenate([ref[i] for ref in pair], axis=0)
 
-    def level(i, wy):
+    def put(i, wy):
         y = add_at_edge(pick(rhs, i) + wy, lane_unedge(flow[...], i))
         value = pick(r, i) * y
         z[0][i] = value[:x]
@@ -427,7 +464,11 @@
             z[1][i] = value[x:]
         return pick(w, i) * y
 
-    loop(levels, level, jnp.zeros((flow.shape[0], width), F32), unroll=U_SWEEP)
+    def level(i, carry):
+        return (put(i, carry[0]), put(levels - 1 - i, carry[1]))
+
+    zero = jnp.zeros((flow.shape[0], width), F32)
+    loop(levels // 2, level, (zero, zero), unroll=U_SWEEP)
 
 
 def packed(a, b):
@@ -503,27 +544,38 @@
     return jnp.where(active, F32(creep_rate * inv_e), F32(0.0))
 
 
+def across(above, below, w, wb, d):
+    return (d * (below + wb * above), d * (above + w * below))
+
+
 def column_solve(count, first, *refs):
     g_sets, h_sets, refs = refs[:count], refs[count : 2 * count], refs[2 * count :]
     b_sets = h_sets
     if not first:
         b_sets, refs = refs[:count], refs[count:]
-    z, zh, w, wh, r, rh, yr, yrh, t, th, pack_ref, flow_ref = refs
+    z, zh, w, wh, yr, yrh, d, dh, t, th, pack_ref, flow_ref = refs
     levels, x, width = z.shape
     rows = x + SUB
     top, bottom = block_flows(g_sets, h_sets, b_sets, x, rows)
     flow_ref[0], flow_ref[1] = top[:x], bottom[:x]
 
     def level(i, carry):
-        add, pack = carry
-        value = both(z, zh, i) + top * both(yr, yrh, i) + add
-        t[i] = value[:x]
-        th[i] = value[x:]
-        pack = lane_edge_of(value, i, pack)
-        return (both(w, wh, jnp.maximum(i - 1, 0)) * value, pack)
-
-    init = (bottom * both(r, rh, levels - 1), jnp.zeros((rows, LANES), F32))
-    _, pack_ref[...] = loop(levels, level, init, unroll=U_SOLVE, reverse=True)
+        above, below, pack = carry
+        b = levels - 1 - i
+        above = both(z, zh, i) + top * both(yr, yrh, i) + both(w, wh, i) * above
+        below = both(z, zh, b) + bottom * both(yr, yrh, b) + both(w, wh, b) * below
+        for place, value in ((i, above), (b, below)):
+            t[place] = value[:x]
+            th[place] = value[x:]
+            pack = lane_edge_of(value, place, pack)
+        return (above, below, pack)
+
+    half = levels // 2
+    above = both(z, zh, half - 1) + top * both(yr, yrh, half - 1)
+    below = both(z, zh, half) + bottom * both(yr, yrh, half)
+    d_all = jnp.concatenate([d[...], dh[...]], axis=0)
+    init = across(above, below, both(w, wh, half - 1), both(w, wh, half), d_all)
+    *_, pack_ref[...] = loop(half, level, init + (jnp.zeros((rows, LANES), F32),), unroll=U_SOLVE, reverse=True)
 
 
 def prepare_creep(code_ref, flag_ref, mod, exp, rate):
@@ -580,25 +632,31 @@
 
 def solve_and_creep(count, *refs):
     g_sets, b_sets, refs = refs[:count], refs[count : 2 * count], refs[2 * count :]
-    z, w, r, yr, mod, exp, rate, dist, creep, hard = refs[:10]
+    z, w, yr, d, mod, exp, rate, dist, creep, hard = refs[:10]
     t, creep_out, hard_out, s, flow_ref, xa, xb, pack_ref = refs[10:]
     levels, x, width = z.shape
     top, bottom = block_flows(g_sets, None, b_sets, x, x)
 
-    def level(i, carry):
-        add, pack = carry
-        value = z[i] + top * yr[i] + add
+    def put(i, value, pack):
         t[i] = value
         m = mod[i]
         elastic, new, hard_out[i] = creep_cells(value, m, exp[i], rate[i], dist[i], creep[i], hard[i])
         creep_out[i] = new
         stress = m * (elastic - new)
         s[i] = stress
-        pack = lane_edge_of(stress, i, pack)
-        return (w[jnp.maximum(i - 1, 0)] * value, pack)
-
-    init = (bottom * r[levels - 1], jnp.zeros((x, LANES), F32))
-    _, pack_ref[...] = loop(levels, level, init, unroll=U_FINAL, reverse=True)
+        return lane_edge_of(stress, i, pack)
+
+    def level(i, carry):
+        above, below, pack = carry
+        b = levels - 1 - i
+        above = z[i] + top * yr[i] + w[i] * above
+        below = z[b] + bottom * yr[b] + w[b] * below
+        return (above, below, put(b, below, put(i, above, pack)))
+
+    half = levels // 2
+    above, below = z[half - 1] + top * yr[half - 1], z[half] + bottom * yr[half]
+    init = across(above, below, w[half - 1], w[half], d[...])
+    *_, pack_ref[...] = loop(half, level, init + (jnp.zeros((x, LANES), F32),), unroll=U_FINAL, reverse=True)
     flow_ref[0], flow_ref[1] = top, bottom
     is_even = even("plane")
     upper, lower = s[:, x - 1, :], s[:, 0, :]
@@ -693,8 +751,8 @@
         vmem=60,
     )
     rows_a, rows_b = plane_exchange(rows_a, rows_b)
-    pack, k, w, r, yr, left, right, g = call(
-        factor_main, (code, temp), [(4, x, LANES)] + [main] * 6 + [(3, x, width)], "factor_main", 30 * cells
+    pack, k, w, r, yr, left, right, g, d = call(
+        factor_main, (code, temp), [(4, x, LANES)] + [main] * 6 + [(3, x, width), (x, width)], "factor_main", 30 * cells
     )
     gx, gy, diag, part = call(lateral_main, (k, temp, source), [main] * 4, "lateral_main", 40 * cells)
     za, zb = call(edge_layers, (code, flag, distortion, creep, hard, g), [(8, x, width)] * 2, "edge_layers", cells, after=(part,))
@@ -708,10 +766,10 @@
     other_packh = lax.ppermute(packh, "phys", swap)
     rows = x + SUB
     groups = 2 * x // SUB
-    gxh, gyh, diagh, wh, rh, yrh, lefth, righth, rhs, rhsh, send, packh_lr = call(
+    gxh, gyh, diagh, wh, rh, yrh, lefth, righth, dh, rhs, rhsh, send, packh_lr = call(
         first_side,
         (part, temp, k, left, right, th, kh, qh),
-        [halo] * 8 + [main, halo, (groups + 3, SUB, width), (2, SUB, LANES)],
+        [halo] * 8 + [(SUB, width), main, halo, (groups + 3, SUB, width), (2, SUB, LANES)],
         "first_side",
         40 * cells,
     )
@@ -756,7 +814,7 @@
             break
         temp, th, own, flow = call(
             functools.partial(column_solve, count, first),
-            g_sets + h_sets + ([] if first else b_sets) + [z, zh, w, wh, r, rh, yr, yrh],
+            g_sets + h_sets + ([] if first else b_sets) + [z, zh, w, wh, yr, yrh, d, dh],
             [main, halo, (rows, LANES), layers],
             "column_solve",
             10 * cells,
@@ -766,7 +824,7 @@
 
     temp, creep, hard, stress, flow, xa, xb, pack = call(
         functools.partial(solve_and_creep, count),
-        g_sets + b_sets + [z, w, r, yr, mod, exp, rate, distortion, creep, hard],
+        g_sets + b_sets + [z, w, yr, d, mod, exp, rate, distortion, creep, hard],
         [main] * 4 + [layers] + [(levels, width)] * 2 + [(x, LANES)],
         "solve_and_creep",
         70 * cells,

time: 50.5 us -> 50.5 us (level)
  transfers between devices with their start and end apart: 21 -> 21, of which waited for: 8 -> 9; matrix products, arithmetic and copies ran while one was open for 0% -> 0% of each run, Pallas kernels for 33% -> 32%
where the time goes in v7:
time: 50.5 us; the launch traced here: 50.3 us
  Pallas kernels  22.9 us (45%)
  starting transfers between devices  20.7 us (41%)
  waiting for transfers between devices  5.78 us (11%)
  between operations  0.92 us (2%)
    pallas_call x23, Pallas kernels, call(): pl.pallas_call(kernel if after else body, in_specs=[HBM] * in_hbm + [VMEM...  22.9 us
    ppermute x9, starting transfers between devices, per_device(): b_sets = [send] + [lax.ppermute(send, 'stack', peer) for peer in peers]  10.5 us
    ppermute x2, starting transfers between devices, plane_exchange(): a = lax.ppermute(a, 'plane', pairs + [(j, i) for i, j in pairs])  5.38 us
    ppermute x9, waiting for transfers between devices, per_device(): b_sets = [send] + [lax.ppermute(send, 'stack', peer) for peer in peers]  4.07 us
    ppermute x2, waiting for transfers between devices, plane_exchange(): a = lax.ppermute(a, 'plane', pairs + [(j, i) for i, j in pairs])  1.56 us
    ppermute x1, starting transfers between devices, per_device(): lax.ppermute(za, 'stack', peers[0])  1.56 us
    ppermute x1, starting transfers between devices, per_device(): lax.ppermute(zb, 'stack', peers[2])  1.49 us
  transfers between devices with their start and end apart: 21, of which 9 were waited for; matrix products, arithmetic and copies ran while one was open for 0% of the time, Pallas kernels for 32%

profile of v7, /device:TPU:0, one launch (start us, length us, event | category | flops | bytes accessed | tf_op | source)
XLA Modules:
  0.0 50.3 jit_solution(1364691685729651199)
XLA Ops:
  0.7 2.5 %edge_rows.1 = (f32[6,64,256]{2,1,0:T(8,128)}, f32[6,64,256]{2,1,0:T(8,128)}) custom-call(f32[64,16,256]{2,1,0:T(8,128)} %t.1, s32[64,16,256]{2,1,0:T(8,128)} %refs_0_.3, f32[64,16,256]{2,1,0:T(8,128)} %refs_2_.5), custom_call_target="tpu_custom_call" | custom-call | flops 262144 | bytes 3932160 | tf_op jit(solution)/shard_map/edge_rows/pallas_call | solution.py:78
  3.2 3.1 %collective-permute-start.3 = (f32[6,64,256]{2,1,0:T(8,128)}, f32[6,64,256]{2,1,0:T(8,128)S(1)}, u32[]{:S(2)}, u32[]{:S(2)}) collective-permute-start(f32[6,64,256]{2,1,0:T(8,128)} %get-tuple-element.91), channel_id=1, source_target_pairs={{0,2},{4,6},{2,0},{6,4},{1,3},{5,7},{3,1},{7,5},{8,10},{12,14},{10... | collective-permute-start | bytes 1179656 | tf_op jit(solution)/shard_map/ppermute | solution.py:94
  6.3 1.9 %factor_main.1 = (f32[4,16,128]{2,1,0:T(8,128)S(1)}, f32[64,16,256]{2,1,0:T(8,128)S(1)}, f32[64,16,256]{2,1,0:T(8,128)S(1)}, f32[64,16,256]{2,1,0:T(8,128)S(1)},...) custom-call(s32[64,16,256]{2,1,0:T(8,128)S(1)} %copy-done.2, ...), custom_call_target="tpu_custom_call" | custom-call | flops 7864320 | bytes 8486912 | tf_op jit(solution)/shard_map/factor_main/pallas_call | solution.py:78
  8.2 2.2 %lateral_main.1 = (f32[64,16,256]{2,1,0:T(8,128)S(1)}, f32[64,16,256]{2,1,0:T(8,128)S(1)}, f32[64,16,256]{2,1,0:T(8,128)S(1)}, f32[64,16,256]{2,1,0:T(8,128)S(1)}) custom-call(f32[64,16,256]{2,1,0:T(8,128)S(1)} %get-tuple-element.85.k_ref.k.refs_1_.refs_8_, f32[64,16,256]{2,1,0:T(8,128)S(1)} %copy-done.1, f32[64,16,256]{2,1,0:T(8,128)S(1)} %copy-done.3), custom_call_target="tpu_custom_call" | custom-call | flops 10485760 | bytes 7340032 | tf_op jit(solution)/shard_map/lateral_main/pallas_call | solution.py:78
  10.5 1.6 %collective-permute-start = (f32[8,16,256]{2,1,0:T(8,128)S(1)}, f32[8,16,256]{2,1,0:T(8,128)S(1)}, u32[]{:S(2)}, u32[]{:S(2)}) collective-permute-start(f32[8,16,256]{2,1,0:T(8,128)S(1)} %get-tuple-element.87), channel_id=1, source_target_pairs={{0,8},{8,0},{16,24},{24,16},{1,9},{9,1},{17,25},{25,17},{2,10},{10... | collective-permute-start | bytes 393224 | tf_op jit(solution)/shard_map/ppermute | solution.py:759
  12.1 1.5 %collective-permute-start.2 = (f32[8,16,256]{2,1,0:T(8,128)S(1)}, f32[8,16,256]{2,1,0:T(8,128)S(1)}, u32[]{:S(2)}, u32[]{:S(2)}) collective-permute-start(f32[8,16,256]{2,1,0:T(8,128)S(1)} %get-tuple-element.88), channel_id=1, source_target_pairs={{0,24},{8,16},{16,8},{24,0},{1,25},{9,17},{17,9},{25,1},{2,26},{10... | collective-permute-start | bytes 393224 | tf_op jit(solution)/shard_map/ppermute | solution.py:759
  14.1 1.5 %collective-permute-done.3.refs_0_ = f32[6,64,256]{2,1,0:T(8,128)S(1)} collective-permute-done((f32[6,64,256]{2,1,0:T(8,128)}, f32[6,64,256]{2,1,0:T(8,128)S(1)}, u32[]{:S(2)}, u32[]{:S(2)}) %collective-permute-start.3) | collective-permute-done | bytes 393248 | tf_op jit(solution)/shard_map/ppermute | solution.py:94
  16.0 0.6 %collective-permute-start.6 = (f32[2,8,128]{2,1,0:T(8,128)S(1)}, f32[2,8,128]{2,1,0:T(8,128)S(1)}, u32[]{:S(2)}, u32[]{:S(2)}) collective-permute-start(f32[2,8,128]{2,1,0:T(8,128)S(1)} %get-tuple-element.98.refs_2_), channel_id=1, source_target_pairs={{0,1},{1,0},{2,3},{3,2},{4,5},{5,4},{6,7},{7,6},{8,9},{9,8},{10,11... | collective-permute-start | bytes 24584 | tf_op jit(solution)/shard_map/ppermute | solution.py:766
  16.6 1.9 %first_side.1 = (f32[64,8,256]{2,1,0:T(8,128)S(1)}, f32[64,8,256]{2,1,0:T(8,128)S(1)}, f32[64,8,256]{2,1,0:T(8,128)S(1)}, f32[64,8,256]{2,1,0:T(8,128)S(1)}, f32...) custom-call(f32[64,16,256]{2,1,0:T(8,128)S(1)} %get-tuple-element.86, ...), custom_call_target="tpu_custom_call" | custom-call | flops 10485760 | bytes 12656640 | tf_op jit(solution)/shard_map/first_side/pallas_call | solution.py:78
  18.6 2.6 %collective-permute-start.9 = (f32[7,8,256]{2,1,0:T(8,128)S(1)}, f32[7,8,256]{2,1,0:T(8,128)S(1)}, u32[]{:S(2)}, u32[]{:S(2)}) collective-permute-start(f32[7,8,256]{2,1,0:T(8,128)S(1)} %get-tuple-element.100.refs_4_), channel_id=1, source_target_pairs={{0,24},{8,16},{16,8},{24,0},{1,25},{9,17},{17,9},{25,1},{2,26},{10... | collective-permute-start | bytes 172040 | tf_op jit(solution)/shard_map/ppermute | solution.py:795
  22.6 0.6 %prepare_creep.1 = (f32[64,16,256]{2,1,0:T(8,128)S(1)}, f32[64,16,256]{2,1,0:T(8,128)S(1)}, f32[64,16,256]{2,1,0:T(8,128)S(1)}) custom-call(s32[64,16,256]{2,1,0:T(8,128)S(1)} %copy-done.2, s32[64,16,256]{2,1,0:T(8,128)S(1)} %copy-done.4, f32[64,16,256]{2,1,0:T(8,128)S(1)} %get-tuple-element.108.refs_2_.refs_8_), custom_call_target="tpu_custom_call" | custom-call | flops 2621440 | bytes 5242880 | tf_op jit(solution)/shard_map/prepare_creep/pallas_call | solution.py:78
  23.7 1.7 %collective-permute-done.8.refs_6_ = f32[7,8,256]{2,1,0:T(8,128)S(1)} collective-permute-done((f32[7,8,256]{2,1,0:T(8,128)S(1)}, f32[7,8,256]{2,1,0:T(8,128)S(1)}, u32[]{:S(2)}, u32[]{:S(2)}) %collective-permute-start.8) | collective-permute-done | bytes 57376 | tf_op jit(solution)/shard_map/ppermute | solution.py:795
  26.4 1.5 %right_side.2 = (f32[64,16,256]{2,1,0:T(8,128)S(1)}, f32[64,8,256]{2,1,0:T(8,128)S(1)}, f32[5,8,256]{2,1,0:T(8,128)S(1)}) custom-call(f32[64,16,256]{2,1,0:T(8,128)S(1)} %get-tuple-element.119.refs_0_, f32[64,8,256]{2,1,0:T(8,128)S(1)} %get-tuple-element.120.refs_1_, f32[64,16,256]{2,1,0:T(8,128)S(1)} %copy-done.3, ...), custom_call_target="tpu_custom_call" | custom-call | flops 7864320 | bytes 12623872 | tf_op jit(solution)/shard_map/right_side/pallas_call | solution.py:78
  28.0 1.5 %collective-permute-start.13 = (f32[5,8,256]{2,1,0:T(8,128)S(1)}, f32[5,8,256]{2,1,0:T(8,128)S(1)}, u32[]{:S(2)}, u32[]{:S(2)}) collective-permute-start(f32[5,8,256]{2,1,0:T(8,128)S(1)} %get-tuple-element.129.refs_8_), channel_id=1, source_target_pairs={{0,24},{8,16},{16,8},{24,0},{1,25},{9,17},{17,9},{25,1},{2,26},{10... | collective-permute-start | bytes 122888 | tf_op jit(solution)/shard_map/ppermute | solution.py:795
  29.9 1.6 %collective-permute-start.11 = (f32[5,8,256]{2,1,0:T(8,128)S(1)}, f32[5,8,256]{2,1,0:T(8,128)S(1)}, u32[]{:S(2)}, u32[]{:S(2)}) collective-permute-start(f32[5,8,256]{2,1,0:T(8,128)S(1)} %get-tuple-element.129.refs_8_), channel_id=1, source_target_pairs={{0,8},{8,0},{16,24},{24,16},{1,9},{9,1},{17,25},{25,17},{2,10},{10... | collective-permute-start | bytes 122888 | tf_op jit(solution)/shard_map/ppermute | solution.py:795
  31.5 1.5 %creep_step.2 = (f32[64,16,256]{2,1,0:T(8,128)S(1)}, f32[64,16,256]{2,1,0:T(8,128)S(1)}, f32[4,16,256]{2,1,0:T(8,128)S(1)}) custom-call(f32[64,16,256]{2,1,0:T(8,128)S(1)} %get-tuple-element.119.refs_0_, f32[64,16,256]{2,1,0:T(8,128)S(1)} %get-tuple-element.135.refs_1_.refs_12_, f32[64,16,256]{2,1,0:T(8,128)S(1)} %get-tuple-element.136.refs_2_.refs_13_, ...), custom_call_target="tpu_custom_call" | custom-call | flops 15728640 | bytes 10846208 | tf_op jit(solution)/shard_map/creep_step/pallas_call | solution.py:78
  34.4 1.0 %right_side.3 = (f32[64,16,256]{2,1,0:T(8,128)S(1)}, f32[4,8,256]{2,1,0:T(8,128)S(1)}) custom-call(f32[64,16,256]{2,1,0:T(8,128)S(1)} %get-tuple-element.139.refs_0_, f32[64,8,256]{2,1,0:T(8,128)S(1)} %get-tuple-element.140.refs_1_, f32[64,16,256]{2,1,0:T(8,128)S(1)} %copy-done.3, f32[64,8,256]{2,1,0:T(8,128)S(1)} %get-tuple-element.95.qh.refs_3_, ...), custom_call_target="tpu_custom_call" | custom-call | flops 7864320 | bytes 12091392 | tf_op jit(solution)/shard_map/right_side/pallas_call | solution.py:78
  35.7 2.6 %collective-permute-start.17 = (f32[4,8,256]{2,1,0:T(8,128)S(1)}, f32[4,8,256]{2,1,0:T(8,128)S(1)}, u32[]{:S(2)}, u32[]{:S(2)}) collective-permute-start(f32[4,8,256]{2,1,0:T(8,128)S(1)} %get-tuple-element.143.refs_4_), channel_id=1, source_target_pairs={{0,24},{8,16},{16,8},{24,0},{1,25},{9,17},{17,9},{25,1},{2,26},{10... | collective-permute-start | bytes 98312 | tf_op jit(solution)/shard_map/ppermute | solution.py:795
  39.2 1.6 %creep_step.3 = (f32[64,16,256]{2,1,0:T(8,128)S(1)}, f32[64,16,256]{2,1,0:T(8,128)S(1)}, f32[4,16,256]{2,1,0:T(8,128)S(1)}) custom-call(f32[64,16,256]{2,1,0:T(8,128)S(1)} %get-tuple-element.139.refs_0_, f32[64,16,256]{2,1,0:T(8,128)S(1)} %get-tuple-element.135.refs_1_.refs_12_, f32[64,16,256]{2,1,0:T(8,128)S(1)} %get-tuple-element.136.refs_2_.refs_13_, ...), custom_call_target="tpu_custom_call" | custom-call | flops 15728640 | bytes 10911744 | tf_op jit(solution)/shard_map/creep_step/pallas_call | solution.py:78
  41.2 1.0 %collective-permute-done.16.refs_6_ = f32[4,8,256]{2,1,0:T(8,128)S(1)} collective-permute-done((f32[4,8,256]{2,1,0:T(8,128)S(1)}, f32[4,8,256]{2,1,0:T(8,128)S(1)}, u32[]{:S(2)}, u32[]{:S(2)}) %collective-permute-start.16) | collective-permute-done | bytes 32800 | tf_op jit(solution)/shard_map/ppermute | solution.py:795
  42.7 1.9 %solve_and_creep.1 = (f32[64,16,256]{2,1,0:T(8,128)S(1)}, f32[64,16,256]{2,1,0:T(8,128)S(1)}, f32[64,16,256]{2,1,0:T(8,128)S(1)}, f32[64,16,256]{2,1,0:T(8,128)S...) custom-call(f32[3,16,256]{2,1,0:T(8,128)S(1)} %get-tuple-element.84.refs, ...), custom_call_target="tpu_custom_call" | custom-call | flops 18350080 | bytes 14311424 | tf_op jit(solution)/shard_map/solve_and_creep/pallas_call | solution.py:78
  44.7 2.3 %collective-permute-start.18 = (f32[64,256]{1,0:T(8,128)S(1)}, f32[64,256]{1,0:T(8,128)S(1)}, u32[]{:S(2)}, u32[]{:S(2)}) collective-permute-start(f32[64,256]{1,0:T(8,128)S(1)} %get-tuple-element.161), channel_id=1, source_target_pairs={{0,2},{4,6},{2,0},{6,4},{1,3},{5,7},{3,1},{7,5},{8,10},{12,14},{10... | collective-permute-start | bytes 196616 | tf_op jit(solution)/shard_map/ppermute | solution.py:94
  47.5 1.7 %balance_inside.1 = (f32[64,16,256]{2,1,0:T(8,128)}, f32[64,16,256]{2,1,0:T(8,128)}, f32[64,16,256]{2,1,0:T(8,128)}, f32[64,16,256]{2,1,0:T(8,128)S(1)}) custom-call(f32[64,16,256]{2,1,0:T(8,128)S(1)} %get-tuple-element.151.s, f32[64,16,256]{2,1,0:T(8,128)S(1)} %get-tuple-element.152.t, f32[64,16,256]{2,1,0:T(8,128)S(1)} %get-tuple-element.153.creep, ...), custom_call_target="tpu_custom_call" | custom-call | flops 5242880 | bytes 9797632 | tf_op jit(solution)/shard_map/balance_inside/pallas_call | solution.py:78
  49.2 1.1 %balance_edges.1 = f32[64,16,256]{2,1,0:T(8,128)} custom-call(f32[64,16,256]{2,1,0:T(8,128)S(1)} %get-tuple-element.160.inside, f32[64,256]{1,0:T(8,128)S(1)} %collective-permute-done.18.xa, f32[64,256]{1,0:T(8,128)S(1)} %collective-permute-done.19.xb, f32[16,128]{1,0:T(8,128)S(1)} %collective-permute-done.20.other), custom_call_target="tpu_custom_call" | custom-call | flops 2621440 | bytes 2236416 | tf_op jit(solution)/shard_map/balance_edges/pallas_call | solution.py:78
  (56 shorter events, 8.3 us)
Async XLA Ops:
  0.6 5.6 %copy-start.2 = (s32[64,16,256]{2,1,0:T(8,128)S(1)}, s32[64,16,256]{2,1,0:T(8,128)}, u32[]{:S(2)}) copy-start(s32[64,16,256]{2,1,0:T(8,128)} %refs_0_.3) | copy-start | bytes 3145732
  0.6 5.6 %copy-start.1 = (f32[64,16,256]{2,1,0:T(8,128)S(1)}, f32[64,16,256]{2,1,0:T(8,128)}, u32[]{:S(2)}) copy-start(f32[64,16,256]{2,1,0:T(8,128)} %t.1) | copy-start | bytes 3145732
  3.2 12.4 %collective-permute-start.3 = (f32[6,64,256]{2,1,0:T(8,128)}, f32[6,64,256]{2,1,0:T(8,128)S(1)}, u32[]{:S(2)}, u32[]{:S(2)}) collective-permute-start(f32[6,64,256]{2,1,0:T(8,128)} %get-tuple-element.91), channel_id=1, source_target_pairs={{0,2},{4,6},{2,0},{6,4},{1,3},{5,7},{3,1},{7,5},{8,10},{12,14},{10... | collective-permute-start | bytes 1179656 | tf_op jit(solution)/shard_map/ppermute | solution.py:94
  6.3 9.3 %collective-permute-start.4 = (f32[6,64,256]{2,1,0:T(8,128)}, f32[6,64,256]{2,1,0:T(8,128)S(1)}, u32[]{:S(2)}, u32[]{:S(2)}) collective-permute-start(f32[6,64,256]{2,1,0:T(8,128)} %get-tuple-element.92), channel_id=1, source_target_pairs={{2,4},{3,5},{0,1},{6,7},{4,2},{5,3},{1,0},{7,6},{10,12},{11,13},{8... | collective-permute-start | bytes 1179656 | tf_op jit(solution)/shard_map/ppermute | solution.py:97
  6.3 4.2 %copy-start.6 = (f32[64,16,256]{2,1,0:T(8,128)S(1)}, f32[64,16,256]{2,1,0:T(8,128)}, u32[]{:S(2)}) copy-start(f32[64,16,256]{2,1,0:T(8,128)} %refs_6_.1) | copy-start | bytes 3145732
  10.5 13.1 %collective-permute-start = (f32[8,16,256]{2,1,0:T(8,128)S(1)}, f32[8,16,256]{2,1,0:T(8,128)S(1)}, u32[]{:S(2)}, u32[]{:S(2)}) collective-permute-start(f32[8,16,256]{2,1,0:T(8,128)S(1)} %get-tuple-element.87), channel_id=1, source_target_pairs={{0,8},{8,0},{16,24},{24,16},{1,9},{9,1},{17,25},{25,17},{2,10},{10... | collective-permute-start | bytes 393224 | tf_op jit(solution)/shard_map/ppermute | solution.py:759
  12.1 11.5 %collective-permute-start.2 = (f32[8,16,256]{2,1,0:T(8,128)S(1)}, f32[8,16,256]{2,1,0:T(8,128)S(1)}, u32[]{:S(2)}, u32[]{:S(2)}) collective-permute-start(f32[8,16,256]{2,1,0:T(8,128)S(1)} %get-tuple-element.88), channel_id=1, source_target_pairs={{0,24},{8,16},{16,8},{24,0},{1,25},{9,17},{17,9},{25,1},{2,26},{10... | collective-permute-start | bytes 393224 | tf_op jit(solution)/shard_map/ppermute | solution.py:759
  13.5 8.2 %collective-permute-start.1 = (f32[3,16,256]{2,1,0:T(8,128)S(1)}, f32[3,16,256]{2,1,0:T(8,128)S(1)}, u32[]{:S(2)}, u32[]{:S(2)}) collective-permute-start(f32[3,16,256]{2,1,0:T(8,128)S(1)} %get-tuple-element.84.refs_5_.refs_0_), channel_id=1, source_target_pairs={{0,16},{8,24},{16,0},{24,8},{1,17},{9,25},{17,1},{25,9},{2,18},{10... | collective-permute-start | bytes 147464 | tf_op jit(solution)/shard_map/ppermute | solution.py:759
  15.6 2.9 %collective-permute-start.5 = (f32[2,16,128]{2,1,0:T(8,128)S(1)}, f32[2,16,128]{2,1,0:T(8,128)S(1)}, u32[]{:S(2)}, u32[]{:S(2)}) collective-permute-start(f32[2,16,128]{2,1,0:T(8,128)S(1)} %slice.3), channel_id=1, source_target_pairs={{0,1},{1,0},{2,3},{3,2},{4,5},{5,4},{6,7},{7,6},{8,9},{9,8},{10,11... | collective-permute-start | bytes 49160 | tf_op jit(solution)/shard_map/ppermute | solution.py:761
  16.0 2.5 %collective-permute-start.6 = (f32[2,8,128]{2,1,0:T(8,128)S(1)}, f32[2,8,128]{2,1,0:T(8,128)S(1)}, u32[]{:S(2)}, u32[]{:S(2)}) collective-permute-start(f32[2,8,128]{2,1,0:T(8,128)S(1)} %get-tuple-element.98.refs_2_), channel_id=1, source_target_pairs={{0,1},{1,0},{2,3},{3,2},{4,5},{5,4},{6,7},{7,6},{8,9},{9,8},{10,11... | collective-permute-start | bytes 24584 | tf_op jit(solution)/shard_map/ppermute | solution.py:766
  18.6 5.1 %collective-permute-start.9 = (f32[7,8,256]{2,1,0:T(8,128)S(1)}, f32[7,8,256]{2,1,0:T(8,128)S(1)}, u32[]{:S(2)}, u32[]{:S(2)}) collective-permute-start(f32[7,8,256]{2,1,0:T(8,128)S(1)} %get-tuple-element.100.refs_4_), channel_id=1, source_target_pairs={{0,24},{8,16},{16,8},{24,0},{1,25},{9,17},{17,9},{25,1},{2,26},{10... | collective-permute-start | bytes 172040 | tf_op jit(solution)/shard_map/ppermute | solution.py:795
  21.2 4.2 %collective-permute-start.8 = (f32[7,8,256]{2,1,0:T(8,128)S(1)}, f32[7,8,256]{2,1,0:T(8,128)S(1)}, u32[]{:S(2)}, u32[]{:S(2)}) collective-permute-start(f32[7,8,256]{2,1,0:T(8,128)S(1)} %get-tuple-element.100.refs_4_), channel_id=1, source_target_pairs={{0,16},{8,24},{16,0},{24,8},{1,17},{9,25},{17,1},{25,9},{2,18},{10... | collective-permute-start | bytes 172040 | tf_op jit(solution)/shard_map/ppermute | solution.py:795
  21.7 4.2 %collective-permute-start.7 = (f32[7,8,256]{2,1,0:T(8,128)S(1)}, f32[7,8,256]{2,1,0:T(8,128)S(1)}, u32[]{:S(2)}, u32[]{:S(2)}) collective-permute-start(f32[7,8,256]{2,1,0:T(8,128)S(1)} %get-tuple-element.100.refs_4_), channel_id=1, source_target_pairs={{0,8},{8,0},{16,24},{24,16},{1,9},{9,1},{17,25},{25,17},{2,10},{10... | collective-permute-start | bytes 172040 | tf_op jit(solution)/shard_map/ppermute | solution.py:795
  26.3 1.6 %collective-permute-start.10 = (f32[24,128]{1,0:T(8,128)S(1)}, f32[24,128]{1,0:T(8,128)S(1)}, u32[]{:S(2)}, u32[]{:S(2)}) collective-permute-start(f32[24,128]{1,0:T(8,128)S(1)} %get-tuple-element.128.refs_6_), channel_id=1, source_target_pairs={{0,1},{1,0},{2,3},{3,2},{4,5},{5,4},{6,7},{7,6},{8,9},{9,8},{10,11... | collective-permute-start | bytes 36872 | tf_op jit(solution)/shard_map/ppermute | solution.py:823
  28.0 5.6 %collective-permute-start.13 = (f32[5,8,256]{2,1,0:T(8,128)S(1)}, f32[5,8,256]{2,1,0:T(8,128)S(1)}, u32[]{:S(2)}, u32[]{:S(2)}) collective-permute-start(f32[5,8,256]{2,1,0:T(8,128)S(1)} %get-tuple-element.129.refs_8_), channel_id=1, source_target_pairs={{0,24},{8,16},{16,8},{24,0},{1,25},{9,17},{17,9},{25,1},{2,26},{10... | collective-permute-start | bytes 122888 | tf_op jit(solution)/shard_map/ppermute | solution.py:795
  29.5 4.2 %collective-permute-start.12 = (f32[5,8,256]{2,1,0:T(8,128)S(1)}, f32[5,8,256]{2,1,0:T(8,128)S(1)}, u32[]{:S(2)}, u32[]{:S(2)}) collective-permute-start(f32[5,8,256]{2,1,0:T(8,128)S(1)} %get-tuple-element.129.refs_8_), channel_id=1, source_target_pairs={{0,16},{8,24},{16,0},{24,8},{1,17},{9,25},{17,1},{25,9},{2,18},{10... | collective-permute-start | bytes 122888 | tf_op jit(solution)/shard_map/ppermute | solution.py:795
  29.9 4.0 %collective-permute-start.11 = (f32[5,8,256]{2,1,0:T(8,128)S(1)}, f32[5,8,256]{2,1,0:T(8,128)S(1)}, u32[]{:S(2)}, u32[]{:S(2)}) collective-permute-start(f32[5,8,256]{2,1,0:T(8,128)S(1)} %get-tuple-element.129.refs_8_), channel_id=1, source_target_pairs={{0,8},{8,0},{16,24},{24,16},{1,9},{9,1},{17,25},{25,17},{2,10},{10... | collective-permute-start | bytes 122888 | tf_op jit(solution)/shard_map/ppermute | solution.py:795
  34.4 1.2 %collective-permute-start.14 = (f32[24,128]{1,0:T(8,128)S(1)}, f32[24,128]{1,0:T(8,128)S(1)}, u32[]{:S(2)}, u32[]{:S(2)}) collective-permute-start(f32[24,128]{1,0:T(8,128)S(1)} %get-tuple-element.142.refs_6_), channel_id=1, source_target_pairs={{0,1},{1,0},{2,3},{3,2},{4,5},{5,4},{6,7},{7,6},{8,9},{9,8},{10,11... | collective-permute-start | bytes 36872 | tf_op jit(solution)/shard_map/ppermute | solution.py:823
  35.7 5.5 %collective-permute-start.17 = (f32[4,8,256]{2,1,0:T(8,128)S(1)}, f32[4,8,256]{2,1,0:T(8,128)S(1)}, u32[]{:S(2)}, u32[]{:S(2)}) collective-permute-start(f32[4,8,256]{2,1,0:T(8,128)S(1)} %get-tuple-element.143.refs_4_), channel_id=1, source_target_pairs={{0,24},{8,16},{16,8},{24,0},{1,25},{9,17},{17,9},{25,1},{2,26},{10... | collective-permute-start | bytes 98312 | tf_op jit(solution)/shard_map/ppermute | solution.py:795
  38.3 3.9 %collective-permute-start.16 = (f32[4,8,256]{2,1,0:T(8,128)S(1)}, f32[4,8,256]{2,1,0:T(8,128)S(1)}, u32[]{:S(2)}, u32[]{:S(2)}) collective-permute-start(f32[4,8,256]{2,1,0:T(8,128)S(1)} %get-tuple-element.143.refs_4_), channel_id=1, source_target_pairs={{0,16},{8,24},{16,0},{24,8},{1,17},{9,25},{17,1},{25,9},{2,18},{10... | collective-permute-start | bytes 98312 | tf_op jit(solution)/shard_map/ppermute | solution.py:795
  38.8 3.9 %collective-permute-start.15 = (f32[4,8,256]{2,1,0:T(8,128)S(1)}, f32[4,8,256]{2,1,0:T(8,128)S(1)}, u32[]{:S(2)}, u32[]{:S(2)}) collective-permute-start(f32[4,8,256]{2,1,0:T(8,128)S(1)} %get-tuple-element.143.refs_4_), channel_id=1, source_target_pairs={{0,8},{8,0},{16,24},{24,16},{1,9},{9,1},{17,25},{25,17},{2,10},{10... | collective-permute-start | bytes 98312 | tf_op jit(solution)/shard_map/ppermute | solution.py:795
  44.7 4.5 %collective-permute-start.18 = (f32[64,256]{1,0:T(8,128)S(1)}, f32[64,256]{1,0:T(8,128)S(1)}, u32[]{:S(2)}, u32[]{:S(2)}) collective-permute-start(f32[64,256]{1,0:T(8,128)S(1)} %get-tuple-element.161), channel_id=1, source_target_pairs={{0,2},{4,6},{2,0},{6,4},{1,3},{5,7},{3,1},{7,5},{8,10},{12,14},{10... | collective-permute-start | bytes 196616 | tf_op jit(solution)/shard_map/ppermute | solution.py:94
  47.0 2.2 %collective-permute-start.19 = (f32[64,256]{1,0:T(8,128)S(1)}, f32[64,256]{1,0:T(8,128)S(1)}, u32[]{:S(2)}, u32[]{:S(2)}) collective-permute-start(f32[64,256]{1,0:T(8,128)S(1)} %get-tuple-element.162), channel_id=1, source_target_pairs={{2,4},{3,5},{0,1},{6,7},{4,2},{5,3},{1,0},{7,6},{10,12},{11,13},{8... | collective-permute-start | bytes 196616 | tf_op jit(solution)/shard_map/ppermute | solution.py:97
  47.0 2.2 %collective-permute-start.20 = (f32[16,128]{1,0:T(8,128)S(1)}, f32[16,128]{1,0:T(8,128)S(1)}, u32[]{:S(2)}, u32[]{:S(2)}) collective-permute-start(f32[16,128]{1,0:T(8,128)S(1)} %get-tuple-element.163), channel_id=1, source_target_pairs={{0,1},{1,0},{2,3},{3,2},{4,5},{5,4},{6,7},{7,6},{8,9},{9,8},{10,11... | collective-permute-start | bytes 24584 | tf_op jit(solution)/shard_map/ppermute | solution.py:833
  (4 other events, 8.7 us)
